TPU v7x, 32 devices: a whole 2x2x4 slice. The times are simulated.
32 devices in a mesh: dp: 2 (over y), mp: 4 (over z), img: 4 (over x, core).
Axes of the slice: x: 2, y: 2, z: 4, core: 2. Of those that a mesh axis runs over, the one named last changes fastest.
Arguments:
- tokens: bfloat16 [16, 256, 2048], P(('dp', 'img'), 'mp'), may hold values from -6 to 6
- slot_index: int32 [16, 256], P(('dp', 'img'), 'mp'), may hold values from -1 to 1023, as said below
- out_grad: bfloat16 [16, 256, 2048], P(('dp', 'img'), 'mp'), may hold values from -6 to 6
- features: bfloat16 [32, 256, 1024], P(('dp', 'mp', 'img')), may hold values from -6 to 6
- query_weight: bfloat16 [2048, 2048], P(('dp', 'img'), 'mp'), may hold values from -0.125 to 0.125
- key_weight: bfloat16 [2048, 2048], P(('dp', 'img'), 'mp'), may hold values from -0.125 to 0.125
- value_weight: bfloat16 [2048, 2048], P(('dp', 'img'), 'mp'), may hold values from -0.125 to 0.125
- output_weight: bfloat16 [2048, 2048], P('mp', ('dp', 'img')), may hold values from -0.125 to 0.125
- up_weight: bfloat16 [2048, 8192], P(('dp', 'img'), 'mp'), may hold values from -0.125 to 0.125
- down_weight: bfloat16 [8192, 2048], P('mp', ('dp', 'img')), may hold values from -0.0625 to 0.0625
- norm_input: bfloat16 [2048], P(('dp', 'mp', 'img')), may hold values from 0.25 to 1.75
- norm_attention: bfloat16 [16, 128], P('mp', ('dp', 'img')), may hold values from 0.25 to 1.75
- norm_middle: bfloat16 [2048], P(('dp', 'mp', 'img')), may hold values from 0.25 to 1.75
- norm_hidden: bfloat16 [64, 128], P('mp', ('dp', 'img')), may hold values from 0.25 to 1.75
- sampler_query: bfloat16 [2048, 2048], P(('dp', 'mp', 'img')), may hold values from -0.125 to 0.125
- sampler_key: bfloat16 [1024, 2048], P(('dp', 'mp', 'img')), may hold values from -0.1875 to 0.1875
- sampler_value: bfloat16 [1024, 2048], P(('dp', 'mp', 'img')), may hold values from -0.1875 to 0.1875
- sampler_output: bfloat16 [2048, 2048], P(('dp', 'mp', 'img')), may hold values from -0.5 to 0.5
- latents: bfloat16 [64, 2048], P(None, ('dp', 'mp', 'img')), may hold values from -6 to 6
- norm_vision: bfloat16 [1024], P(('dp', 'mp', 'img')), may hold values from 0.25 to 1.75
Outputs:
- output: bfloat16 [16, 256, 2048], P(('dp', 'img'), 'mp')
- tokens_grad: bfloat16 [16, 256, 2048], P(('dp', 'img'), 'mp')
- query_weight_grad: float32 [2048, 2048], P(('dp', 'img'), 'mp')
- key_weight_grad: float32 [2048, 2048], P(('dp', 'img'), 'mp')
- value_weight_grad: float32 [2048, 2048], P(('dp', 'img'), 'mp')
- output_weight_grad: float32 [2048, 2048], P('mp', ('dp', 'img'))
- up_weight_grad: float32 [2048, 8192], P(('dp', 'img'), 'mp')
- down_weight_grad: float32 [8192, 2048], P('mp', ('dp', 'img'))
- norm_input_grad: float32 [2048], P(('dp', 'mp', 'img'))
- norm_attention_grad: float32 [16, 128], P('mp', ('dp', 'img'))
- norm_middle_grad: float32 [2048], P(('dp', 'mp', 'img'))
- norm_hidden_grad: float32 [64, 128], P('mp', ('dp', 'img'))
- sampler_query_grad: float32 [2048, 2048], P(('dp', 'mp', 'img'))
- sampler_key_grad: float32 [1024, 2048], P(('dp', 'mp', 'img'))
- sampler_value_grad: float32 [1024, 2048], P(('dp', 'mp', 'img'))
- sampler_output_grad: float32 [2048, 2048], P(('dp', 'mp', 'img'))
- latents_grad: float32 [64, 2048], P(None, ('dp', 'mp', 'img'))
- norm_vision_grad: float32 [1024], P(('dp', 'mp', 'img'))
Inputs may be any that keep to these rules, and one draw needn't show every extreme that they name: `slot_index`: image e of a data group fills the 64 positions b * 64 to b * 64 + 63 of one sequence of that group, with values e * 64 to e * 64 + 63 in order; each of the group's 16 images appears exactly once; every other position holds -1.
All inputs are finite; a program needn't handle non-finite values.
Results may differ from a plain program's by a relative error of at most 0.024.
Values may be sent and summed in bfloat16 or wider, within the bound.
A program may use at most 160 MiB of HBM per device.

v0:
```python
from functools import partial

import jax
import jax.numpy as jnp
from jax import lax
from jax.sharding import PartitionSpec as P

D = 2048
FF = 8192
HD = 64
LAT = 64
LANE = 128
SEQ = 256


EPS = 1e-05


def layer_norm(field, scaling):
    average = jnp.mean(field, -1, keepdims=True)
    centred = field - average
    spread = jnp.mean(centred * centred, -1, keepdims=True)
    return centred * lax.rsqrt(spread + EPS) * scaling


def exact_gelu(field):
    return jax.nn.gelu(field, approximate=False)


def rotary_tables(length, head_size):
    half_size = head_size // 2
    position = jnp.arange(length, dtype=jnp.float32)[:, None]
    pair_index = jnp.arange(half_size, dtype=jnp.float32)[None, :]
    angles = position * jnp.power(10000.0, -pair_index / half_size)
    zeta_base = (pair_index / half_size + 0.4) / 1.4
    growth = jnp.power(zeta_base, position / 512.0)
    return (jnp.cos(angles), jnp.sin(angles), growth)


def rotate(field, tables, inverse):
    cosine, sine_part, growth = tables
    half_size = field.shape[-1] // 2
    factor = 1.0 / growth if inverse else growth
    cosine = cosine[:, None, :]
    sine_part = sine_part[:, None, :]
    factor = factor[:, None, :]
    first_half = field[..., :half_size]
    second_half = field[..., half_size:]
    return jnp.concatenate(
        [
            (first_half * cosine - second_half * sine_part) * factor,
            (second_half * cosine + first_half * sine_part) * factor,
        ],
        -1,
    )


def gather_rows(field):
    return lax.all_gather(field, "mp", axis=0, tiled=True)


def sum_rows(field):
    return lax.psum_scatter(
        field.astype(jnp.bfloat16), "mp", scatter_dimension=0, tiled=True
    ).astype(jnp.float32)


def row_sums(first_sum, second):
    return lax.psum((first_sum, second), "mp")


def split_norm(field, scaling, width_total):
    first_sum, second = row_sums(jnp.sum(field, -1), jnp.sum(field * field, -1))
    average = (first_sum / width_total)[:, None]
    spread = (second / width_total)[:, None] - average * average
    factor = lax.rsqrt(spread + EPS)
    normed = (field - average) * factor
    return (normed * scaling, normed, factor)


def split_norm_back(gradient, normed, factor, scaling, width_total):
    scaled = gradient * scaling
    gain_grad = jnp.sum(gradient * normed, 0)
    first_sum, second = row_sums(jnp.sum(scaled, -1), jnp.sum(scaled * normed, -1))
    field_grad = factor * (
        scaled - (first_sum / width_total)[:, None] - normed * (second / width_total)[:, None]
    )
    return (field_grad, gain_grad)


def causal_scores(queries, keyset, factor):
    scores = (
        jnp.einsum("qhd,khd->hqk", queries, keyset, preferred_element_type=jnp.float32) * factor
    )
    length = queries.shape[0]
    row_ids = lax.broadcasted_iota(jnp.int32, (length, length), 0)
    col_ids = lax.broadcasted_iota(jnp.int32, (length, length), 1)
    return jnp.where((col_ids <= row_ids)[None], scores, -1e30)


def local(
    tokens,
    slot_index,
    out_grad,
    features,
    query_weight,
    key_weight,
    value_weight,
    output_weight,
    up_weight,
    down_weight,
    norm_input,
    norm_attention,
    norm_middle,
    norm_hidden,
    sampler_query,
    sampler_key,
    sampler_value,
    sampler_output,
    latents,
    norm_vision,
):
    fp32 = jnp.float32
    half_type = jnp.bfloat16
    factor = HD ** (-0.5)
    query_all, key_all, value_all, output_all, latents_all, vision_gain, input_gain, middle_gain = (
        lax.all_gather(sampler_query, ("dp", "mp", "img"), axis=0, tiled=True),
        lax.all_gather(sampler_key, ("dp", "mp", "img"), axis=0, tiled=True),
        lax.all_gather(sampler_value, ("dp", "mp", "img"), axis=0, tiled=True),
        lax.all_gather(sampler_output, ("dp", "mp", "img"), axis=0, tiled=True),
        lax.all_gather(latents, ("dp", "mp", "img"), axis=1, tiled=True),
        lax.all_gather(norm_vision, ("dp", "mp", "img"), axis=0, tiled=True),
        lax.all_gather(norm_input, ("dp", "mp", "img"), axis=0, tiled=True),
        lax.all_gather(norm_middle, ("dp", "mp", "img"), axis=0, tiled=True),
    )
    input_gain = input_gain.astype(fp32)
    middle_gain = middle_gain.astype(fp32)
    model_width = query_all.shape[1]
    head_all = model_width // HD
    images = features.shape[0]
    patches = features.shape[1]
    feature_rows = features.astype(fp32)
    vision_normed, vision_back = jax.vjp(layer_norm, feature_rows, vision_gain.astype(fp32))
    vision_low = vision_normed.astype(half_type)
    latent_query = jnp.dot(latents_all, query_all, preferred_element_type=fp32).astype(half_type)
    head_query = latent_query.reshape(LAT, head_all, HD)
    image_keys = jnp.einsum("ipv,vd->ipd", vision_low, key_all, preferred_element_type=fp32).astype(
        half_type
    )
    image_values = jnp.einsum(
        "ipv,vd->ipd", vision_low, value_all, preferred_element_type=fp32
    ).astype(half_type)
    keys_split = image_keys.reshape(images, patches, head_all, HD)
    values_split = image_values.reshape(images, patches, head_all, HD)
    pool_scores = (
        jnp.einsum("lhd,iphd->ihlp", head_query, keys_split, preferred_element_type=fp32) * factor
    )
    pool_probs = jax.nn.softmax(pool_scores, -1)
    pool_low = pool_probs.astype(half_type)
    pooled = (
        jnp.einsum("ihlp,iphd->ilhd", pool_low, values_split, preferred_element_type=fp32)
        .astype(half_type)
        .reshape(images, LAT, model_width)
    )
    pool_branch = jnp.einsum("ild,de->ile", pooled, output_all, preferred_element_type=fp32)
    embedded = (latents_all.astype(fp32)[None] + pool_branch).astype(half_type)
    row_table = lax.all_gather(embedded, ("mp", "img"), axis=0, tiled=True).reshape(-1, model_width)
    tables = rotary_tables(SEQ, HD)
    rotate_plain = partial(rotate, tables=tables, inverse=False)
    rotate_inverse = partial(rotate, tables=tables, inverse=True)
    layer_total = None
    input_total = jnp.zeros_like(input_gain)
    middle_total = jnp.zeros_like(middle_gain)
    slot_total = jnp.zeros(row_table.shape, fp32)
    outputs = []
    input_grads = []
    for micro_step in range(tokens.shape[0]):
        current = (
            lax.all_gather(query_weight, ("dp", "img"), axis=0, tiled=True),
            lax.all_gather(key_weight, ("dp", "img"), axis=0, tiled=True),
            lax.all_gather(value_weight, ("dp", "img"), axis=0, tiled=True),
            lax.all_gather(output_weight, ("dp", "img"), axis=1, tiled=True),
            lax.all_gather(up_weight, ("dp", "img"), axis=0, tiled=True),
            lax.all_gather(down_weight, ("dp", "img"), axis=1, tiled=True),
            lax.all_gather(norm_attention, ("dp", "img"), axis=1, tiled=True),
            lax.all_gather(norm_hidden, ("dp", "img"), axis=1, tiled=True),
        )
        wq_full, wk_full, wv_full, wo_full, up_full, down_full, attn_gain_rows, hidden_gain_rows = (
            current
        )
        attention_gain = attn_gain_rows.reshape(-1).astype(fp32)
        hidden_gain = hidden_gain_rows.reshape(-1).astype(fp32)
        local_width = wq_full.shape[1]
        local_heads = local_width // HD
        own_rows = tokens[micro_step].astype(fp32)
        slot_rows = slot_index[micro_step]
        is_image = (slot_rows >= 0)[:, None]
        picked = jnp.take(row_table, jnp.maximum(slot_rows, 0), axis=0).astype(fp32)
        entry_rows = jnp.where(is_image, picked, own_rows)
        first_norm, first_back = jax.vjp(layer_norm, entry_rows, input_gain)
        normed_rows = gather_rows(first_norm.astype(half_type))
        seq_len = normed_rows.shape[0]
        query_proj = jnp.dot(normed_rows, wq_full, preferred_element_type=fp32).reshape(
            seq_len, local_heads, HD
        )
        query_rot, query_back = jax.vjp(rotate_plain, query_proj)
        query_low = query_rot.astype(half_type)
        key_proj = jnp.dot(normed_rows, wk_full, preferred_element_type=fp32).reshape(
            seq_len, local_heads, HD
        )
        key_rot, key_back = jax.vjp(rotate_inverse, key_proj)
        key_low = key_rot.astype(half_type)
        value_low = (
            jnp.dot(normed_rows, wv_full, preferred_element_type=fp32)
            .astype(half_type)
            .reshape(seq_len, local_heads, HD)
        )
        scores = causal_scores(query_low, key_low, factor)
        highest = jnp.max(scores, -1, keepdims=True)
        exponent = jnp.exp(scores - highest)
        denominator = jnp.sum(exponent, -1, keepdims=True)
        logsum = highest + jnp.log(denominator)
        attention_probs = exponent / denominator
        attended = jnp.einsum(
            "hqk,khd->qhd",
            attention_probs.astype(half_type),
            value_low,
            preferred_element_type=fp32,
        ).reshape(seq_len, local_width)
        attn_scaled, attn_normed, attn_factor = split_norm(attended, attention_gain, D)
        attn_low = attn_scaled.astype(half_type)
        after_attention = entry_rows + sum_rows(
            jnp.dot(attn_low, wo_full, preferred_element_type=fp32)
        )
        middle_norm, middle_back = jax.vjp(layer_norm, after_attention, middle_gain)
        middle_rows = gather_rows(middle_norm.astype(half_type))
        upward = jnp.dot(middle_rows, up_full, preferred_element_type=fp32)
        activated, gelu_back = jax.vjp(exact_gelu, upward)
        hidden_scaled, hidden_normed, hidden_factor = split_norm(activated, hidden_gain, FF)
        hidden_low = hidden_scaled.astype(half_type)
        result = after_attention + sum_rows(
            jnp.dot(hidden_low, down_full, preferred_element_type=fp32)
        )
        outputs.append(result.astype(half_type))
        grad_own = out_grad[micro_step].astype(fp32)
        grad_rows = gather_rows(grad_own.astype(half_type))
        d_down = jnp.dot(hidden_low.T, grad_rows, preferred_element_type=fp32)
        d_hidden = jnp.dot(grad_rows, down_full.T, preferred_element_type=fp32)
        d_active, d_hgain = split_norm_back(d_hidden, hidden_normed, hidden_factor, hidden_gain, FF)
        d_upward = gelu_back(d_active)[0].astype(half_type)
        d_up = jnp.dot(middle_rows.T, d_upward, preferred_element_type=fp32)
        d_middle = sum_rows(jnp.dot(d_upward, up_full.T, preferred_element_type=fp32))
        d_after, d_mgain = middle_back(d_middle)
        d_after = d_after + grad_own
        after_rows = gather_rows(d_after.astype(half_type))
        d_output = jnp.dot(attn_low.T, after_rows, preferred_element_type=fp32)
        d_mixed = jnp.dot(after_rows, wo_full.T, preferred_element_type=fp32)
        d_attended, d_again = split_norm_back(d_mixed, attn_normed, attn_factor, attention_gain, D)
        d_att_low = d_attended.astype(half_type).reshape(seq_len, local_heads, HD)
        again_scores = causal_scores(query_low, key_low, factor)
        probs_again = jnp.exp(again_scores - logsum)
        d_probs = jnp.einsum("qhd,khd->hqk", d_att_low, value_low, preferred_element_type=fp32)
        d_value_low = (
            jnp.einsum(
                "hqk,qhd->khd",
                probs_again.astype(half_type),
                d_att_low,
                preferred_element_type=fp32,
            )
            .astype(half_type)
            .reshape(seq_len, local_width)
        )
        d_scores = (
            probs_again * (d_probs - jnp.sum(probs_again * d_probs, -1, keepdims=True))
        ).astype(half_type)
        d_query_rot = (
            jnp.einsum("hqk,khd->qhd", d_scores, key_low, preferred_element_type=fp32) * factor
        )
        d_key_rot = (
            jnp.einsum("hqk,qhd->khd", d_scores, query_low, preferred_element_type=fp32) * factor
        )
        d_query_low = query_back(d_query_rot)[0].reshape(seq_len, local_width).astype(half_type)
        d_key_low = key_back(d_key_rot)[0].reshape(seq_len, local_width).astype(half_type)
        d_wq = jnp.dot(normed_rows.T, d_query_low, preferred_element_type=fp32)
        d_wk = jnp.dot(normed_rows.T, d_key_low, preferred_element_type=fp32)
        d_wv = jnp.dot(normed_rows.T, d_value_low, preferred_element_type=fp32)
        d_first = (
            jnp.dot(d_query_low, wq_full.T, preferred_element_type=fp32)
            + jnp.dot(d_key_low, wk_full.T, preferred_element_type=fp32)
            + jnp.dot(d_value_low, wv_full.T, preferred_element_type=fp32)
        )
        d_entry, d_igain = first_back(sum_rows(d_first))
        d_entry = d_entry + d_after
        input_grads.append(jnp.where(is_image, 0.0, d_entry).astype(half_type))
        target_rows = jnp.where(slot_rows >= 0, slot_rows, row_table.shape[0])
        slot_total = slot_total.at[target_rows].add(d_entry, mode="drop")
        input_total = input_total + d_igain
        middle_total = middle_total + d_mgain
        pieces = (
            d_wq,
            d_wk,
            d_wv,
            d_output,
            d_up,
            d_down,
            d_again.reshape(-1, LANE),
            d_hgain.reshape(-1, LANE),
        )
        pieces = (
            lax.psum_scatter(
                pieces[0].astype(jnp.bfloat16), ("dp", "img"), scatter_dimension=0, tiled=True
            ).astype(jnp.float32),
            lax.psum_scatter(
                pieces[1].astype(jnp.bfloat16), ("dp", "img"), scatter_dimension=0, tiled=True
            ).astype(jnp.float32),
            lax.psum_scatter(
                pieces[2].astype(jnp.bfloat16), ("dp", "img"), scatter_dimension=0, tiled=True
            ).astype(jnp.float32),
            lax.psum_scatter(
                pieces[3].astype(jnp.bfloat16), ("dp", "img"), scatter_dimension=1, tiled=True
            ).astype(jnp.float32),
            lax.psum_scatter(
                pieces[4].astype(jnp.bfloat16), ("dp", "img"), scatter_dimension=0, tiled=True
            ).astype(jnp.float32),
            lax.psum_scatter(
                pieces[5].astype(jnp.bfloat16), ("dp", "img"), scatter_dimension=1, tiled=True
            ).astype(jnp.float32),
            lax.psum_scatter(
                pieces[6].astype(jnp.bfloat16), ("dp", "img"), scatter_dimension=1, tiled=True
            ).astype(jnp.float32),
            lax.psum_scatter(
                pieces[7].astype(jnp.bfloat16), ("dp", "img"), scatter_dimension=1, tiled=True
            ).astype(jnp.float32),
        )
        if layer_total is None:
            layer_total = pieces
        else:
            layer_total = tuple((left + right for left, right in zip(layer_total, pieces)))
    slot_grad = lax.psum_scatter(
        slot_total.reshape(-1, LAT, model_width).astype(jnp.bfloat16),
        ("mp", "img"),
        scatter_dimension=0,
        tiled=True,
    ).astype(jnp.float32)
    d_latent_rows = jnp.sum(slot_grad, 0)
    slot_low = slot_grad.astype(half_type)
    d_sampler_output = jnp.einsum("ild,ile->de", pooled, slot_low, preferred_element_type=fp32)
    d_pooled = (
        jnp.einsum("ile,de->ild", slot_low, output_all, preferred_element_type=fp32)
        .astype(half_type)
        .reshape(images, LAT, head_all, HD)
    )
    d_pool_probs = jnp.einsum(
        "ilhd,iphd->ihlp", d_pooled, values_split, preferred_element_type=fp32
    )
    d_image_values = (
        jnp.einsum("ihlp,ilhd->iphd", pool_low, d_pooled, preferred_element_type=fp32)
        .astype(half_type)
        .reshape(images, patches, model_width)
    )
    d_pool_scores = (
        pool_probs * (d_pool_probs - jnp.sum(pool_probs * d_pool_probs, -1, keepdims=True))
    ).astype(half_type)
    d_latent_query = (
        (
            jnp.einsum("ihlp,iphd->ilhd", d_pool_scores, keys_split, preferred_element_type=fp32)
            * factor
        )
        .astype(half_type)
        .reshape(images, LAT, model_width)
    )
    d_image_keys = (
        (
            jnp.einsum("ihlp,lhd->iphd", d_pool_scores, head_query, preferred_element_type=fp32)
            * factor
        )
        .astype(half_type)
        .reshape(images, patches, model_width)
    )
    d_sampler_query = jnp.einsum(
        "ld,ile->de", latents_all, d_latent_query, preferred_element_type=fp32
    )
    d_latents = d_latent_rows + jnp.einsum(
        "ile,de->ld", d_latent_query, query_all, preferred_element_type=fp32
    )
    d_sampler_key = jnp.einsum("ipv,ipd->vd", vision_low, d_image_keys, preferred_element_type=fp32)
    d_sampler_value = jnp.einsum(
        "ipv,ipd->vd", vision_low, d_image_values, preferred_element_type=fp32
    )
    d_vision = jnp.einsum(
        "ipd,vd->ipv", d_image_keys, key_all, preferred_element_type=fp32
    ) + jnp.einsum("ipd,vd->ipv", d_image_values, value_all, preferred_element_type=fp32)
    d_vgain = vision_back(d_vision)[1]
    shared_total = (
        lax.psum_scatter(d_sampler_query, ("dp", "mp", "img"), scatter_dimension=0, tiled=True),
        lax.psum_scatter(d_sampler_key, ("dp", "mp", "img"), scatter_dimension=0, tiled=True),
        lax.psum_scatter(d_sampler_value, ("dp", "mp", "img"), scatter_dimension=0, tiled=True),
        lax.psum_scatter(d_sampler_output, ("dp", "mp", "img"), scatter_dimension=0, tiled=True),
        lax.psum_scatter(d_latents, ("dp", "mp", "img"), scatter_dimension=1, tiled=True),
        lax.psum_scatter(d_vgain, ("dp", "mp", "img"), scatter_dimension=0, tiled=True),
        lax.psum_scatter(input_total, ("dp", "mp", "img"), scatter_dimension=0, tiled=True),
        lax.psum_scatter(middle_total, ("dp", "mp", "img"), scatter_dimension=0, tiled=True),
    )
    return (
        jnp.stack(outputs),
        jnp.stack(input_grads),
        layer_total[0],
        layer_total[1],
        layer_total[2],
        layer_total[3],
        layer_total[4],
        layer_total[5],
        shared_total[6],
        layer_total[6],
        shared_total[7],
        layer_total[7],
        shared_total[0],
        shared_total[1],
        shared_total[2],
        shared_total[3],
        shared_total[4],
        shared_total[5],
    )


def solution(mesh):
    in_specs = (
        P(("dp", "img"), "mp", None),
        P(("dp", "img"), "mp"),
        P(("dp", "img"), "mp", None),
        P(("dp", "mp", "img"), None, None),
        P(("dp", "img"), "mp"),
        P(("dp", "img"), "mp"),
        P(("dp", "img"), "mp"),
        P("mp", ("dp", "img")),
        P(("dp", "img"), "mp"),
        P("mp", ("dp", "img")),
        P(("dp", "mp", "img")),
        P("mp", ("dp", "img")),
        P(("dp", "mp", "img")),
        P("mp", ("dp", "img")),
        P(("dp", "mp", "img"), None),
        P(("dp", "mp", "img"), None),
        P(("dp", "mp", "img"), None),
        P(("dp", "mp", "img"), None),
        P(None, ("dp", "mp", "img")),
        P(("dp", "mp", "img")),
    )
    out_specs = (
        P(("dp", "img"), "mp", None),
        P(("dp", "img"), "mp", None),
        P(("dp", "img"), "mp"),
        P(("dp", "img"), "mp"),
        P(("dp", "img"), "mp"),
        P("mp", ("dp", "img")),
        P(("dp", "img"), "mp"),
        P("mp", ("dp", "img")),
        P(("dp", "mp", "img")),
        P("mp", ("dp", "img")),
        P(("dp", "mp", "img")),
        P("mp", ("dp", "img")),
        P(("dp", "mp", "img"), None),
        P(("dp", "mp", "img"), None),
        P(("dp", "mp", "img"), None),
        P(("dp", "mp", "img"), None),
        P(None, ("dp", "mp", "img")),
        P(("dp", "mp", "img")),
    )
    return jax.shard_map(local, mesh=mesh, in_specs=in_specs, out_specs=out_specs, check_vma=False)
```

profile of v0, /device:TPU:8, one launch (start us, length us, event | category | flops | bytes accessed | tf_op | source)
XLA Modules:
  0.0 2819.9 jit_solution(5220618721311750865)
XLA Ops:
  12.6 41.0 %all-reduce.19 = (bf16[1024]{0:T(1024)(128)(2,1)S(1)}, bf16[2048]{0:T(1024)(128)(2,1)S(1)}, bf16[2048]{0:T(1024)(128)(2,1)}) all-reduce(bf16[1024]{0:T(1024)(128)(2,1)S(1)} %dynamic-update-slice, bf16[2048]{0:T(1024)(128)(2,1)S(1)} %dynamic-update-slice.1, ...), channel_id=1, replica_groups=mesh['dp'=2,'mp'=4,'img'=4] {'dp','mp','img'}, use_global_device_ids=true, to_apply=%add.8 | all-reduce | flops 5120 | bytes 20480
  97.8 41.8 %all-gather.24.cloned.1.call-done = bf16[1024,2048]{1,0:T(8,128)(2,1)} async-done(((bf16[32,2048]{1,0:T(8,128)(2,1)}), bf16[1024,2048]{1,0:T(8,128)(2,1)}) %all-gather.24.cloned.1.call-update) | async-done | bytes 4194320 | tf_op jit(solution)/shard_map/all_gather | solution.py:129
  144.5 74.1 %all-gather.28.cloned.1.call-done = bf16[2048,2048]{1,0:T(8,128)(2,1)} async-done(((bf16[64,2048]{1,0:T(8,128)(2,1)}), bf16[2048,2048]{1,0:T(8,128)(2,1)}) %all-gather.28.cloned.1.call-update) | async-done | bytes 8388624 | tf_op jit(solution)/shard_map/all_gather | solution.py:127
  227.0 70.4 %all-gather.30.cloned.1.call-done = bf16[2048,2048]{1,0:T(8,128)(2,1)} async-done(((bf16[64,2048]{1,0:T(8,128)(2,1)}), bf16[2048,2048]{1,0:T(8,128)(2,1)}) %all-gather.30.cloned.1.call-update) | async-done | bytes 8388624 | tf_op jit(solution)/shard_map/all_gather | solution.py:130
  304.1 48.3 %all-gather.56.cloned.1.call-done = bf16[1024,2048]{1,0:T(8,128)(2,1)} async-done(((bf16[64,2048]{1,0:T(8,128)(2,1)}), bf16[1024,2048]{1,0:T(8,128)(2,1)}) %all-gather.56.cloned.1.call-update) | async-done | bytes 4194320 | tf_op jit(solution)/shard_map/all_gather | solution.py:167
  616.8 57.2 %all-gather.46.cloned.1.call-done = bf16[2048,2048]{1,0:T(8,128)(2,1)} async-done(((bf16[2048,256]{1,0:T(8,128)(2,1)}), bf16[2048,2048]{1,0:T(8,128)(2,1)}) %all-gather.46.cloned.1.call-update) | async-done | bytes 8388624 | tf_op jit(solution)/shard_map/all_gather | solution.py:184
  681.5 48.7 %all-gather.44.cloned.1.call-done = bf16[2048,2048]{1,0:T(8,128)(2,1)} async-done(((bf16[256,2048]{1,0:T(8,128)(2,1)}), bf16[2048,2048]{1,0:T(8,128)(2,1)}) %all-gather.44.cloned.1.call-update) | async-done | bytes 8388624 | tf_op jit(solution)/shard_map/all_gather | solution.py:183
  1357.4 42.2 %reduce-scatter.71.cloned.1.call-done = bf16[512,256]{1,0:T(8,128)(2,1)} async-done(((bf16[512,2048]{1,0:T(8,128)(2,1)}), bf16[512,256]{1,0:T(8,128)(2,1)}) %reduce-scatter.71.cloned.1.call-update) | async-done | bytes 262160 | tf_op jit(solution)/shard_map/reduce_scatter | solution.py:319
  1399.6 44.5 %reduce-scatter.73.cloned.1.call-done = bf16[512,256]{1,0:T(8,128)(2,1)} async-done(((bf16[512,2048]{1,0:T(8,128)(2,1)}), bf16[512,256]{1,0:T(8,128)(2,1)}) %reduce-scatter.73.cloned.1.call-update) | async-done | bytes 262160 | tf_op jit(solution)/shard_map/reduce_scatter | solution.py:319
  1446.0 43.0 %reduce-scatter.67.cloned.1.call-done = bf16[256,512]{1,0:T(8,128)(2,1)} async-done(((bf16[2048,512]{1,0:T(8,128)(2,1)}), bf16[256,512]{1,0:T(8,128)(2,1)}) %reduce-scatter.67.cloned.1.call-update) | async-done | bytes 262160 | tf_op jit(solution)/shard_map/reduce_scatter | solution.py:316
  1489.0 44.4 %reduce-scatter.69.cloned.1.call-done = bf16[256,512]{1,0:T(8,128)(2,1)} async-done(((bf16[2048,512]{1,0:T(8,128)(2,1)}), bf16[256,512]{1,0:T(8,128)(2,1)}) %reduce-scatter.69.cloned.1.call-update) | async-done | bytes 262160 | tf_op jit(solution)/shard_map/reduce_scatter | solution.py:316
  1535.3 42.8 %reduce-scatter.63.cloned.1.call-done = bf16[256,512]{1,0:T(8,128)(2,1)} async-done(((bf16[2048,512]{1,0:T(8,128)(2,1)}), bf16[256,512]{1,0:T(8,128)(2,1)}) %reduce-scatter.63.cloned.1.call-update) | async-done | bytes 262160 | tf_op jit(solution)/shard_map/reduce_scatter | solution.py:313
  1578.2 44.5 %reduce-scatter.65.cloned.1.call-done = bf16[256,512]{1,0:T(8,128)(2,1)} async-done(((bf16[2048,512]{1,0:T(8,128)(2,1)}), bf16[256,512]{1,0:T(8,128)(2,1)}) %reduce-scatter.65.cloned.1.call-update) | async-done | bytes 262160 | tf_op jit(solution)/shard_map/reduce_scatter | solution.py:313
  1624.6 42.8 %reduce-scatter.59.cloned.1.call-done = bf16[256,512]{1,0:T(8,128)(2,1)} async-done(((bf16[2048,512]{1,0:T(8,128)(2,1)}), bf16[256,512]{1,0:T(8,128)(2,1)}) %reduce-scatter.59.cloned.1.call-update) | async-done | bytes 262160 | tf_op jit(solution)/shard_map/reduce_scatter | solution.py:310
  1667.4 45.1 %reduce-scatter.61.cloned.1.call-done = bf16[256,512]{1,0:T(8,128)(2,1)} async-done(((bf16[2048,512]{1,0:T(8,128)(2,1)}), bf16[256,512]{1,0:T(8,128)(2,1)}) %reduce-scatter.61.cloned.1.call-update) | async-done | bytes 262160 | tf_op jit(solution)/shard_map/reduce_scatter | solution.py:310
  1719.6 39.8 %all-reduce.14 = (f32[2048]{0:T(1024)S(1)}, f32[2048]{0:T(1024)S(1)}, f32[1024]{0:T(1024)S(1)}) all-reduce(f32[2048]{0:T(1024)S(1)} %add.396, f32[2048]{0:T(1024)S(1)} %add.398, f32[1024]{0:T(1024)S(1)} %fusion.31), channel_id=25, replica_groups=mesh['dp'=2,'mp'=4,'img'=4] {'dp','mp','img'}, use_global_device_ids=true, to_apply=%region_80.82.clone | all-reduce | flops 5120 | bytes 40960
  1788.4 74.8 %reduce-scatter.79.cloned.1.call-done = bf16[2048,256]{1,0:T(8,128)(2,1)} async-done(((bf16[2048,2048]{1,0:T(8,128)(2,1)}), bf16[2048,256]{1,0:T(8,128)(2,1)}) %reduce-scatter.79.cloned.1.call-update) | async-done | bytes 1048592 | tf_op jit(solution)/shard_map/reduce_scatter | solution.py:325
  1866.2 71.9 %reduce-scatter.77.cloned.1.call-done = bf16[256,2048]{1,0:T(8,128)(2,1)} async-done(((bf16[2048,2048]{1,0:T(8,128)(2,1)}), bf16[256,2048]{1,0:T(8,128)(2,1)}) %reduce-scatter.77.cloned.1.call-update) | async-done | bytes 1048592 | tf_op jit(solution)/shard_map/reduce_scatter | solution.py:322
  1938.1 74.8 %reduce-scatter.75.cloned.1.call-done = bf16[256,2048]{1,0:T(8,128)(2,1)} async-done(((bf16[2048,2048]{1,0:T(8,128)(2,1)}), bf16[256,2048]{1,0:T(8,128)(2,1)}) %reduce-scatter.75.cloned.1.call-update) | async-done | bytes 1048592 | tf_op jit(solution)/shard_map/reduce_scatter | solution.py:322
  2016.1 123.9 %reduce-scatter.101.cloned.1.call-done = f32[64,64]{1,0:T(8,128)} async-done(((f32[2048,64]{1,0:T(8,128)}), f32[64,64]{1,0:T(8,128)}) %reduce-scatter.101.cloned.1.call-update) | async-done | bytes 16400
  2141.5 146.3 %reduce-scatter.87.cloned.1.call-done = f32[32,2048]{1,0:T(8,128)} async-done(((f32[1024,2048]{1,0:T(8,128)}), f32[32,2048]{1,0:T(8,128)}) %reduce-scatter.87.cloned.1.call-update) | async-done | bytes 262160 | tf_op jit(solution)/shard_map/reduce_scatter | solution.py:397
  2287.8 148.2 %reduce-scatter.85.cloned.1.call-done = f32[32,2048]{1,0:T(8,128)} async-done(((f32[1024,2048]{1,0:T(8,128)}), f32[32,2048]{1,0:T(8,128)}) %reduce-scatter.85.cloned.1.call-update) | async-done | bytes 262160 | tf_op jit(solution)/shard_map/reduce_scatter | solution.py:396
  2436.0 189.9 %reduce-scatter.99.cloned.1.call-done = f32[64,2048]{1,0:T(8,128)} async-done(((f32[2048,2048]{1,0:T(8,128)}), f32[64,2048]{1,0:T(8,128)}) %reduce-scatter.99.cloned.1.call-update) | async-done | bytes 524304
  2625.9 186.7 %reduce-scatter.89.cloned.1.call-done = f32[64,2048]{1,0:T(8,128)} async-done(((f32[2048,2048]{1,0:T(8,128)}), f32[64,2048]{1,0:T(8,128)}) %reduce-scatter.89.cloned.1.call-update) | async-done | bytes 524304 | tf_op jit(solution)/shard_map/reduce_scatter | solution.py:398
  (677 shorter events, 1015.2 us)
Async XLA Ops:
  8.7 209.9 %all-gather.28.cloned.1.call-start = ((), (), s32[]{:S(2)}) async-start(), calls=%async_computation.32 | async-start | bytes 8650752 | tf_op jit(solution)/shard_map/all_gather | solution.py:127
  9.4 288.0 %all-gather.30.cloned.1.call-start = ((), (), s32[]{:S(2)}) async-start(), calls=%async_computation.33 | async-start | bytes 8650752 | tf_op jit(solution)/shard_map/all_gather | solution.py:130
  10.0 342.4 %all-gather.56.cloned.1.call-start = ((), (), s32[]{:S(2)}) async-start(), calls=%async_computation.70 | async-start | bytes 4456448 | tf_op jit(solution)/shard_map/all_gather | solution.py:167
  541.8 218.4 %all-gather.50.cloned.1.call-start = ((), (), s32[]{:S(2)}) async-start(), calls=%async_computation.46 | async-start | bytes 1310720 | tf_op jit(solution)/shard_map/all_gather | solution.py:59
  591.5 228.0 %all-gather.58.cloned.1.call-start = ((), (), s32[]{:S(2)}) async-start(), calls=%async_computation.71 | async-start | bytes 1310720 | tf_op jit(solution)/shard_map/all_gather | solution.py:59
  592.2 287.8 %reduce-scatter.55.cloned.1.call-start = ((), (), s32[]{:S(2)}) async-start(), calls=%async_computation.51 | async-start | bytes 1310720 | tf_op jit(solution)/shard_map/reduce_scatter | solution.py:63
  1147.2 207.7 %reduce-scatter.93.cloned.1.call-start = ((), (), s32[]{:S(2)}) async-start(), calls=%async_computation.74 | async-start | bytes 36864
  1148.0 251.6 %reduce-scatter.71.cloned.1.call-start = ((), (), s32[]{:S(2)}) async-start(), calls=%async_computation.60 | async-start | bytes 2359296 | tf_op jit(solution)/shard_map/reduce_scatter | solution.py:319
  1151.7 292.5 %reduce-scatter.73.cloned.1.call-start = ((), (), s32[]{:S(2)}) async-start(), calls=%async_computation.61 | async-start | bytes 2359296 | tf_op jit(solution)/shard_map/reduce_scatter | solution.py:319
  1154.0 335.1 %reduce-scatter.67.cloned.1.call-start = ((), (), s32[]{:S(2)}) async-start(), calls=%async_computation.58 | async-start | bytes 2359296 | tf_op jit(solution)/shard_map/reduce_scatter | solution.py:316
  1156.3 377.1 %reduce-scatter.69.cloned.1.call-start = ((), (), s32[]{:S(2)}) async-start(), calls=%async_computation.59 | async-start | bytes 2359296 | tf_op jit(solution)/shard_map/reduce_scatter | solution.py:316
  1158.5 419.7 %reduce-scatter.63.cloned.1.call-start = ((), (), s32[]{:S(2)}) async-start(), calls=%async_computation.56 | async-start | bytes 2359296 | tf_op jit(solution)/shard_map/reduce_scatter | solution.py:313
  1160.8 461.8 %reduce-scatter.65.cloned.1.call-start = ((), (), s32[]{:S(2)}) async-start(), calls=%async_computation.57 | async-start | bytes 2359296 | tf_op jit(solution)/shard_map/reduce_scatter | solution.py:313
  1163.0 504.4 %reduce-scatter.59.cloned.1.call-start = ((), (), s32[]{:S(2)}) async-start(), calls=%async_computation.54 | async-start | bytes 2359296 | tf_op jit(solution)/shard_map/reduce_scatter | solution.py:310
  1165.2 547.3 %reduce-scatter.61.cloned.1.call-start = ((), (), s32[]{:S(2)}) async-start(), calls=%async_computation.55 | async-start | bytes 2359296 | tf_op jit(solution)/shard_map/reduce_scatter | solution.py:310
  1167.4 621.0 %reduce-scatter.81.cloned.1.call-start = ((), (), s32[]{:S(2)}) async-start(), calls=%async_computation.65 | async-start | bytes 9437184 | tf_op jit(solution)/shard_map/reduce_scatter | solution.py:325
  1174.5 688.7 %reduce-scatter.79.cloned.1.call-start = ((), (), s32[]{:S(2)}) async-start(), calls=%async_computation.64 | async-start | bytes 9437184 | tf_op jit(solution)/shard_map/reduce_scatter | solution.py:325
  1182.5 755.6 %reduce-scatter.77.cloned.1.call-start = ((), (), s32[]{:S(2)}) async-start(), calls=%async_computation.63 | async-start | bytes 9437184 | tf_op jit(solution)/shard_map/reduce_scatter | solution.py:322
  1189.8 823.1 %reduce-scatter.75.cloned.1.call-start = ((), (), s32[]{:S(2)}) async-start(), calls=%async_computation.62 | async-start | bytes 9437184 | tf_op jit(solution)/shard_map/reduce_scatter | solution.py:322
  1197.0 943.1 %reduce-scatter.101.cloned.1.call-start = ((), (), s32[]{:S(2)}) async-start(), calls=%async_computation.78 | async-start | bytes 1081344
  1236.5 1051.3 %reduce-scatter.87.cloned.1.call-start = ((), (), s32[]{:S(2)}) async-start(), calls=%async_computation.68 | async-start | bytes 8650752 | tf_op jit(solution)/shard_map/reduce_scatter | solution.py:397
  1244.4 1191.6 %reduce-scatter.85.cloned.1.call-start = ((), (), s32[]{:S(2)}) async-start(), calls=%async_computation.67 | async-start | bytes 8650752 | tf_op jit(solution)/shard_map/reduce_scatter | solution.py:396
  1252.0 1373.9 %reduce-scatter.99.cloned.1.call-start = ((), (), s32[]{:S(2)}) async-start(), calls=%async_computation.77 | async-start | bytes 17301504
  1278.8 1533.9 %reduce-scatter.89.cloned.1.call-start = ((), (), s32[]{:S(2)}) async-start(), calls=%async_computation.69 | async-start | bytes 17301504 | tf_op jit(solution)/shard_map/reduce_scatter | solution.py:398
  (198 other events, 6334.4 us)
Sparse Core Ops, SparseCore 0:
  10.9 65.2 all-gather.25
  79.0 60.6 all-gather.23
  142.5 76.1 all-gather.27
  221.3 76.0 all-gather.29
  303.3 49.1 all-gather.55
  618.6 55.4 all-gather.45
  675.8 54.3 all-gather.43
  1144.4 72.6 reduce-scatter.82
  1358.4 41.2 reduce-scatter.70
  1402.9 41.2 reduce-scatter.72
  1447.8 41.2 reduce-scatter.66
  1492.2 41.1 reduce-scatter.68
  1536.9 41.2 reduce-scatter.62
  1581.4 41.1 reduce-scatter.64
  1626.2 41.2 reduce-scatter.58
  1716.4 71.9 reduce-scatter.80
  1791.8 71.2 reduce-scatter.78
  1866.9 71.2 reduce-scatter.76
  1941.6 71.2 reduce-scatter.74
  2015.1 124.9 reduce-scatter.100
  2142.8 144.9 reduce-scatter.86
  2290.5 145.4 reduce-scatter.84
  2438.7 187.1 reduce-scatter.98
  2628.6 183.9 reduce-scatter.88
  (25 shorter events, 700.5 us)
where the time goes:
time: 2830 us; the launch traced here: 2820 us
  waiting for transfers between devices  2230 us (79%)
  matrix products  222 us (8%)
  blocking collectives  177 us (6%)
  other arithmetic  90.8 us (3%)
  local copies, waits for them, and re-layouts  75.8 us (3%)
    unnamed x55, waiting for transfers between devices  385 us
    reduce_scatter x1, waiting for transfers between devices, local(): lax.psum_scatter(d_sampler_output, ('dp', 'mp', 'img'), scatter_dimension...  187 us
    all_gather x8, waiting for transfers between devices, gather_rows(): return lax.all_gather(field, 'mp', axis=0, tiled=True)  173 us
    reduce_scatter x8, waiting for transfers between devices, sum_rows(): lax.psum_scatter(field.astype(jnp.bfloat16), 'mp', scatter_dimension=0, t...  172 us
    reduce_scatter x1, waiting for transfers between devices, local(): lax.psum_scatter(d_sampler_key, ('dp', 'mp', 'img'), scatter_dimension=0,...  148 us
    reduce_scatter x2, waiting for transfers between devices, local(): lax.psum_scatter(pieces[4].astype(jnp.bfloat16), ('dp', 'img'), scatter_d...  147 us
    reduce_scatter x1, waiting for transfers between devices, local(): lax.psum_scatter(d_sampler_value, ('dp', 'mp', 'img'), scatter_dimension=...  146 us
    reduce_scatter x2, waiting for transfers between devices, local(): lax.psum_scatter(pieces[5].astype(jnp.bfloat16), ('dp', 'img'), scatter_d...  102 us
  transfers between devices with their start and end apart: 49, of which 46 were waited for; matrix products, arithmetic and copies ran while one was open for 10% of the time, Pallas kernels for 0%

commit v1 on v0

--- a/solution.py
+++ b/solution.py
@@ -2,9 +2,13 @@
 
 import jax
 import jax.numpy as jnp
+import numpy as np
 from jax import lax
+from jax.experimental import pallas as pl
+from jax.experimental.pallas import tpu as pltpu
 from jax.sharding import PartitionSpec as P
 
+DP, MP, IMG = "dp", "mp", "img"
 D = 2048
 FF = 8192
 HD = 64
@@ -56,17 +60,17 @@
 
 
 def gather_rows(field):
-    return lax.all_gather(field, "mp", axis=0, tiled=True)
+    return lax.all_gather(field, MP, axis=0, tiled=True)
 
 
 def sum_rows(field):
     return lax.psum_scatter(
-        field.astype(jnp.bfloat16), "mp", scatter_dimension=0, tiled=True
+        field.astype(jnp.bfloat16), MP, scatter_dimension=0, tiled=True
     ).astype(jnp.float32)
 
 
 def row_sums(first_sum, second):
-    return lax.psum((first_sum, second), "mp")
+    return lax.psum((first_sum, second), MP)
 
 
 def split_norm(field, scaling, width_total):
@@ -124,14 +128,14 @@
     half_type = jnp.bfloat16
     factor = HD ** (-0.5)
     query_all, key_all, value_all, output_all, latents_all, vision_gain, input_gain, middle_gain = (
-        lax.all_gather(sampler_query, ("dp", "mp", "img"), axis=0, tiled=True),
-        lax.all_gather(sampler_key, ("dp", "mp", "img"), axis=0, tiled=True),
-        lax.all_gather(sampler_value, ("dp", "mp", "img"), axis=0, tiled=True),
-        lax.all_gather(sampler_output, ("dp", "mp", "img"), axis=0, tiled=True),
-        lax.all_gather(latents, ("dp", "mp", "img"), axis=1, tiled=True),
-        lax.all_gather(norm_vision, ("dp", "mp", "img"), axis=0, tiled=True),
-        lax.all_gather(norm_input, ("dp", "mp", "img"), axis=0, tiled=True),
-        lax.all_gather(norm_middle, ("dp", "mp", "img"), axis=0, tiled=True),
+        lax.all_gather(sampler_query, (DP, MP, IMG), axis=0, tiled=True),
+        lax.all_gather(sampler_key, (DP, MP, IMG), axis=0, tiled=True),
+        lax.all_gather(sampler_value, (DP, MP, IMG), axis=0, tiled=True),
+        lax.all_gather(sampler_output, (DP, MP, IMG), axis=0, tiled=True),
+        lax.all_gather(latents, (DP, MP, IMG), axis=1, tiled=True),
+        lax.all_gather(norm_vision, (DP, MP, IMG), axis=0, tiled=True),
+        lax.all_gather(norm_input, (DP, MP, IMG), axis=0, tiled=True),
+        lax.all_gather(norm_middle, (DP, MP, IMG), axis=0, tiled=True),
     )
     input_gain = input_gain.astype(fp32)
     middle_gain = middle_gain.astype(fp32)
@@ -164,7 +168,7 @@
     )
     pool_branch = jnp.einsum("ild,de->ile", pooled, output_all, preferred_element_type=fp32)
     embedded = (latents_all.astype(fp32)[None] + pool_branch).astype(half_type)
-    row_table = lax.all_gather(embedded, ("mp", "img"), axis=0, tiled=True).reshape(-1, model_width)
+    row_table = lax.all_gather(embedded, (MP, IMG), axis=0, tiled=True).reshape(-1, model_width)
     tables = rotary_tables(SEQ, HD)
     rotate_plain = partial(rotate, tables=tables, inverse=False)
     rotate_inverse = partial(rotate, tables=tables, inverse=True)
@@ -176,14 +180,14 @@
     input_grads = []
     for micro_step in range(tokens.shape[0]):
         current = (
-            lax.all_gather(query_weight, ("dp", "img"), axis=0, tiled=True),
-            lax.all_gather(key_weight, ("dp", "img"), axis=0, tiled=True),
-            lax.all_gather(value_weight, ("dp", "img"), axis=0, tiled=True),
-            lax.all_gather(output_weight, ("dp", "img"), axis=1, tiled=True),
-            lax.all_gather(up_weight, ("dp", "img"), axis=0, tiled=True),
-            lax.all_gather(down_weight, ("dp", "img"), axis=1, tiled=True),
-            lax.all_gather(norm_attention, ("dp", "img"), axis=1, tiled=True),
-            lax.all_gather(norm_hidden, ("dp", "img"), axis=1, tiled=True),
+            lax.all_gather(query_weight, (DP, IMG), axis=0, tiled=True),
+            lax.all_gather(key_weight, (DP, IMG), axis=0, tiled=True),
+            lax.all_gather(value_weight, (DP, IMG), axis=0, tiled=True),
+            lax.all_gather(output_weight, (DP, IMG), axis=1, tiled=True),
+            lax.all_gather(up_weight, (DP, IMG), axis=0, tiled=True),
+            lax.all_gather(down_weight, (DP, IMG), axis=1, tiled=True),
+            lax.all_gather(norm_attention, (DP, IMG), axis=1, tiled=True),
+            lax.all_gather(norm_hidden, (DP, IMG), axis=1, tiled=True),
         )
         wq_full, wk_full, wv_full, wo_full, up_full, down_full, attn_gain_rows, hidden_gain_rows = (
             current
@@ -308,28 +312,28 @@
         )
         pieces = (
             lax.psum_scatter(
-                pieces[0].astype(jnp.bfloat16), ("dp", "img"), scatter_dimension=0, tiled=True
+                pieces[0].astype(jnp.bfloat16), (DP, IMG), scatter_dimension=0, tiled=True
             ).astype(jnp.float32),
             lax.psum_scatter(
-                pieces[1].astype(jnp.bfloat16), ("dp", "img"), scatter_dimension=0, tiled=True
+                pieces[1].astype(jnp.bfloat16), (DP, IMG), scatter_dimension=0, tiled=True
             ).astype(jnp.float32),
             lax.psum_scatter(
-                pieces[2].astype(jnp.bfloat16), ("dp", "img"), scatter_dimension=0, tiled=True
+                pieces[2].astype(jnp.bfloat16), (DP, IMG), scatter_dimension=0, tiled=True
             ).astype(jnp.float32),
             lax.psum_scatter(
-                pieces[3].astype(jnp.bfloat16), ("dp", "img"), scatter_dimension=1, tiled=True
+                pieces[3].astype(jnp.bfloat16), (DP, IMG), scatter_dimension=1, tiled=True
             ).astype(jnp.float32),
             lax.psum_scatter(
-                pieces[4].astype(jnp.bfloat16), ("dp", "img"), scatter_dimension=0, tiled=True
+                pieces[4].astype(jnp.bfloat16), (DP, IMG), scatter_dimension=0, tiled=True
             ).astype(jnp.float32),
             lax.psum_scatter(
-                pieces[5].astype(jnp.bfloat16), ("dp", "img"), scatter_dimension=1, tiled=True
+                pieces[5].astype(jnp.bfloat16), (DP, IMG), scatter_dimension=1, tiled=True
             ).astype(jnp.float32),
             lax.psum_scatter(
-                pieces[6].astype(jnp.bfloat16), ("dp", "img"), scatter_dimension=1, tiled=True
+                pieces[6].astype(jnp.bfloat16), (DP, IMG), scatter_dimension=1, tiled=True
             ).astype(jnp.float32),
             lax.psum_scatter(
-                pieces[7].astype(jnp.bfloat16), ("dp", "img"), scatter_dimension=1, tiled=True
+                pieces[7].astype(jnp.bfloat16), (DP, IMG), scatter_dimension=1, tiled=True
             ).astype(jnp.float32),
         )
         if layer_total is None:
@@ -338,7 +342,7 @@
             layer_total = tuple((left + right for left, right in zip(layer_total, pieces)))
     slot_grad = lax.psum_scatter(
         slot_total.reshape(-1, LAT, model_width).astype(jnp.bfloat16),
-        ("mp", "img"),
+        (MP, IMG),
         scatter_dimension=0,
         tiled=True,
     ).astype(jnp.float32)
@@ -392,14 +396,14 @@
     ) + jnp.einsum("ipd,vd->ipv", d_image_values, value_all, preferred_element_type=fp32)
     d_vgain = vision_back(d_vision)[1]
     shared_total = (
-        lax.psum_scatter(d_sampler_query, ("dp", "mp", "img"), scatter_dimension=0, tiled=True),
-        lax.psum_scatter(d_sampler_key, ("dp", "mp", "img"), scatter_dimension=0, tiled=True),
-        lax.psum_scatter(d_sampler_value, ("dp", "mp", "img"), scatter_dimension=0, tiled=True),
-        lax.psum_scatter(d_sampler_output, ("dp", "mp", "img"), scatter_dimension=0, tiled=True),
-        lax.psum_scatter(d_latents, ("dp", "mp", "img"), scatter_dimension=1, tiled=True),
-        lax.psum_scatter(d_vgain, ("dp", "mp", "img"), scatter_dimension=0, tiled=True),
-        lax.psum_scatter(input_total, ("dp", "mp", "img"), scatter_dimension=0, tiled=True),
-        lax.psum_scatter(middle_total, ("dp", "mp", "img"), scatter_dimension=0, tiled=True),
+        lax.psum_scatter(d_sampler_query, (DP, MP, IMG), scatter_dimension=0, tiled=True),
+        lax.psum_scatter(d_sampler_key, (DP, MP, IMG), scatter_dimension=0, tiled=True),
+        lax.psum_scatter(d_sampler_value, (DP, MP, IMG), scatter_dimension=0, tiled=True),
+        lax.psum_scatter(d_sampler_output, (DP, MP, IMG), scatter_dimension=0, tiled=True),
+        lax.psum_scatter(d_latents, (DP, MP, IMG), scatter_dimension=1, tiled=True),
+        lax.psum_scatter(d_vgain, (DP, MP, IMG), scatter_dimension=0, tiled=True),
+        lax.psum_scatter(input_total, (DP, MP, IMG), scatter_dimension=0, tiled=True),
+        lax.psum_scatter(middle_total, (DP, MP, IMG), scatter_dimension=0, tiled=True),
     )
     return (
         jnp.stack(outputs),
@@ -423,47 +427,1664 @@
     )
 
 
+MESH = pl.DeviceIdType.MESH
+VMEM = pltpu.VMEM
+BIG = 60 * 2**20
+
+
+class Wire:
+    def __init__(self, send, recv):
+        self.send, self.recv, self.used, self.sent = send, recv, 0, []
+
+    def take(self, count=1):
+        first = self.used
+        self.used += count
+        return first
+
+    def copy(self, src, dst, where, at):
+        return pltpu.make_async_remote_copy(
+            src_ref=src,
+            dst_ref=dst,
+            send_sem=self.send.at[at],
+            recv_sem=self.recv.at[at],
+            device_id=where,
+            device_id_type=MESH,
+        )
+
+    def go(self, make, when=None):
+        self.sent.append((make, when))
+        if when is None:
+            make().start()
+        else:
+            pl.when(when)(lambda: make().start())
+
+    def finish(self):
+        for make, when in self.sent:
+            if when is None:
+                make().wait_send()
+            else:
+                pl.when(when)(lambda make=make: make().wait_send())
+
+
+def greet(partners):
+    barrier = pltpu.get_barrier_semaphore()
+    for partner in partners:
+        pl.semaphore_signal(barrier, inc=1, device_id=partner, device_id_type=MESH)
+    pl.semaphore_wait(barrier, len(partners))
+
+
+class Spot:
+    def __init__(self, n_mp):
+        self.n = n_mp
+        self.y, self.z, self.img = lax.axis_index(DP), lax.axis_index(MP), lax.axis_index(IMG)
+        self.x, self.c = self.img // 2, lax.rem(self.img, 2)
+        self.p = self.y * 4 + self.img
+        self.right = {MP: lax.rem(self.z + 1, n_mp)}
+        self.left = {MP: lax.rem(self.z + n_mp - 1, n_mp)}
+
+    def other(self, flip):
+        fy, fx, fc = flip
+        y = 1 - self.y if fy else self.y
+        x = 1 - self.x if fx else self.x
+        c = 1 - self.c if fc else self.c
+        return y, x, c
+
+    def place(self, flip):
+        y, x, c = self.other(flip)
+        return y * 4 + x * 2 + c
+
+    def device(self, flip):
+        y, x, c = self.other(flip)
+        return {DP: y, IMG: x * 2 + c}
+
+    def plane_others(self):
+        return [self.device(f) for f in FLIPS]
+
+    def line_others(self):
+        return [{MP: lax.rem(self.z + d, self.n)} for d in range(1, self.n)]
+
+
+X, Y, C, XY = (0, 1, 0), (1, 0, 0), (0, 0, 1), (1, 1, 0)
+FLIPS = [(a, b, c) for a in (0, 1) for b in (0, 1) for c in (0, 1) if (a, b, c) != (0, 0, 0)]
+
+
+class LineGather:
+    def __init__(self, wire, spot, ref):
+        self.wire, self.spot, self.ref = wire, spot, ref
+        self.n = spot.n
+        self.base = (wire.take(self.n - 1), wire.take(self.n - 1))
+
+    def make(self, way, hop):
+        block = self.block(way, hop)
+        where = self.spot.right if way == 0 else self.spot.left
+        return self.wire.copy(self.ref(block), self.ref(block), where, self.base[way] + hop)
+
+    def block(self, way, hop):
+        return self.spot.z - hop if way == 0 else self.spot.z + hop
+
+    def there(self, way, hop):
+        block = self.block(way, hop)
+        return block >= 0 if way == 0 else block < self.n
+
+    def stage(self, hop, arrived=None):
+        for way in (0, 1):
+            if hop > 0:
+
+                def take(way=way):
+                    block = self.block(way, hop)
+                    self.wire.copy(
+                        self.ref(block),
+                        self.ref(block),
+                        self.spot.right if way == 0 else self.spot.left,
+                        self.base[way] + hop - 1,
+                    ).wait_recv()
+
+                pl.when(self.there(way, hop))(take)
+            if hop < self.n - 1:
+                can = self.spot.z < self.n - 1 if way == 0 else self.spot.z > 0
+                self.wire.go(partial(self.make, way, hop), jnp.logical_and(self.there(way, hop), can))
+            if hop > 0 and arrived is not None:
+                pl.when(self.there(way, hop))(
+                    lambda way=way: arrived(self.block(way, hop))
+                )
+
+
+class LineScatter:
+    def __init__(self, wire, spot, part, land, hold):
+        self.wire, self.spot, self.part, self.land, self.hold = wire, spot, part, land, hold
+        self.n = spot.n
+        self.base = (wire.take(self.n), wire.take(self.n))
+
+    def move(self, way, owner, src):
+        where = self.spot.right if way == 0 else self.spot.left
+        return self.wire.copy(src, self.land(way, owner), where, self.base[way] + owner)
+
+    def relay(self, ready=None):
+        n, z = self.n, self.spot.z
+        fresh = set()
+        for step in range(n - 1):
+            for way in (0, 1):
+                owner = n - 1 - step if way == 0 else step
+                if ready is not None and owner not in fresh:
+                    fresh.add(owner)
+                    ready(owner)
+                end = 0 if way == 0 else n - 1
+                self.wire.go(
+                    lambda way=way, owner=owner: self.move(way, owner, self.part(owner)), z == end
+                )
+                inner = jnp.logical_and(z > 0, z < owner) if way == 0 else jnp.logical_and(z < n - 1, z > owner)
+
+                def add(way=way, owner=owner):
+                    self.move(way, owner, self.hold(way, owner)).wait_recv()
+                    total = self.part(owner)[...].astype(jnp.float32) + self.land(way, owner)[...].astype(
+                        jnp.float32
+                    )
+                    self.hold(way, owner)[...] = total.astype(jnp.bfloat16)
+
+                pl.when(inner)(add)
+                self.wire.go(
+                    lambda way=way, owner=owner: self.move(way, owner, self.hold(way, owner)), inner
+                )
+
+    def own(self, total):
+        n, z = self.n, self.spot.z
+        total[...] = self.part(z)[...].astype(jnp.float32)
+        for way in (0, 1):
+
+            def add(way=way):
+                self.move(way, z, self.part(z)).wait_recv()
+                total[...] += self.land(way, z)[...].astype(jnp.float32)
+
+            pl.when(z > 0 if way == 0 else z < n - 1)(add)
+
+
+class PlaneGather:
+    def __init__(self, wire, spot, ref, chunks=1):
+        self.wire, self.spot, self.ref = wire, spot, ref
+        self.at = [wire.take(8) for _ in range(chunks)]
+
+    def make(self, chunk, flip_block, to, half, at):
+        block = self.ref(self.spot.place(flip_block), chunk, half)
+        return self.wire.copy(block, block, self.spot.device(to), self.at[chunk] + at)
+
+    def begin(self, chunk=0):
+        own = (0, 0, 0)
+        self.wire.go(partial(self.make, chunk, own, X, None, 0))
+        self.wire.go(partial(self.make, chunk, own, Y, None, 1))
+        self.wire.go(partial(self.make, chunk, own, C, None, 2))
+
+    def middle(self, chunk=0):
+        self.make(chunk, X, X, None, 0).wait_recv()
+        self.wire.go(partial(self.make, chunk, X, Y, 0, 3))
+        self.wire.go(partial(self.make, chunk, X, C, None, 4))
+        self.make(chunk, Y, Y, None, 1).wait_recv()
+        self.wire.go(partial(self.make, chunk, Y, X, 1, 5))
+        self.wire.go(partial(self.make, chunk, Y, C, None, 6))
+
+    def end(self, chunk=0):
+        self.make(chunk, XY, Y, 0, 3).wait_recv()
+        self.make(chunk, XY, X, 1, 5).wait_recv()
+        self.wire.go(partial(self.make, chunk, XY, C, None, 7))
+
+    def core(self, chunk=0):
+        for flip, at in (((0, 0, 1), 2), ((0, 1, 1), 4), ((1, 0, 1), 6), ((1, 1, 1), 7)):
+            self.make(chunk, flip, C, None, at).wait_recv()
+
+
+def chunked(array, chunks):
+    rows = array.shape[1] // chunks
+
+    def ref(block, chunk, half):
+        if half is None:
+            return array.at[block, pl.ds(chunk * rows, rows)]
+        return array.at[block, pl.ds(chunk * rows + half * (rows // 2), rows // 2)]
+
+    return ref
+
+
+class Steps:
+    def __init__(self):
+        self.steps = []
+
+    def add(self, time, step):
+        self.steps.append((time, len(self.steps), step))
+
+    def run(self):
+        for _, _, step in sorted(self.steps, key=lambda entry: entry[:2]):
+            step()
+
+
+class Line:
+    def __init__(self, n, cycle, chunk, at, part, land, rows):
+        self.n, self.cycle, self.chunk, self.at = n, cycle, chunk, at
+        self.part, self.land, self.rows = part, land, rows
+
+    def sum_time(self, way, z, owner):
+        from_end = z if way == 0 else self.n - 1 - z
+        order = self.n - 1 - owner if way == 0 else owner
+        return self.cycle * self.chunk + order + HOP * from_end
+
+    def settle_time(self, z):
+        times = []
+        if z > 0:
+            times.append(self.sum_time(0, z - 1, z))
+        if z < self.n - 1:
+            times.append(self.sum_time(1, z + 1, z))
+        return max(times) + HOP
+
+    def sums(self, steps, wire, spot, z):
+        n = self.n
+        for way in (0, 1):
+            ahead = range(z + 1, n) if way == 0 else range(z)
+            first = z == 0 if way == 0 else z == n - 1
+            for owner in ahead:
+                steps.add(self.sum_time(way, z, owner), partial(self.pass_sum, wire, spot, way, owner, first))
+
+    def sum_copy(self, wire, spot, way, owner, src):
+        where = spot.right if way == 0 else spot.left
+        return wire.copy(src, self.land(way, owner), where, self.at + way * self.n + owner)
+
+    def pass_sum(self, wire, spot, way, owner, first):
+        if first:
+            src = self.part(owner)
+        else:
+            src = self.land(way, owner)
+            self.sum_copy(wire, spot, way, owner, src).wait_recv()
+            total = self.part(owner)[...].astype(jnp.float32) + src[...].astype(jnp.float32)
+            src[...] = total.astype(jnp.bfloat16)
+        wire.go(partial(self.sum_copy, wire, spot, way, owner, src))
+
+    def own(self, wire, spot, z):
+        total = self.part(z)[...].astype(jnp.float32)
+        for way in (0, 1):
+            if z > 0 if way == 0 else z < self.n - 1:
+                self.sum_copy(wire, spot, way, z, self.part(z)).wait_recv()
+                total = total + self.land(way, z)[...].astype(jnp.float32)
+        return total
+
+    def row_copy(self, wire, spot, way, block, hop):
+        where = spot.right if way == 0 else spot.left
+        at = self.at + 2 * self.n + way * (self.n - 1) + hop
+        return wire.copy(self.rows(block), self.rows(block), where, at)
+
+    def begin_rows(self, wire, spot, z):
+        for way in (0, 1):
+            if z < self.n - 1 if way == 0 else z > 0:
+                wire.go(partial(self.row_copy, wire, spot, way, z, 0))
+
+    def pass_rows(self, wire, spot, way, block, hop, last):
+        self.row_copy(wire, spot, way, block, hop - 1).wait_recv()
+        if not last:
+            wire.go(partial(self.row_copy, wire, spot, way, block, hop))
+
+    def gathers(self, steps, wire, spot, z):
+        for block in range(self.n):
+            if block != z:
+                way = 0 if block < z else 1
+                hop = abs(block - z)
+                last = z == self.n - 1 if way == 0 else z == 0
+                steps.add(
+                    self.settle_time(block) + HOP * hop,
+                    partial(self.pass_rows, wire, spot, way, block, hop, last),
+                )
+
+
+class PlaneScatter:
+    def __init__(self, wire, spot, part, near, land, out, chunks):
+        self.wire, self.spot = wire, spot
+        self.part, self.near, self.land, self.out = part, near, land, out
+        self.rows = part.shape[1] // chunks
+        self.at = [wire.take(8) for _ in range(chunks)]
+        self.order = (XY, X, Y, (0, 0, 0))
+
+    def span(self, chunk, half=None):
+        if half is None:
+            return pl.ds(chunk * self.rows, self.rows)
+        size = self.rows // 2
+        return pl.ds(chunk * self.rows + half * size, size)
+
+    def place(self, k, same):
+        y, x, c = self.spot.other(self.order[k])
+        return y * 4 + x * 2 + (c if same else 1 - c)
+
+    def core(self, chunk, k):
+        r = self.span(chunk)
+        return self.wire.copy(
+            self.part.at[self.place(k, False), r], self.near.at[k, r], self.spot.device(C), self.at[chunk] + k
+        )
+
+    def corner(self, chunk, half):
+        r = self.span(chunk, half)
+        where = self.spot.device(Y if half else X)
+        return self.wire.copy(self.near.at[0, r], self.land.at[0, r], where, self.at[chunk] + 4 + half)
+
+    def side(self, chunk, k):
+        r = self.span(chunk)
+        where = self.spot.device(self.order[k])
+        return self.wire.copy(self.near.at[k, r], self.land.at[k, r], where, self.at[chunk] + 5 + k)
+
+    def both(self, chunk, k):
+        self.core(chunk, k).wait_recv()
+        r = self.span(chunk)
+        return self.part[self.place(k, True), r].astype(jnp.float32) + self.near[k, r].astype(jnp.float32)
+
+    def begin(self, chunk):
+        for k in range(4):
+            self.wire.go(partial(self.core, chunk, k))
+
+    def first(self, chunk):
+        self.near[0, self.span(chunk)] = self.both(chunk, 0).astype(jnp.bfloat16)
+        for half in (0, 1):
+            self.wire.go(partial(self.corner, chunk, half))
+
+    def second(self, chunk):
+        size = self.rows // 2
+        for k, half in ((1, 1), (2, 0)):
+            total = self.both(chunk, k)
+            self.corner(chunk, half).wait_recv()
+            more = self.land[0, self.span(chunk, half)].astype(jnp.float32)
+            mine = total[half * size : (half + 1) * size] + more
+            rest = total[(1 - half) * size : (2 - half) * size]
+            self.near[k, self.span(chunk, half)] = mine.astype(jnp.bfloat16)
+            self.near[k, self.span(chunk, 1 - half)] = rest.astype(jnp.bfloat16)
+            self.wire.go(partial(self.side, chunk, k))
+
+    def third(self, chunk):
+        total = self.both(chunk, 3)
+        for k in (1, 2):
+            self.side(chunk, k).wait_recv()
+            total = total + self.land[k, self.span(chunk)].astype(jnp.float32)
+        self.out[self.span(chunk)] = total
+
+    def timed(self, step, lag, start=0):
+        parts = []
+        for c in range(len(self.at)):
+            now = start + c * step
+            parts.append((self.begin, c, now - step))
+            for i, stage in enumerate((self.first, self.second, self.third)):
+                parts.append((stage, c, now + (i + 1) * lag))
+        return parts
+
+
+def sampler_gather_kernel(
+    n_mp, feat, key_value, pack, rq_part, slots, wout, latents,
+    feats_o, kv_o, pack_o, slots_o, rq_o, wout_o, latents_o,
+    rq_plane, rq_line, send, recv, here,
+):
+    spot = Spot(n_mp)
+    wire = Wire(send, recv)
+    f32, bf = jnp.float32, jnp.bfloat16
+    y, z, img, p = spot.y, spot.z, spot.img, spot.p
+    greet(spot.plane_others() + spot.line_others())
+    own = [
+        pltpu.make_async_copy(key_value.at[p], kv_o.at[y, z, img], here.at[0]),
+        pltpu.make_async_copy(pack, pack_o.at[p, z], here.at[1]),
+        pltpu.make_async_copy(slots, slots_o.at[z], here.at[2]),
+        pltpu.make_async_copy(feat, feats_o.at[p], here.at[3]),
+        pltpu.make_async_copy(wout, wout_o.at[z], here.at[4]),
+        pltpu.make_async_copy(latents, latents_o.at[z], here.at[5]),
+    ]
+    for copy in own:
+        copy.start()
+    others = [(spot.device(flip), spot.place(flip)) for flip in FLIPS]
+    at_kv, at_rq, at_pack = wire.take(7), wire.take(7), wire.take(7)
+    kv_move = lambda k: wire.copy(
+        key_value.at[others[k][1]], kv_o.at[y, z, img], others[k][0], at_kv + k
+    )
+    rq_move = lambda k: wire.copy(rq_part.at[others[k][1]], rq_plane.at[p], others[k][0], at_rq + k)
+    pack_move = lambda k: wire.copy(pack_o.at[p], pack_o.at[p], others[k][0], at_pack + k)
+    for k in range(7):
+        wire.go(partial(kv_move, k))
+    pack_line = LineGather(wire, spot, lambda j: pack_o.at[p, j])
+    slot_line = LineGather(wire, spot, lambda j: slots_o.at[j])
+    latent_line = LineGather(wire, spot, lambda j: latents_o.at[j])
+    kv_line = LineGather(wire, spot, lambda j: kv_o.at[:, j])
+    for copy in own:
+        copy.wait()
+    pack_line.stage(0)
+    slot_line.stage(0)
+    for k in range(7):
+        wire.go(partial(rq_move, k))
+    images = PlaneGather(wire, spot, chunked(feats_o, 1))
+    images.begin()
+    for k in range(7):
+        kv_move(k).wait_recv()
+    kv_line.stage(0)
+    wout_line = LineGather(wire, spot, lambda j: wout_o.at[j])
+    wout_line.stage(0)
+    latent_line.stage(0)
+    for hop in range(1, n_mp):
+        pack_line.stage(hop)
+        slot_line.stage(hop)
+        latent_line.stage(hop)
+    for k in range(7):
+        wire.go(partial(pack_move, k))
+    rq_plane[p] = rq_part[p]
+    for k in range(7):
+        rq_move(k).wait_recv()
+    total = rq_plane[0].astype(f32)
+    for q in range(1, 8):
+        total = total + rq_plane[q].astype(f32)
+    rq_line[z] = total.astype(bf)
+    line_at = wire.take(n_mp)
+    line_move = lambda d: wire.copy(rq_line.at[z], rq_line.at[z], {MP: lax.rem(z + d, n_mp)}, line_at + d)
+    for d in range(1, n_mp):
+        wire.go(partial(line_move, d))
+    kv_line.stage(1)
+    wout_line.stage(1)
+    images.middle()
+    kv_line.stage(2)
+    wout_line.stage(2)
+    images.end()
+    for hop in range(3, n_mp):
+        kv_line.stage(hop)
+        wout_line.stage(hop)
+    images.core()
+    for d in range(1, n_mp):
+        line_move(d).wait_recv()
+    total = rq_line[0].astype(f32)
+    for j in range(1, n_mp):
+        total = total + rq_line[j].astype(f32)
+    rq_o[...] = total.astype(bf)
+    for k in range(7):
+        pack_move(k).wait_recv()
+    wire.finish()
+
+
+def call_sampler_gather(n_mp, feat, key_value, pack, rq_part, slots, wout, latents):
+    shape = jax.ShapeDtypeStruct
+    rows_v, width_v = feat.shape[1:]
+    bf = jnp.bfloat16
+    outs = (
+        shape((8, rows_v, width_v), bf),
+        shape((2, n_mp, 4) + key_value.shape[1:], bf),
+        shape((8, n_mp) + pack.shape, bf),
+        shape((n_mp,) + slots.shape, jnp.int32),
+        shape(rq_part.shape[1:], bf),
+        shape((n_mp,) + wout.shape, bf),
+        shape((n_mp,) + latents.shape, bf),
+    )
+    wires = 7 * 3 + 8 + 5 * 2 * (n_mp - 1) + n_mp
+    anywhere = pl.BlockSpec(memory_space=pl.ANY)
+    near = pl.BlockSpec(memory_space=VMEM)
+    return pl.pallas_call(
+        partial(sampler_gather_kernel, n_mp),
+        name="sampler_gather",
+        out_shape=outs,
+        in_specs=[near] * 7,
+        out_specs=(anywhere,) * 4 + (near, anywhere, anywhere),
+        scratch_shapes=[
+            VMEM(rq_part.shape, bf),
+            VMEM((n_mp,) + rq_part.shape[1:], bf),
+            pltpu.SemaphoreType.DMA((wires,)),
+            pltpu.SemaphoreType.DMA((wires,)),
+            pltpu.SemaphoreType.DMA((6,)),
+        ],
+        compiler_params=pltpu.CompilerParams(collective_id=1, has_side_effects=True, vmem_limit_bytes=BIG),
+    )(feat[0], key_value, pack, rq_part, slots, wout, latents)
+
+
+def table_kernel(n_mp, part, table, near_c, half_x, half_y, full_x, full_y, sums, emb, send, recv, here):
+    spot = Spot(n_mp)
+    wire = Wire(send, recv)
+    y, z, img, c = spot.y, spot.z, spot.img, spot.c
+    greet([spot.device(X), spot.device(Y), spot.device(C), spot.left, spot.right])
+    order = (XY, X, Y, (0, 0, 0))
+    at_c = wire.take(4)
+
+    def core(k):
+        fy, fx, _ = spot.other(order[k])
+        return wire.copy(part.at[fy, fx, 1 - c], near_c.at[k], spot.device(C), at_c + k)
+
+    for k in range(4):
+        wire.go(partial(core, k))
+    f32 = jnp.float32
+    half = emb.shape[0] // 2
+
+    def gathered(k):
+        core(k).wait_recv()
+        fy, fx, _ = spot.other(order[k])
+        return part[fy, fx, c].astype(f32) + near_c[k].astype(f32)
+
+    at = wire.take(4)
+    low_half, high_half = pl.ds(0, half), pl.ds(half, half)
+    to_x_half = lambda: wire.copy(sums.at[0, low_half], half_x, spot.device(X), at)
+    to_y_half = lambda: wire.copy(sums.at[0, high_half], half_y, spot.device(Y), at + 1)
+    to_x = lambda: wire.copy(sums.at[1], full_x, spot.device(X), at + 2)
+    to_y = lambda: wire.copy(sums.at[2], full_y, spot.device(Y), at + 3)
+    sums[0] = gathered(0).astype(jnp.bfloat16)
+    wire.go(to_x_half)
+    wire.go(to_y_half)
+    total = gathered(1)
+    to_y_half().wait_recv()
+    sums[1, low_half] = total[:half].astype(jnp.bfloat16)
+    sums[1, high_half] = (total[half:] + half_y[...].astype(f32)).astype(jnp.bfloat16)
+    wire.go(to_x)
+    total = gathered(2)
+    to_x_half().wait_recv()
+    sums[2, low_half] = (total[:half] + half_x[...].astype(f32)).astype(jnp.bfloat16)
+    sums[2, high_half] = total[half:].astype(jnp.bfloat16)
+    wire.go(to_y)
+    total = gathered(3)
+    to_x().wait_recv()
+    total = total + full_x[...].astype(f32)
+    to_y().wait_recv()
+    emb[...] = (total + full_y[...].astype(f32)).astype(jnp.bfloat16)
+
+    place = pltpu.make_async_copy(emb, table.at[z, img], here.at[0])
+    place.start()
+    place.wait()
+    other_x = spot.x * 2 + c
+    line = LineGather(wire, spot, lambda j: table.at[j, img])
+    at_x, at_c1, at_c2 = wire.take(n_mp), wire.take(n_mp), wire.take(n_mp)
+    img_x, img_c = lax.rem(img + 2, 4), img + 1 - 2 * c
+    img_xc = lax.rem(img_c + 2, 4)
+    over = lambda j, which, to, base: wire.copy(
+        table.at[j, which], table.at[j, which], spot.device(to), base + j
+    )
+
+    def spread(j):
+        over(j, img, X, at_x).start()
+        over(j, img, C, at_c1).start()
+
+    line.stage(0)
+    spread(z)
+    for hop in range(1, n_mp):
+        line.stage(hop, spread)
+        if hop == 1:
+            pass
+    for j in range(n_mp):
+        over(j, img_x, X, at_x).wait_recv()
+        over(j, img_x, C, at_c2).start()
+    for j in range(n_mp):
+        over(j, img_c, C, at_c1).wait_recv()
+        over(j, img_xc, C, at_c2).wait_recv()
+    for j in range(n_mp):
+        over(j, img, X, at_x).wait_send()
+        over(j, img, C, at_c1).wait_send()
+        over(j, img_x, C, at_c2).wait_send()
+    wire.finish()
+
+
+def call_table(n_mp, part):
+    rows, width = part.shape[1:]
+    wires = 8 + 2 * (n_mp - 1) + 3 * n_mp
+    near = pl.BlockSpec(memory_space=VMEM)
+    bf = jnp.bfloat16
+    return pl.pallas_call(
+        partial(table_kernel, n_mp),
+        name="table",
+        out_shape=jax.ShapeDtypeStruct((n_mp, 4, rows, width), bf),
+        in_specs=[near],
+        out_specs=pl.BlockSpec(memory_space=pl.ANY),
+        scratch_shapes=[
+            VMEM((4, rows, width), bf),
+            VMEM((rows // 2, width), bf),
+            VMEM((rows // 2, width), bf),
+            VMEM((rows, width), bf),
+            VMEM((rows, width), bf),
+            VMEM((3, rows, width), bf),
+            VMEM((rows, width), bf),
+            pltpu.SemaphoreType.DMA((wires,)),
+            pltpu.SemaphoreType.DMA((wires,)),
+            pltpu.SemaphoreType.DMA((1,)),
+        ],
+        compiler_params=pltpu.CompilerParams(collective_id=2, has_side_effects=True, vmem_limit_bytes=BIG),
+    )(part.reshape(2, 2, 2, rows, width))
+
+
+def slot_kernel(n_mp, part, out, near_c, near_x, sum_x, sum_o, land, hold, total, send, recv):
+    spot = Spot(n_mp)
+    wire = Wire(send, recv)
+    img, c, x = spot.img, spot.c, spot.x
+    f32, bf = jnp.float32, jnp.bfloat16
+    greet([spot.device(X), spot.device(Y), spot.device(C), spot.left, spot.right])
+    at_c, at_x = wire.take(2 * n_mp), wire.take(n_mp)
+    img_x = lax.rem(img + 2, 4)
+    far = (1 - x) * 2 + 1 - c
+    beside = x * 2 + 1 - c
+    core_x = lambda j: wire.copy(part.at[j, far], near_c.at[0, j], spot.device(C), at_c + j)
+    core_o = lambda j: wire.copy(part.at[j, beside], near_c.at[1, j], spot.device(C), at_c + n_mp + j)
+    to_x = lambda j: wire.copy(sum_x.at[j], near_x.at[j], spot.device(X), at_x + j)
+    ends = [j for pair in zip(range(n_mp - 1, -1, -1), range(n_mp)) for j in pair][:n_mp]
+    line = LineScatter(
+        wire, spot, lambda j: sum_o.at[j], lambda way, j: land.at[way, j], lambda way, j: hold.at[way, j]
+    )
+    for j in ends:
+        wire.go(partial(core_x, j))
+    for j in ends:
+        wire.go(partial(core_o, j))
+    for j in ends:
+        core_x(j).wait_recv()
+        sum_x[j] = (part[j, img_x].astype(f32) + near_c[0, j].astype(f32)).astype(bf)
+        wire.go(partial(to_x, j))
+
+    def gathered(j):
+        core_o(j).wait_recv()
+        to_x(j).wait_recv()
+        sum_o[j] = (
+            part[j, img].astype(f32) + near_c[1, j].astype(f32) + near_x[j].astype(f32)
+        ).astype(bf)
+
+    line.relay(gathered)
+    line.own(total)
+    out[spot.p] = total[...].astype(bf)
+    spread = PlaneGather(wire, spot, chunked(out, 1))
+    spread.begin()
+    spread.middle()
+    spread.end()
+    spread.core()
+    wire.finish()
+
+
+def call_slot(n_mp, part):
+    rows, width = part.shape[2:]
+    wires = 3 * n_mp + 2 * n_mp + 8
+    bf = jnp.bfloat16
+    near = pl.BlockSpec(memory_space=VMEM)
+    return pl.pallas_call(
+        partial(slot_kernel, n_mp),
+        name="slot_grads",
+        out_shape=jax.ShapeDtypeStruct((8, rows, width), bf),
+        in_specs=[near],
+        out_specs=near,
+        scratch_shapes=[
+            VMEM((2, n_mp, rows, width), bf),
+            VMEM((n_mp, rows, width), bf),
+            VMEM((n_mp, rows, width), bf),
+            VMEM((n_mp, rows, width), bf),
+            VMEM((2, n_mp, rows, width), bf),
+            VMEM((2, n_mp, rows, width), bf),
+            VMEM((rows, width), jnp.float32),
+            pltpu.SemaphoreType.DMA((wires,)),
+            pltpu.SemaphoreType.DMA((wires,)),
+        ],
+        compiler_params=pltpu.CompilerParams(collective_id=3, has_side_effects=True, vmem_limit_bytes=BIG),
+    )(part)
+
+
+def sampler_scatter_kernel(
+    n_mp, dkv, dwout, side_1, side_2, drq, resid, gains, local_gains,
+    dkv_o, dwout_o, sum_1, sum_2, drq_o, resid_o, gains_o,
+    kv_land, kv_low, w_land, rq_line, resid_line, gain_line, gain_plane, gain_low,
+    near_1, land_1, near_2, land_2, send, recv,
+):
+    spot = Spot(n_mp)
+    y, z, img, p = spot.y, spot.z, spot.img, spot.p
+    f32, bf = jnp.float32, jnp.bfloat16
+    greet(spot.plane_others() + spot.line_others())
+    rq_line[z] = drq[...]
+    resid_line[z] = resid[z]
+    gain_line[z] = gains[z]
+    others = [(spot.device(flip), spot.place(flip)) for flip in FLIPS]
+    per_line = 2 * n_mp
+    half_rows = dwout.shape[1] // 2
+
+    def run(k):
+        wire = Wire(send, recv)
+        wire.take(4 * per_line)
+        at, at_plane = wire.take(3 * n_mp), wire.take(21)
+        small = []
+        for d in range(1, n_mp):
+            there = (k + d) % n_mp
+            where = {MP: there}
+            moves = (
+                lambda d=d, where=where: wire.copy(rq_line.at[k], rq_line.at[k], where, at + d),
+                lambda d=d, where=where, there=there: wire.copy(
+                    resid.at[there], resid_line.at[k], where, at + n_mp + d
+                ),
+                lambda d=d, where=where, there=there: wire.copy(
+                    gains.at[there], gain_line.at[k], where, at + 2 * n_mp + d
+                ),
+            )
+            for move in moves:
+                wire.go(move)
+            small += moves
+        steps = Steps()
+        lines = [
+            Line(
+                n_mp, n_mp - 1, h, h * per_line,
+                lambda j, h=h: dkv.at[h, j], lambda way, j, h=h: kv_land.at[way, h, j], None,
+            )
+            for h in range(2)
+        ] + [
+            Line(
+                n_mp, n_mp - 1, 2 + h, (2 + h) * per_line,
+                lambda j, h=h: dwout.at[j, pl.ds(h * half_rows, half_rows)],
+                lambda way, j, h=h: w_land.at[way, j, pl.ds(h * half_rows, half_rows)],
+                None,
+            )
+            for h in range(2)
+        ]
+        for line in lines:
+            line.sums(steps, wire, spot, k)
+        sent = [
+            (
+                lambda i=i, there=there, q=q: wire.copy(drq_o.at[p], drq_o.at[p], there, at_plane + i),
+                lambda i=i, there=there, q=q: wire.copy(gain_low.at[q], gain_plane.at[p], there, at_plane + 7 + i),
+                lambda i=i, there=there, q=q: wire.copy(kv_low.at[q], dkv_o.at[p], there, at_plane + 14 + i),
+            )
+            for i, (there, q) in enumerate(others)
+        ]
+
+        def add_small():
+            for move in small:
+                move().wait_recv()
+            total, rest, gain = rq_line[0], resid_line[0], gain_line[0]
+            for j in range(1, n_mp):
+                total, rest, gain = total + rq_line[j], rest + resid_line[j], gain + gain_line[j]
+            resid_o[...] = rest
+            drq_o[p] = total
+            gain_low[...] = gain + local_gains[...]
+            gain_plane[p] = gain_low[p]
+            for moves in sent:
+                wire.go(moves[0])
+                wire.go(moves[1])
+
+        def own_kv():
+            for h in range(2):
+                total = lines[h].own(wire, spot, k).astype(bf)
+                kv_low[pl.ds(4 * h, 4)] = total
+            dkv_o[p] = kv_low[p]
+            for moves in sent:
+                wire.go(moves[2])
+
+        def own_w(h):
+            dwout_o[pl.ds(h * half_rows, half_rows)] = lines[2 + h].own(wire, spot, k)
+
+        steps.add(4.5, add_small)
+        steps.add(lines[1].settle_time(k), own_kv)
+        for h in range(2):
+            steps.add(lines[2 + h].settle_time(k), partial(own_w, h))
+        first = PlaneScatter(wire, spot, side_1, near_1, land_1, sum_1, SIDE)
+        second = PlaneScatter(wire, spot, side_2, near_2, land_2, sum_2, 2)
+        for step, c, time in first.timed(2.5, 2.5, 1) + second.timed(1.5, 2, 12):
+            steps.add(time + 0.25, partial(step, c))
+        steps.run()
+        for moves in sent:
+            for move in moves:
+                move().wait_recv()
+        wire.finish()
+
+    for k in range(n_mp):
+        pl.when(z == k)(partial(run, k))
+    gain = gain_plane[0]
+    for q in range(1, 8):
+        gain = gain + gain_plane[q]
+    gains_o[...] = gain
+
+
+def call_sampler_scatter(n_mp, dkv, dwout, sides, drq, resid, gains, local_gains):
+    shape = jax.ShapeDtypeStruct
+    f32, bf = jnp.float32, jnp.bfloat16
+    rows, cols = dkv.shape[3:]
+    wires = 3 * n_mp + 8 * n_mp + 21 + 8 * (SIDE + 2)
+    near = pl.BlockSpec(memory_space=VMEM)
+    return pl.pallas_call(
+        partial(sampler_scatter_kernel, n_mp),
+        name="sampler_scatter",
+        out_shape=(
+            shape((8, rows, cols), bf),
+            shape(dwout.shape[1:], f32),
+            shape(sides[0].shape[1:], f32),
+            shape(sides[1].shape[1:], f32),
+            shape((8,) + drq.shape, f32),
+            shape(resid.shape[1:], f32),
+            shape(gains.shape[2:], f32),
+        ),
+        in_specs=[near] * 8,
+        out_specs=(near,) * 7,
+        scratch_shapes=[
+            VMEM((2, 2, n_mp, 4, rows, cols), bf),
+            VMEM((8, rows, cols), bf),
+            VMEM((2,) + dwout.shape, bf),
+            VMEM((n_mp,) + drq.shape, f32),
+            VMEM(resid.shape, f32),
+            VMEM(gains.shape, f32),
+            VMEM(gains.shape[1:], f32),
+            VMEM(gains.shape[1:], f32),
+        ]
+        + [VMEM((k,) + side.shape[1:], bf) for side in sides for k in (4, 3)]
+        + [
+            pltpu.SemaphoreType.DMA((wires,)),
+            pltpu.SemaphoreType.DMA((wires,)),
+        ],
+        compiler_params=pltpu.CompilerParams(collective_id=4, has_side_effects=True, vmem_limit_bytes=BIG),
+    )(dkv, dwout, *sides, drq, resid, gains, local_gains)
+
+
+def line_sum_kernel(n_mp, own, out, line, send, recv):
+    z = lax.axis_index(MP)
+    wire = Wire(send, recv)
+    greet([{MP: lax.rem(z + d, n_mp)} for d in range(1, n_mp)])
+    line[z] = own[...]
+    at = wire.take(n_mp)
+    make = lambda d: wire.copy(own, line.at[z], {MP: lax.rem(z + d, n_mp)}, at + d)
+    for d in range(1, n_mp):
+        wire.go(partial(make, d))
+    for d in range(1, n_mp):
+        make(d).wait_recv()
+    total = line[0]
+    for j in range(1, n_mp):
+        total = total + line[j]
+    out[...] = total
+    wire.finish()
+
+
+def line_sum(n_mp, number, own):
+    near = pl.BlockSpec(memory_space=VMEM)
+    return pl.pallas_call(
+        partial(line_sum_kernel, n_mp),
+        name=f"line_sum_{number}",
+        out_shape=jax.ShapeDtypeStruct(own.shape, jnp.float32),
+        in_specs=[near],
+        out_specs=near,
+        scratch_shapes=[
+            VMEM((n_mp,) + own.shape, jnp.float32),
+            pltpu.SemaphoreType.DMA((n_mp,)),
+            pltpu.SemaphoreType.DMA((n_mp,)),
+        ],
+        compiler_params=pltpu.CompilerParams(collective_id=number, has_side_effects=True),
+    )(own)
+
+
+def norm_parts(field):
+    average = jnp.mean(field, -1, keepdims=True)
+    centred = field - average
+    factor = lax.rsqrt(jnp.mean(centred * centred, -1, keepdims=True) + EPS)
+    return centred * factor, factor
+
+
+def norm_back(gradient, normed, factor, gain):
+    scaled = gradient * gain
+    return factor * (
+        scaled
+        - jnp.mean(scaled, -1, keepdims=True)
+        - normed * jnp.mean(scaled * normed, -1, keepdims=True)
+    )
+
+
+CHUNK = 16
+HOP = 2
+SIDE = 4
+SIDE_STEP = 6
+
+
+def rows_kernel(n_mp, kind, *refs):
+    f32, bf = jnp.float32, jnp.bfloat16
+    if kind == "forward":
+        part, side_in, entry, gain, stats, after, rows_out, stats_out, side_out, land, send, recv, here, stats_line = refs
+    elif kind == "middle":
+        part, side, after, grad, gain, entry, turned, after_grad, gain_grad, rows_out, sums_out, side_sum, land, send, recv, sums, *room = refs
+    else:
+        part, side, entry, after_grad, gain, text, low, tokens_grad, gain_grad, side_sum, land, send, recv, *room = refs
+    spot = Spot(n_mp)
+    z = spot.z
+    greet(spot.line_others() + [spot.device(X), spot.device(Y), spot.device(C)])
+    if kind == "forward":
+        stats_line[z] = stats[...]
+        place = pltpu.make_async_copy(side_in, side_out.at[spot.p], here.at[0])
+        place.start()
+        place.wait()
+    else:
+        gain_grad[...] = jnp.zeros_like(gain_grad)
+    batch, _, block, _ = part.shape
+    pieces = block // CHUNK
+    spans = [(s, pl.ds(i * CHUNK, CHUNK)) for s in range(batch) for i in range(pieces)]
+    per_chunk = 2 * n_mp + 2 * (n_mp - 1)
+
+    def settle(line, wire, k, s, r):
+        value = line.own(wire, spot, k)
+        if kind == "forward":
+            at = s * block + r.start
+            rows = jnp.transpose(stats_out[:, k * LANE : (k + 1) * LANE])[at : at + CHUNK] / value.shape[-1]
+            average, square = rows[:, 0:1], rows[:, 1:2]
+            value = (value - average * stats_out[0:1, n_mp * LANE :]) * lax.rsqrt(square - average * average + EPS)
+            value = value + entry[s, r].astype(f32)
+            after[s, r] = value
+            normed, _ = norm_parts(value)
+            rows_out[s, k, r] = (normed * gain[...]).astype(bf)
+        elif kind == "middle":
+            normed, factor = norm_parts(after[s, r])
+            gain_grad[...] += jnp.sum(value * normed, 0, keepdims=True)
+            value = norm_back(value, normed, factor, gain[...]) + grad[s, r].astype(f32)
+            after_grad[s, r] = value
+            rows_out[s, k, r] = value.astype(bf)
+            value = value.astype(bf).astype(f32)
+            first = jnp.sum(value * turned[...], -1, keepdims=True)
+            branch = after[s, r] - entry[s, r].astype(f32)
+            second = jnp.sum(value * branch, -1, keepdims=True)
+            lane = lax.broadcasted_iota(jnp.int32, (CHUNK, LANE), 1)
+            sums[pl.ds(s * block + r.start, CHUNK)] = jnp.where(lane == 0, first, jnp.where(lane == 1, second, 0.0))
+        else:
+            normed, factor = norm_parts(entry[s, r].astype(f32))
+            gain_grad[...] += jnp.sum(value * normed, 0, keepdims=True)
+            value = norm_back(value, normed, factor, gain[...]) + after_grad[s, r]
+            low[s, r] = value.astype(bf)
+            tokens_grad[s, r] = jnp.where(text[s, r][:, :1] > 0, value, 0.0).astype(bf)
+        if kind != "last":
+            line.begin_rows(wire, spot, k)
+
+    def run(k):
+        wire = Wire(send, recv)
+        wire.take(len(spans) * per_chunk)
+        around = wire.take(n_mp)
+        steps = Steps()
+        if kind == "forward":
+            stats_move = lambda d: wire.copy(
+                stats, stats_line.at[k], {MP: (k + d) % n_mp}, around + d
+            )
+            for d in range(1, n_mp):
+                wire.go(partial(stats_move, d))
+
+            def add_stats():
+                for d in range(1, n_mp):
+                    stats_move(d).wait_recv()
+                total = stats_line[0]
+                for j in range(1, n_mp):
+                    total = total + stats_line[j]
+                stats_out[...] = total
+
+            steps.add(4.2, add_stats)
+        if kind == "middle":
+            sums_move = lambda d: wire.copy(
+                sums_out.at[k], sums_out.at[k], {MP: (k + d) % n_mp}, around + d
+            )
+
+            def send_sums():
+                sums_out[k] = jnp.transpose(sums[...])[:8]
+                for d in range(1, n_mp):
+                    wire.go(partial(sums_move, d))
+
+        if kind == "forward":
+            plane = PlaneGather(wire, spot, chunked(side_out, SIDE), SIDE)
+            parts = [(plane.begin, 0), (plane.middle, 5), (plane.end, 9), (plane.core, 12)]
+            parts = [(step, c, late + c * SIDE_STEP) for step, late in parts for c in range(SIDE)]
+        else:
+            plane = PlaneScatter(wire, spot, side, *room, side_sum, SIDE)
+            parts = plane.timed(SIDE_STEP, 4)
+        for step, c, time in parts:
+            steps.add(time + 0.5, partial(step, c))
+        for c, (s, r) in enumerate(spans):
+            line = Line(
+                n_mp,
+                n_mp - 1 if kind == "last" else n_mp,
+                c,
+                c * per_chunk,
+                lambda j, s=s, r=r: part.at[s, j, r],
+                lambda way, j, s=s, r=r: land.at[way, j, s, r],
+                None if kind == "last" else lambda j, s=s, r=r: rows_out.at[s, j, r],
+            )
+            line.sums(steps, wire, spot, k)
+            steps.add(line.settle_time(k), partial(settle, line, wire, k, s, r))
+            if kind != "last":
+                line.gathers(steps, wire, spot, k)
+        if kind == "middle":
+            steps.add(line.settle_time(k), send_sums)
+        steps.run()
+        if kind == "middle":
+            for d in range(1, n_mp):
+                sums_move(d).wait_recv()
+        wire.finish()
+
+    for k in range(n_mp):
+        pl.when(z == k)(partial(run, k))
+
+
+def call_rows(n_mp, kind, number, outs, part, side, *args):
+    batch, _, block, width = part.shape
+    chunks = batch * block // CHUNK
+    wires = chunks * (2 * n_mp + 2 * (n_mp - 1)) + 8 * SIDE + n_mp
+    near = pl.BlockSpec(memory_space=VMEM)
+    bf = jnp.bfloat16
+    args = (part, side, *args)
+    out_specs = [near] * len(outs)
+    if kind == "forward":
+        out_specs[-1] = pl.BlockSpec(memory_space=pl.ANY)
+        more = [pltpu.SemaphoreType.DMA((1,)), VMEM((n_mp,) + args[-1].shape, jnp.float32)]
+    else:
+        more = [VMEM((k,) + side.shape[1:], bf) for k in (4, 3)]
+        if kind == "middle":
+            more = [VMEM((batch * block, LANE), jnp.float32)] + more
+    return pl.pallas_call(
+        partial(rows_kernel, n_mp, kind),
+        name=f"rows_{kind}",
+        out_shape=outs,
+        in_specs=[near] * len(args),
+        out_specs=tuple(out_specs),
+        scratch_shapes=[
+            VMEM((2, n_mp, batch, block, width), bf),
+            pltpu.SemaphoreType.DMA((wires,)),
+            pltpu.SemaphoreType.DMA((wires,)),
+        ]
+        + more,
+        compiler_params=pltpu.CompilerParams(collective_id=number, has_side_effects=True, vmem_limit_bytes=BIG),
+    )(*args)
+
+
+def swap_halves(field, lane):
+    width = field.shape[-1]
+    return jnp.where(
+        lane % HD < HD // 2,
+        pltpu.roll(field, width - HD // 2, 1),
+        pltpu.roll(field, HD // 2, 1),
+    )
+
+
+def head_probs(query, key, factor):
+    scores = lax.dot_general(query, key, (((1,), (1,)), ((), ())), preferred_element_type=jnp.float32) * factor
+    row_ids = lax.broadcasted_iota(jnp.int32, scores.shape, 0)
+    col_ids = lax.broadcasted_iota(jnp.int32, scores.shape, 1)
+    scores = jnp.where(col_ids <= row_ids, scores, -1e30)
+    exponent = jnp.exp(scores - jnp.max(scores, -1, keepdims=True))
+    return exponent / jnp.sum(exponent, -1, keepdims=True)
+
+
+def attention_kernel(proj, tables, low, attended):
+    f32, bf = jnp.float32, jnp.bfloat16
+    width = attended.shape[-1]
+    lane = lax.broadcasted_iota(jnp.int32, (proj.shape[0], LANE), 1)
+    low[:, 2 * width :] = proj[:, 2 * width :].astype(bf)
+    for at in range(0, width, LANE):
+        query, key = (
+            proj[:, start : start + LANE] * tables[c]
+            + swap_halves(proj[:, start : start + LANE], lane) * tables[c + 1]
+            for start, c in ((at, 0), (width + at, 2))
+        )
+        low[:, at : at + LANE] = query.astype(bf)
+        key = key.astype(bf)
+        low[:, width + at : width + at + LANE] = key
+        value = low[:, 2 * width + at : 2 * width + at + LANE]
+        both = None
+        for side in range(LANE // HD):
+            mine = lane // HD == side
+            probs = head_probs(jnp.where(mine, query, 0.0).astype(bf), key, HD ** (-0.5))
+            out = jnp.dot(probs.astype(bf), value, preferred_element_type=f32)
+            both = out if both is None else jnp.where(mine, out, both)
+        attended[:, at : at + LANE] = both
+
+
+def call_attention(batch, proj, tables):
+    rows = proj.shape[0] // batch
+    width = proj.shape[1] // 3
+    shape = jax.ShapeDtypeStruct
+    return pl.pallas_call(
+        attention_kernel,
+        name="attention",
+        grid=(batch,),
+        out_shape=(shape(proj.shape, jnp.bfloat16), shape((proj.shape[0], width), jnp.float32)),
+        in_specs=[
+            pl.BlockSpec((rows, 3 * width), lambda s: (s, 0)),
+            pl.BlockSpec(tables.shape, lambda s: (0, 0, 0)),
+        ],
+        out_specs=(
+            pl.BlockSpec((rows, 3 * width), lambda s: (s, 0)),
+            pl.BlockSpec((rows, width), lambda s: (s, 0)),
+        ),
+        compiler_params=pltpu.CompilerParams(vmem_limit_bytes=BIG),
+    )(proj, tables)
+
+
+def attention_back_kernel(low, grad, tables, out):
+    f32, bf = jnp.float32, jnp.bfloat16
+    width = grad.shape[-1]
+    factor = HD ** (-0.5)
+    rows_in = (((0,), (0,)), ((), ()))
+    lane = lax.broadcasted_iota(jnp.int32, (low.shape[0], LANE), 1)
+    for at in range(0, width, LANE):
+        query = low[:, at : at + LANE]
+        key = low[:, width + at : width + at + LANE]
+        value = low[:, 2 * width + at : 2 * width + at + LANE]
+        above = grad[:, at : at + LANE]
+        d_query = d_key = d_value = None
+        for side in range(LANE // HD):
+            mine = lane // HD == side
+            probs = head_probs(jnp.where(mine, query.astype(f32), 0.0).astype(bf), key, factor)
+            d_probs = lax.dot_general(
+                jnp.where(mine, above.astype(f32), 0.0).astype(bf),
+                value,
+                (((1,), (1,)), ((), ())),
+                preferred_element_type=f32,
+            )
+            dv = lax.dot_general(probs.astype(bf), above, rows_in, preferred_element_type=f32)
+            d_scores = (probs * (d_probs - jnp.sum(probs * d_probs, -1, keepdims=True))).astype(bf)
+            dq = jnp.dot(d_scores, key, preferred_element_type=f32) * factor
+            dk = lax.dot_general(d_scores, query, rows_in, preferred_element_type=f32) * factor
+            d_query = dq if side == 0 else jnp.where(mine, dq, d_query)
+            d_key = dk if side == 0 else jnp.where(mine, dk, d_key)
+            d_value = dv if side == 0 else jnp.where(mine, dv, d_value)
+        out[:, 2 * width + at : 2 * width + at + LANE] = d_value.astype(bf)
+        for field, start, c in ((d_query, at, 0), (d_key, width + at, 2)):
+            out[:, start : start + LANE] = (
+                field * tables[c] + swap_halves(field * tables[c + 1], lane)
+            ).astype(bf)
+
+
+def call_attention_back(batch, low, grad, tables):
+    rows = low.shape[0] // batch
+    width = low.shape[1] // 3
+    return pl.pallas_call(
+        attention_back_kernel,
+        name="attention_back",
+        grid=(batch,),
+        out_shape=jax.ShapeDtypeStruct(low.shape, jnp.bfloat16),
+        in_specs=[
+            pl.BlockSpec((rows, 3 * width), lambda s: (s, 0)),
+            pl.BlockSpec((rows, width), lambda s: (s, 0)),
+            pl.BlockSpec(tables.shape, lambda s: (0, 0, 0)),
+        ],
+        out_specs=pl.BlockSpec((rows, 3 * width), lambda s: (s, 0)),
+        compiler_params=pltpu.CompilerParams(vmem_limit_bytes=BIG),
+    )(low, grad, tables)
+
+
+def pool_probs_of(query, key, factor):
+    scores = lax.dot_general(query, key, (((1,), (1,)), ((), ())), preferred_element_type=jnp.float32) * factor
+    exponent = jnp.exp(scores - jnp.max(scores, -1, keepdims=True))
+    return exponent / jnp.sum(exponent, -1, keepdims=True)
+
+
+def pool_kernel(feats, gain, weights, query, wout, more, vision_low, keys_values, pooled, branch):
+    f32, bf = jnp.float32, jnp.bfloat16
+    cols = query.shape[-1]
+    normed, _ = norm_parts(feats[0].astype(f32))
+    vision_low[0] = (normed * gain[...]).astype(bf)
+    keys_values[0] = jnp.dot(vision_low[0], weights[...], preferred_element_type=f32).astype(bf)
+    lane = lax.broadcasted_iota(jnp.int32, (query.shape[0], LANE), 1)
+    for at in range(0, cols, LANE):
+        both = None
+        for side in range(LANE // HD):
+            mine = lane // HD == side
+            asked = jnp.where(mine, query[:, at : at + LANE].astype(f32), 0.0).astype(bf)
+            probs = pool_probs_of(asked, keys_values[0, :, at : at + LANE], HD ** (-0.5))
+            out = jnp.dot(
+                probs.astype(bf), keys_values[0, :, cols + at : cols + at + LANE], preferred_element_type=f32
+            )
+            both = out if both is None else jnp.where(mine, out, both)
+        pooled[0, :, at : at + LANE] = both.astype(bf)
+    branch[0] = (jnp.dot(pooled[0], wout[...], preferred_element_type=f32) + more[...]).astype(bf)
+
+
+def call_pool(feats, gain, weights, query, wout, more):
+    images, patches, channels = feats.shape
+    width = wout.shape[1]
+    shape, bf = jax.ShapeDtypeStruct, jnp.bfloat16
+    whole = lambda array: pl.BlockSpec(array.shape, lambda i: (0,) * array.ndim)
+    outs = (
+        shape((images, patches, channels), bf),
+        shape((images, patches, weights.shape[1]), bf),
+        shape((images,) + query.shape, bf),
+        shape((images, query.shape[0], width), bf),
+    )
+    one = lambda array: pl.BlockSpec((1,) + array.shape[1:], lambda i: (i, 0, 0))
+    return pl.pallas_call(
+        pool_kernel,
+        name="pool",
+        grid=(images,),
+        out_shape=outs,
+        in_specs=[one(feats), whole(gain), whole(weights), whole(query), whole(wout), whole(more)],
+        out_specs=tuple(one(out) for out in outs),
+        compiler_params=pltpu.CompilerParams(vmem_limit_bytes=BIG),
+    )(feats, gain, weights, query, wout, more)
+
+
+def pool_back_kernel(
+    slot, wout, vision_low, keys_values, query, weights, pooled,
+    d_weights, d_products, d_query, residual, d_wout, total, d_kv, w_total,
+):
+    f32, bf = jnp.float32, jnp.bfloat16
+    i = pl.program_id(0)
+    cols = query.shape[-1]
+    factor = HD ** (-0.5)
+    rows_in = (((0,), (0,)), ((), ()))
+    lanes_in = (((1,), (1,)), ((), ()))
+
+    @pl.when(i == 0)
+    def _():
+        total[...] = jnp.zeros_like(total)
+        w_total[...] = jnp.zeros_like(w_total)
+        d_query[...] = jnp.zeros_like(d_query)
+        residual[...] = jnp.zeros_like(residual)
+
+    above = slot[0]
+    residual[...] += above.astype(f32)
+    w_total[...] += lax.dot_general(pooled[0], above, rows_in, preferred_element_type=f32)
+    d_pooled = lax.dot_general(above, wout[...], lanes_in, preferred_element_type=f32).astype(bf)
+    lane = lax.broadcasted_iota(jnp.int32, (query.shape[0], LANE), 1)
+    patch_lane = lax.broadcasted_iota(jnp.int32, (keys_values.shape[1], LANE), 1)
+    for at in range(0, cols, LANE):
+        key = keys_values[0, :, at : at + LANE]
+        value = keys_values[0, :, cols + at : cols + at + LANE]
+        asked = query[:, at : at + LANE]
+        here = d_pooled[:, at : at + LANE]
+        dq = dk = dv = None
+        for side in range(LANE // HD):
+            mine, patch_mine = lane // HD == side, patch_lane // HD == side
+            probs = pool_probs_of(jnp.where(mine, asked.astype(f32), 0.0).astype(bf), key, factor)
+            d_probs = lax.dot_general(
+                jnp.where(mine, here.astype(f32), 0.0).astype(bf), value, lanes_in, preferred_element_type=f32
+            )
+            v = lax.dot_general(probs.astype(bf), here, rows_in, preferred_element_type=f32)
+            d_scores = (probs * (d_probs - jnp.sum(probs * d_probs, -1, keepdims=True))).astype(bf)
+            q = jnp.dot(d_scores, key, preferred_element_type=f32) * factor
+            k = lax.dot_general(d_scores, asked, rows_in, preferred_element_type=f32) * factor
+            dq = q if side == 0 else jnp.where(mine, q, dq)
+            dk = k if side == 0 else jnp.where(patch_mine, k, dk)
+            dv = v if side == 0 else jnp.where(patch_mine, v, dv)
+        d_query[:, at : at + LANE] += dq.astype(bf).astype(f32)
+        d_kv[:, at : at + LANE] = dk.astype(bf)
+        d_kv[:, cols + at : cols + at + LANE] = dv.astype(bf)
+    total[...] += lax.dot_general(vision_low[0], d_kv[...], rows_in, preferred_element_type=f32)
+
+    @pl.when(i == pl.num_programs(0) - 1)
+    def _():
+        value = total[...]
+        d_weights[...] = value.astype(bf)
+        products = jnp.sum(value * weights[...].astype(f32), -1, keepdims=True)
+        d_products[...] = jnp.broadcast_to(products, d_products.shape)
+        d_wout[...] = w_total[...].astype(bf)
+
+
+def call_pool_back(slot, wout, vision_low, keys_values, query, weights, pooled):
+    images, rows, width = slot.shape
+    shape, f32, bf = jax.ShapeDtypeStruct, jnp.float32, jnp.bfloat16
+    whole = lambda array: pl.BlockSpec(array.shape, lambda i: (0,) * len(array.shape))
+    one = lambda array: pl.BlockSpec((1,) + array.shape[1:], lambda i: (i, 0, 0))
+    outs = (
+        shape(weights.shape, bf),
+        shape((weights.shape[0], LANE), f32),
+        shape(query.shape, f32),
+        shape((rows, width), f32),
+        shape(wout.shape, bf),
+    )
+    return pl.pallas_call(
+        pool_back_kernel,
+        name="pool_back",
+        grid=(images,),
+        out_shape=outs,
+        in_specs=[
+            one(slot), whole(wout), one(vision_low), one(keys_values), whole(query), whole(weights), one(pooled)
+        ],
+        out_specs=tuple(whole(out) for out in outs),
+        scratch_shapes=[
+            VMEM(weights.shape, f32),
+            VMEM((keys_values.shape[1], weights.shape[1]), bf),
+            VMEM(wout.shape, f32),
+        ],
+        compiler_params=pltpu.CompilerParams(vmem_limit_bytes=BIG),
+    )(slot, wout, vision_low, keys_values, query, weights, pooled)
+
+
+def entry_kernel(slot, table, tokens, gain, entry, normed_low):
+    f32 = jnp.float32
+    is_image = slot[pl.program_id(0)] >= 0
+    rows = jnp.where(is_image, table[0].astype(f32), tokens[0].astype(f32))
+    entry[0] = rows.astype(jnp.bfloat16)
+    normed, _ = norm_parts(rows)
+    normed_low[0] = (normed * gain[...]).astype(jnp.bfloat16)
+
+
+def call_entry(slot, table, tokens, gain):
+    blocks, rows, width = tokens.shape
+    one = pl.BlockSpec((1, rows, width), lambda i, slot: (i, 0, 0))
+    shape = jax.ShapeDtypeStruct(tokens.shape, jnp.bfloat16)
+    return pl.pallas_call(
+        entry_kernel,
+        name="entry",
+        grid_spec=pltpu.PrefetchScalarGridSpec(
+            num_scalar_prefetch=1,
+            grid=(blocks,),
+            in_specs=[
+                pl.BlockSpec((1, rows, width), lambda i, slot: (jnp.maximum(slot[i], 0), 0, 0)),
+                one,
+                pl.BlockSpec((1, width), lambda i, slot: (0, 0)),
+            ],
+            out_specs=(one, one),
+        ),
+        out_shape=(shape, shape),
+        compiler_params=pltpu.CompilerParams(vmem_limit_bytes=BIG),
+    )(slot, table, tokens, gain)
+
+
+def rotary_rows():
+    half = HD // 2
+    place = np.arange(SEQ, dtype=np.float64)[:, None]
+    pair = np.arange(half, dtype=np.float64)[None, :]
+    angle = place * 10000.0 ** (-pair / half)
+    growth = ((pair / half + 0.4) / 1.4) ** (place / 512.0)
+    cosine, sine = np.cos(angle), np.sin(angle)
+    plain = lambda field: np.tile(np.concatenate([field, field], -1), (1, LANE // HD))
+    signed = lambda field: np.tile(np.concatenate([-field, field], -1), (1, LANE // HD))
+    rows = [plain(cosine * growth), signed(sine * growth), plain(cosine / growth), signed(sine / growth)]
+    return jnp.asarray(np.stack(rows), jnp.float32)
+
+
+def as_rows(field):
+    return jnp.concatenate([field, jnp.zeros((8 - field.shape[0], field.shape[1]), field.dtype)], 0)
+
+
+def after_those(first, then):
+    return lax.optimization_barrier((first, then))[1]
+
+
+def plane_local(
+    n_mp,
+    tokens,
+    slot_index,
+    out_grad,
+    features,
+    query_weight,
+    key_weight,
+    value_weight,
+    output_weight,
+    up_weight,
+    down_weight,
+    norm_input,
+    norm_attention,
+    norm_middle,
+    norm_hidden,
+    sampler_query,
+    sampler_key,
+    sampler_value,
+    sampler_output,
+    latents,
+    norm_vision,
+):
+    f32, bf = jnp.float32, jnp.bfloat16
+    factor = HD ** (-0.5)
+    dot = partial(jnp.dot, preferred_element_type=f32)
+    batch, block, width = tokens.shape
+    y, z, img = lax.axis_index(DP), lax.axis_index(MP), lax.axis_index(IMG)
+    own_heads = sampler_output.shape[0] // HD
+    head_count = width // HD
+    by_place = lambda field: (
+        field.reshape(field.shape[0], 2, n_mp, 4, own_heads * HD)
+        .transpose(1, 3, 0, 2, 4)
+        .reshape(8, field.shape[0], -1)
+    )
+    key_value = jnp.concatenate([by_place(sampler_key), by_place(sampler_value)], -1)
+    rq_part = by_place(dot(latents, sampler_query).astype(bf))
+    flat_gains = jnp.concatenate(
+        [norm_vision, norm_input, norm_middle, norm_attention.reshape(-1), norm_hidden.reshape(-1)]
+    )
+    n_vision, n_row = norm_vision.shape[0], norm_input.shape[0]
+    n_att, n_hid = norm_attention.size, norm_hidden.size
+    gain_rows = 16
+    pack = jnp.pad(flat_gains, (0, gain_rows * LANE - flat_gains.shape[0])).reshape(gain_rows, LANE)
+    first_slots = jnp.zeros((8, LANE), jnp.int32).at[:batch, 0].set(slot_index[:, 0])
+    feats, kv_all, packs, slots, rq, wout_all, latents_line = call_sampler_gather(
+        n_mp,
+        features,
+        key_value,
+        pack,
+        rq_part,
+        first_slots,
+        sampler_output,
+        latents.reshape(-1, LANE),
+    )
+    over = (DP, IMG)
+    qkv_full = lax.all_gather(
+        jnp.concatenate([query_weight, key_weight, value_weight], 1), over, axis=0, tiled=True
+    )
+    tokens_all = lax.all_gather(tokens, MP, axis=0)
+    wo_full = lax.all_gather(output_weight, over, axis=1, tiled=True)
+    up_full = lax.all_gather(up_weight, over, axis=0, tiled=True)
+
+    own_cols = latents.shape[1]
+    column = lambda n, at: jnp.arange(n) == at
+    here = (column(2, y)[:, None, None] & column(4, img)[None, None, :])[None, ..., None]
+    placed = jnp.where(
+        here, latents_line.reshape(n_mp, LAT, own_cols).transpose(1, 0, 2)[:, None, :, None].astype(f32), 0.0
+    ).reshape(LAT, width)
+    gains_all = packs.reshape(2, 4, n_mp, -1).transpose(0, 2, 1, 3).astype(f32)
+    every = gains_all.reshape(8 * n_mp, -1)
+    vision_gain = every[:, :n_vision].reshape(1, -1)
+    input_gain = every[:, n_vision : n_vision + n_row].reshape(1, -1)
+    middle_gain = every[:, n_vision + n_row : n_vision + 2 * n_row].reshape(1, -1)
+    mine = lax.dynamic_index_in_dim(gains_all, z, 1, keepdims=False).reshape(8, -1)
+    at = n_vision + 2 * n_row
+    by_column = lambda field, rows: field.reshape(8, rows, -1).transpose(1, 0, 2).reshape(-1)
+    attention_gain = by_column(mine[:, at : at + n_att], norm_attention.shape[0])
+    hidden_gain = by_column(mine[:, at + n_att : at + n_att + n_hid], norm_hidden.shape[0])
+    slot_first = slots[:, :batch, 0]
+
+    images, patches = feats.shape[0], feats.shape[1]
+    heads = own_heads * n_mp
+    cols = heads * HD
+    kv_rows = kv_all.reshape(-1, 2 * cols)
+    wout_rows = wout_all.reshape(cols, width)
+    vision_low, keys_values, pooled, branch = call_pool(feats, vision_gain, kv_rows, rq, wout_rows, placed)
+    table = call_table(n_mp, branch).reshape(-1, LAT, width)
+
+    block_image = jnp.where(slot_first >= 0, slot_first // LAT, -1)
+    tokens_blocks = tokens_all.transpose(1, 0, 2, 3).reshape(batch * n_mp, block, width)
+    entry_all, normed_rows = call_entry(
+        block_image.T.reshape(-1).astype(jnp.int32), table, tokens_blocks, input_gain
+    )
+    entry = lax.dynamic_index_in_dim(entry_all.reshape(batch, n_mp, block, width), z, 1, keepdims=False)
+    normed_rows = normed_rows.reshape(-1, width)
+    rows = normed_rows.shape[0]
+    local_width = wo_full.shape[0]
+    tables = rotary_rows()
+    low, attended = call_attention(batch, dot(normed_rows, qkv_full), tables)
+    grads_all = lax.all_gather(after_those(attended, out_grad), MP, axis=0)
+    owner_first = lambda field: field.reshape(batch, n_mp, block).transpose(1, 0, 2).reshape(-1)
+    turned = jnp.sum(wo_full.astype(f32) * attention_gain[:, None], 0)
+    first = jnp.concatenate([owner_first(jnp.sum(attended, -1)), turned])
+    second = jnp.pad(owner_first(jnp.sum(attended * attended, -1)), (0, width))
+    stats = as_rows(jnp.stack([first, second]))
+    shape = jax.ShapeDtypeStruct
+    split_rows = (batch, n_mp, block, width)
+    own_shape = (batch, block, width)
+    hidden_width = up_full.shape[1]
+    side_shape = (8, width // 8, hidden_width)
+    after, middle_rows, stats, down_turned = call_rows(
+        n_mp,
+        "forward",
+        5,
+        (shape(own_shape, f32), shape(split_rows, bf), shape(stats.shape, f32), shape(side_shape, bf)),
+        dot((attended * attention_gain).astype(bf), wo_full).astype(bf).reshape(split_rows),
+        down_weight.T,
+        entry,
+        middle_gain,
+        stats,
+    )
+    sequence_first = lambda field: field.reshape(n_mp, batch, block).transpose(1, 0, 2).reshape(-1)[:, None]
+    turned = stats[:1, rows:]
+    average = sequence_first(stats[0, :rows]) / width
+    attn_factor = lax.rsqrt(sequence_first(stats[1, :rows]) / width - average * average + EPS)
+    attn_normed = (attended - average) * attn_factor
+    attn_low = (attn_normed * attention_gain).astype(bf)
+    middle_rows = middle_rows.reshape(rows, width)
+    down_turned = down_turned.reshape(width, hidden_width)
+    upward = dot(middle_rows, up_full)
+    activated, gelu_back = jax.vjp(exact_gelu, upward)
+    hidden_total = up_full.shape[1] * n_mp
+    grad_rows = grads_all.transpose(1, 0, 2, 3).reshape(rows, width)
+    d_hidden = dot(grad_rows, down_turned)
+    scaled = d_hidden * hidden_gain
+    row_sum = lambda field: jnp.sum(field, -1)
+    sums = line_sum(
+        n_mp,
+        8,
+        as_rows(
+            jnp.stack(
+                [row_sum(activated), row_sum(activated * activated), row_sum(scaled), row_sum(scaled * activated)]
+            )
+        ),
+    )
+    average, square, first, second = ((sums[i] / hidden_total)[:, None] for i in range(4))
+    hidden_factor = lax.rsqrt(square - average * average + EPS)
+    hidden_normed = (activated - average) * hidden_factor
+    hidden_low = (hidden_normed * hidden_gain).astype(bf)
+    result_part = dot(hidden_low, down_turned.T).astype(bf).reshape(split_rows)
+    d_hgain = jnp.sum(d_hidden * hidden_normed, 0)
+    second = (second - average * first) * hidden_factor
+    d_active = hidden_factor * (scaled - first - hidden_normed * second)
+    d_upward = gelu_back(d_active)[0].astype(bf)
+    d_down = dot(grad_rows.T, hidden_low).astype(bf)
+    d_up = dot(middle_rows.T, d_upward).astype(bf)
+    middle_part = dot(d_upward, up_full.T).astype(bf).reshape(split_rows)
+    middle_part, d_down, d_up = lax.optimization_barrier((middle_part, d_down, d_up))
+    side_own = shape(side_shape[1:], f32)
+    d_after, d_mgain, after_rows, sums, d_down_own = call_rows(
+        n_mp,
+        "middle",
+        6,
+        (
+            shape(own_shape, f32),
+            shape((1, width), f32),
+            shape(split_rows, bf),
+            shape((n_mp, 8, LANE), f32),
+            side_own,
+        ),
+        middle_part,
+        d_down.reshape(side_shape),
+        after,
+        out_grad,
+        middle_gain,
+        entry,
+        turned,
+    )
+    result_sum = lax.psum_scatter(
+        after_those(d_mgain, result_part), MP, scatter_dimension=1, tiled=False
+    )
+    result = after + result_sum.astype(f32)
+    after_rows = after_rows.reshape(rows, width)
+    d_mixed = dot(after_rows, wo_full.T)
+    scaled = d_mixed * attention_gain
+    d_again = jnp.sum(d_mixed * attn_normed, 0)
+    d_attended = attn_factor * (
+        scaled - sequence_first(sums[:, 0]) / width - attn_normed * sequence_first(sums[:, 1]) / width
+    )
+    d_qkv = call_attention_back(batch, low, d_attended.astype(bf), tables)
+    d_wo = dot(after_rows.T, attn_low).astype(bf).reshape(8, width // 8, local_width)
+    d_wqkv = dot(normed_rows.T, d_qkv).astype(bf).reshape(8, width // 8, 3 * local_width)
+    text = jnp.broadcast_to((slot_index < 0).astype(f32)[..., None], (batch, block, LANE))
+    entry_low, tokens_grad, d_igain, d_up_own = call_rows(
+        n_mp,
+        "last",
+        7,
+        (shape(own_shape, bf), shape(own_shape, bf), shape((1, width), f32), side_own),
+        dot(d_qkv, qkv_full.T).astype(bf).reshape(split_rows),
+        d_up.reshape(side_shape),
+        entry,
+        d_after,
+        input_gain,
+        text,
+    )
+
+    own_image = jnp.where(slot_index[:, 0] >= 0, slot_index[:, 0] // LAT, -1)
+    each = jnp.arange(4 * n_mp, dtype=jnp.int32)[:, None, None]
+    spread = jnp.zeros((4 * n_mp, block, width), bf)
+    for s in range(batch):
+        spread = jnp.where(each == own_image[s], entry_low[s][None], spread)
+    slot_low = call_slot(n_mp, spread.reshape(n_mp, 4, block, width))
+    d_kv_weight, d_products, d_rq, residual, d_wout = call_pool_back(
+        slot_low, wout_rows, vision_low, keys_values, rq, kv_rows, pooled
+    )
+    d_vgain = d_products[:, 0] / vision_gain[0]
+    gains_out = jnp.concatenate(
+        [d_vgain.reshape(8 * n_mp, -1), d_igain.reshape(8 * n_mp, -1), d_mgain.reshape(8 * n_mp, -1)], -1
+    )
+    gains_out = jnp.pad(gains_out, ((0, 0), (0, 8 * LANE - gains_out.shape[1])))
+    gains_out = gains_out.reshape(2, n_mp, 4, 8, LANE).transpose(1, 0, 2, 3, 4).reshape(n_mp, 8, 8, LANE)
+    to_column = lambda field, rows: field.reshape(rows, 8, -1).transpose(1, 0, 2).reshape(8, -1)
+    local_gains = jnp.concatenate(
+        [to_column(d_again, norm_attention.shape[0]), to_column(d_hgain, norm_hidden.shape[0])], -1
+    )
+    half = 4 * LANE
+    local_gains = jnp.pad(local_gains, ((0, 0), (half, half - local_gains.shape[1]))).reshape(8, 8, LANE)
+    residual = lax.dynamic_index_in_dim(residual.reshape(LAT, 2, n_mp, 4, own_cols), y, 1, keepdims=False)
+    residual = lax.dynamic_index_in_dim(residual, img, 2, keepdims=False)
+    residual = residual.transpose(1, 0, 2).reshape(n_mp, LAT * own_cols // LANE, LANE)
+    d_kv_own, d_wout_own, d_qkv_own, d_wo_own, d_rq_all, residual, gains_own = call_sampler_scatter(
+        n_mp,
+        d_kv_weight.reshape(2, n_mp, 4, -1, 2 * cols),
+        d_wout.reshape(n_mp, own_heads * HD, width),
+        (d_wqkv, d_wo),
+        d_rq,
+        residual,
+        gains_out,
+        local_gains,
+    )
+    d_kv_own = d_kv_own.astype(f32).reshape(2, 4, -1, 2, n_mp, own_heads * HD).transpose(3, 2, 0, 4, 1, 5)
+    d_kv_own = d_kv_own.reshape(2, sampler_key.shape[0], width)
+    d_rq_all = (
+        d_rq_all.reshape(2, 4, LAT, n_mp, own_heads * HD).transpose(2, 0, 3, 1, 4).reshape(LAT, width)
+    )
+    exact = partial(jnp.dot, precision=lax.Precision.HIGHEST, preferred_element_type=f32)
+    d_sampler_query = exact(latents.astype(f32).T, d_rq_all)
+    d_latents = residual.reshape(LAT, own_cols) + exact(d_rq_all, sampler_query.astype(f32).T)
+    gains_own = gains_own.reshape(-1)
+    parts = jnp.split(gains_own, (n_vision, n_vision + n_row, n_vision + 2 * n_row, half, half + n_att, half + n_att + n_hid))
+    third = local_width
+    return (
+        result.astype(bf),
+        tokens_grad,
+        d_qkv_own[:, :third],
+        d_qkv_own[:, third : 2 * third],
+        d_qkv_own[:, 2 * third :],
+        d_wo_own.T,
+        d_up_own,
+        d_down_own.T,
+        parts[1],
+        parts[4].reshape(norm_attention.shape),
+        parts[2],
+        parts[5].reshape(norm_hidden.shape),
+        d_sampler_query,
+        d_kv_own[0],
+        d_kv_own[1],
+        d_wout_own,
+        d_latents,
+        parts[0],
+    )
+
+
 def solution(mesh):
     in_specs = (
-        P(("dp", "img"), "mp", None),
-        P(("dp", "img"), "mp"),
-        P(("dp", "img"), "mp", None),
-        P(("dp", "mp", "img"), None, None),
-        P(("dp", "img"), "mp"),
-        P(("dp", "img"), "mp"),
-        P(("dp", "img"), "mp"),
-        P("mp", ("dp", "img")),
-        P(("dp", "img"), "mp"),
-        P("mp", ("dp", "img")),
-        P(("dp", "mp", "img")),
-        P("mp", ("dp", "img")),
-        P(("dp", "mp", "img")),
-        P("mp", ("dp", "img")),
-        P(("dp", "mp", "img"), None),
-        P(("dp", "mp", "img"), None),
-        P(("dp", "mp", "img"), None),
-        P(("dp", "mp", "img"), None),
-        P(None, ("dp", "mp", "img")),
-        P(("dp", "mp", "img")),
+        P((DP, IMG), MP, None),
+        P((DP, IMG), MP),
+        P((DP, IMG), MP, None),
+        P((DP, MP, IMG), None, None),
+        P((DP, IMG), MP),
+        P((DP, IMG), MP),
+        P((DP, IMG), MP),
+        P(MP, (DP, IMG)),
+        P((DP, IMG), MP),
+        P(MP, (DP, IMG)),
+        P((DP, MP, IMG)),
+        P(MP, (DP, IMG)),
+        P((DP, MP, IMG)),
+        P(MP, (DP, IMG)),
+        P((DP, MP, IMG), None),
+        P((DP, MP, IMG), None),
+        P((DP, MP, IMG), None),
+        P((DP, MP, IMG), None),
+        P(None, (DP, MP, IMG)),
+        P((DP, MP, IMG)),
     )
     out_specs = (
-        P(("dp", "img"), "mp", None),
-        P(("dp", "img"), "mp", None),
-        P(("dp", "img"), "mp"),
-        P(("dp", "img"), "mp"),
-        P(("dp", "img"), "mp"),
-        P("mp", ("dp", "img")),
-        P(("dp", "img"), "mp"),
-        P("mp", ("dp", "img")),
-        P(("dp", "mp", "img")),
-        P("mp", ("dp", "img")),
-        P(("dp", "mp", "img")),
-        P("mp", ("dp", "img")),
-        P(("dp", "mp", "img"), None),
-        P(("dp", "mp", "img"), None),
-        P(("dp", "mp", "img"), None),
-        P(("dp", "mp", "img"), None),
-        P(None, ("dp", "mp", "img")),
-        P(("dp", "mp", "img")),
-    )
-    return jax.shard_map(local, mesh=mesh, in_specs=in_specs, out_specs=out_specs, check_vma=False)
+        P((DP, IMG), MP, None),
+        P((DP, IMG), MP, None),
+        P((DP, IMG), MP),
+        P((DP, IMG), MP),
+        P((DP, IMG), MP),
+        P(MP, (DP, IMG)),
+        P((DP, IMG), MP),
+        P(MP, (DP, IMG)),
+        P((DP, MP, IMG)),
+        P(MP, (DP, IMG)),
+        P((DP, MP, IMG)),
+        P(MP, (DP, IMG)),
+        P((DP, MP, IMG), None),
+        P((DP, MP, IMG), None),
+        P((DP, MP, IMG), None),
+        P((DP, MP, IMG), None),
+        P(None, (DP, MP, IMG)),
+        P((DP, MP, IMG)),
+    )
+    n_dp, n_mp, n_img = mesh.shape[DP], mesh.shape[MP], mesh.shape[IMG]
+    whole_heads = D % (n_dp * n_mp * n_img * HD) == 0
+    run = partial(plane_local, n_mp) if (n_dp, n_img) == (2, 4) and whole_heads else local
+    return jax.shard_map(run, mesh=mesh, in_specs=in_specs, out_specs=out_specs, check_vma=False)

time: 2830 us -> 819 us (0.29)
  waiting for transfers between devices: 2230 us -> 1.99 us
  Pallas kernels: 0 us -> 615 us
  blocking collectives: 177 us -> 0 us
  matrix products: 222 us -> 94.7 us
  other arithmetic: 90.8 us -> 23 us
    reduce_scatter x24 -> x1, waiting for transfers between devices: 1270 us -> 0.01 us  [plane_local(): lax.psum_scatter(after_those(d_mgain, result_part), MP, scatter_dimension...]
    pallas_call x0 -> x13, Pallas kernels: none -> 615 us  [the longest x3 278 us: call_rows(): pl.pallas_call(partial(rows_kernel, n_mp, kind), name=f'rows_{kind}', out...]
    all_gather x19 -> x5, waiting for transfers between devices: 577 us -> 0.05 us  [the longest x1 0.02 us: plane_local(): tokens_all = lax.all_gather(tokens, MP, axis=0)]
    unnamed x55 -> x6, waiting for transfers between devices: 385 us -> 1.94 us
    dot_general x66 -> x15, matrix products: 222 us -> 94.7 us  [the longest x1 15.8 us: plane_local(): d_hidden = dot(grad_rows, down_turned)]
    unnamed x2 -> x0, blocking collectives: 80.8 us -> none
    all_gather x3 -> x0, blocking collectives: 57.9 us -> none  [the longest x1 38.6 us: local(): lax.all_gather(latents, ('dp', 'mp', 'img'), axis=1, tiled=True)]
    unnamed x368 -> x68, local copies, waits for them, and re-layouts: 55.4 us -> 7.92 us
  transfers between devices with their start and end apart: 49 -> 6, of which waited for: 46 -> 0; matrix products, arithmetic and copies ran while one was open for 10% -> 13% of each run, Pallas kernels for 0% -> 64%
where the time goes in v1:
time: 819 us; the launch traced here: 809 us
  Pallas kernels  615 us (75%)
  matrix products  94.7 us (12%)
  local copies, waits for them, and re-layouts  58.7 us (7%)
  other arithmetic  23 us (3%)
  between operations  15 us (2%)
    pallas_call x3, Pallas kernels, call_rows(): pl.pallas_call(partial(rows_kernel, n_mp, kind), name=f'rows_{kind}', out...  278 us
    pallas_call x1, Pallas kernels, call_sampler_gather(): pl.pallas_call(partial(sampler_gather_kernel, n_mp), name='sampler_gather...  74.4 us
    pallas_call x1, Pallas kernels, call_sampler_scatter(): pl.pallas_call(partial(sampler_scatter_kernel, n_mp), name='sampler_scatt...  70.9 us
    pallas_call x1, Pallas kernels, call_slot(): pl.pallas_call(partial(slot_kernel, n_mp), name='slot_grads', out_shape=j...  57 us
    pallas_call x1, Pallas kernels, call_table(): pl.pallas_call(partial(table_kernel, n_mp), name='table', out_shape=jax.S...  49.4 us
    pallas_call x1, Pallas kernels, call_pool_back(): pl.pallas_call(pool_back_kernel, name='pool_back', grid=(images,), out_sh...  30.2 us
    pallas_call x1, Pallas kernels, call_pool(): pl.pallas_call(pool_kernel, name='pool', grid=(images,), out_shape=outs,...  19.7 us
  transfers between devices with their start and end apart: 6, of which 0 were waited for; matrix products, arithmetic and copies ran while one was open for 13% of the time, Pallas kernels for 64%

profile of v1, /device:TPU:8, one launch (start us, length us, event | category | flops | bytes accessed | tf_op | source)
XLA Modules:
  0.0 808.9 jit_solution(15391149438298847590)
XLA Ops:
  20.4 74.4 %sampler_gather.1 = (bf16[8,256,1024]{2,1,0:T(8,128)(2,1)}, bf16[2,4,4,32,512]{4,3,2,1,0:T(8,128)(2,1)}, bf16[8,4,16,128]{3,2,1,0:T(8,128)(2,1)}, s32[4,8,128]{2...) custom-call(bf16[256,1024]{1,0:T(8,128)(2,1)} %bitcast.181, ...), custom_call_target="tpu_custom_call" | custom-call | tf_op jit(solution)/shard_map/sampler_gather/pallas_call | solution.py:910
  101.7 19.7 %pool.1 = (bf16[8,256,1024]{2,1,0:T(8,128)(2,1)}, bf16[8,256,512]{2,1,0:T(8,128)(2,1)}, bf16[8,64,256]{2,1,0:T(8,128)(2,1)}, bf16[8,64,2048]{2,1,0:T(8,128)(2,1)}) custom-call(bf16[8,256,1024]{2,1,0:T(8,128)(2,1)} %get-tuple-element.76.feats, f32[1,1024]{1,0:T(1,128)} %reshape.448.gain, bf16[1024,512]{1,0:T(8,128)(2,1)} %bitcast.155, ...), custom_call_target="tpu_custom_call" | custom-call | tf_op jit(solution)/shard_map/pool/pallas_call | solution.py:1620
  121.3 49.4 %table.1 = bf16[4,4,64,2048]{3,2,1,0:T(8,128)(2,1)} custom-call(bf16[2,2,2,64,2048]{4,3,2,1,0:T(8,128)(2,1)} %bitcast.159), custom_call_target="tpu_custom_call" | custom-call | tf_op jit(solution)/shard_map/table/pallas_call | solution.py:1014
  173.9 7.7 entry.1
  181.7 8.5 %fusion.24.proj = f32[512,1536]{1,0:T(8,128)} fusion(bf16[512,2048]{1,0:T(8,128)(2,1)} %bitcast.210, bf16[2048,1536]{1,0:T(8,128)(2,1)} %all-gather.8.cloned.1.call-done), kind=kOutput, calls=%fused_computation.117 | convolution fusion | flops 3221225472 | bytes 11534336 | tf_op jit(solution)/shard_map/dot_general | solution.py:1869
  190.2 8.1 attention.1
  213.6 110.8 %rows_forward.1 = (f32[2,64,2048]{2,1,0:T(8,128)}, bf16[2,4,64,2048]{3,2,1,0:T(8,128)(2,1)}, f32[8,2560]{1,0:T(8,128)}, bf16[8,256,2048]{2,1,0:T(8,128)(2,1)}) custom-call(bf16[2,4,64,2048]{3,2,1,0:T(8,128)(2,1)} %bitcast.160, bf16[256,2048]{1,0:T(8,128)(2,1)} %bitcast.152, bf16[2,64,2048]{2,1,0:T(8,128)(2,1)} %dynamic-slice_bitcast_fusion.refs_2_.refs_5_, ...), custom_call_target="tpu_custom_call" | custom-call | tf_op jit(solution)/shard_map/rows_forward/pallas_call | solution.py:1449
  328.8 8.1 %fusion.25 = f32[512,2048]{1,0:T(8,128)S(1)} fusion(bf16[512,2048]{1,0:T(8,128)(2,1)} %bitcast.214, bf16[2048,2048]{1,0:T(8,128)(2,1)} %all-gather.12.cloned.1.call-done), kind=kOutput, calls=%fused_computation.118 | convolution fusion | flops 4294967296 | bytes 14680064 | tf_op jit(solution)/shard_map/dot_general | solution.py:1900
  337.0 15.8 %multiply_reduce_fusion.1 = (f32[512]{0:T(512)S(1)}, f32[512]{0:T(512)S(1)}, f32[512]{0:T(512)S(1)}, f32[512]{0:T(512)S(1)}, f32[512,2048]{1,0:T(8,128)}, /*index=5*/f32[512,2048]{1,0:T(8,128)}, f32[512,2048]{1,0:T(8,128)}) fusion(f32[2048]{0:T(1024)S(1)} %mul.182, f32[512,2048]{1,0:T(8,128)S(1)} %fusion.25, bf16[512,2048]{1,0:T(8,128)(2,1)S(1)} %bitcast.164, ...), kind=kOutput, calls=%fused_computation.10 | convolution fusion | flops 4369414144 | bytes 27279360 | tf_op jit(solution)/shard_map/dot_general | solution.py:1904
  353.4 8.2 %line_sum_8.1 = f32[8,512]{1,0:T(8,128)} custom-call(f32[8,512]{1,0:T(8,128)} %concatenate.31.own), custom_call_target="tpu_custom_call" | custom-call | tf_op jit(solution)/shard_map/line_sum_8/pallas_call | solution.py:1276
  362.5 10.7 %convolution_convert_fusion.5 = bf16[512,2048]{1,0:T(8,128)(2,1)} fusion(bf16[2048,2048]{1,0:T(8,128)(2,1)} %bitcast.208, f32[512,2048]{1,0:T(8,128)} %get-tuple-element.202, f32[512]{0:T(512)S(1)} %bitcast.191, f32[512]{0:T(512)S(1)} %get-tuple-element.223, f32[2048]{0:T(1024)S(1)} %mul.182), kind=kOutput, calls=%fused_computation.30 | convolution fusion | flops 4300210176 | bytes 14692352 | tf_op jit(solution)/shard_map/dot_general | solution.py:1920
  373.1 7.2 convolution_convert_fusion.2
  380.3 4.7 multiply_reduce_fusion
  385.1 6.8 convolution_convert_fusion.1
  391.9 9.3 %convolution_convert_fusion.6 = bf16[512,2048]{1,0:T(8,128)(2,1)} fusion(bf16[512,2048]{1,0:T(8,128)(2,1)S(1)} %get-tuple-element.205, bf16[2048,2048]{1,0:T(8,128)(2,1)} %all-gather.12.cloned.1.call-done), kind=kOutput, calls=%fused_computation.31 | convolution fusion | flops 4296015872 | bytes 12582912 | tf_op jit(solution)/shard_map/dot_general | solution.py:1927
  401.2 92.0 %rows_middle.1 = (f32[2,64,2048]{2,1,0:T(8,128)}, f32[1,2048]{1,0:T(1,128)}, bf16[2,4,64,2048]{3,2,1,0:T(8,128)(2,1)}, f32[4,8,128]{2,1,0:T(8,128)}, f32[256,2048]{1,0:T(8,128)}) custom-call(bf16[2,4,64,2048]{3,2,1,0:T(8,128)(2,1)} %bitcast.170, bf16[8,256,2048]{2,1,0:T(8,128)(2,1)} %bitcast.148, f32[2,64,2048]{2,1,0:T(8,128)} %get-tuple-element.86.refs_2_, ...), custom_call_target="tpu_custom_call" | custom-call | tf_op jit(solution)/shard_map/rows_middle/pallas_call | solution.py:1449
  501.6 11.4 %attention_back.1 = bf16[512,1536]{1,0:T(8,128)(2,1)} custom-call(bf16[512,1536]{1,0:T(8,128)(2,1)} %get-tuple-element.95.low, bf16[512,512]{1,0:T(8,128)(2,1)} %get-tuple-element.207.grad, f32[4,256,128]{2,1,0:T(8,128)} %constant.199.clone.tables), custom_call_target="tpu_custom_call" | custom-call | tf_op jit(solution)/shard_map/attention_back/pallas_call | solution.py:1566
  513.0 8.1 %convolution_convert_fusion.4 = bf16[512,2048]{1,0:T(8,128)(2,1)} fusion(bf16[512,1536]{1,0:T(8,128)(2,1)} %attention_back.1, bf16[2048,1536]{1,0:T(8,128)(2,1)} %all-gather.8.cloned.1.call-done), kind=kOutput, calls=%fused_computation.29 | convolution fusion | flops 3222274048 | bytes 9961472 | tf_op jit(solution)/shard_map/dot_general | solution.py:1969
  523.2 75.3 %rows_last.1 = (bf16[2,64,2048]{2,1,0:T(8,128)(2,1)}, bf16[2,64,2048]{2,1,0:T(8,128)(2,1)}, f32[1,2048]{1,0:T(1,128)}, f32[256,2048]{1,0:T(8,128)}) custom-call(bf16[2,4,64,2048]{3,2,1,0:T(8,128)(2,1)} %bitcast.168, bf16[8,256,2048]{2,1,0:T(8,128)(2,1)} %bitcast.149, bf16[2,64,2048]{2,1,0:T(8,128)(2,1)} %dynamic-slice_bitcast_fusion.refs_2_.refs_5_, ...), custom_call_target="tpu_custom_call" | custom-call | tf_op jit(solution)/shard_map/rows_last/pallas_call | solution.py:1449
  604.5 57.0 %slot_grads.1.slot = bf16[8,64,2048]{2,1,0:T(8,128)(2,1)} custom-call(bf16[4,4,64,2048]{3,2,1,0:T(8,128)(2,1)} %select_select_fusion.part), custom_call_target="tpu_custom_call" | custom-call | tf_op jit(solution)/shard_map/slot_grads/pallas_call | solution.py:1085
  661.5 30.2 %pool_back.1 = (bf16[1024,512]{1,0:T(8,128)(2,1)}, f32[1024,128]{1,0:T(8,128)}, f32[64,256]{1,0:T(8,128)}, f32[64,2048]{1,0:T(8,128)}, bf16[256,2048]{1,0:T(8,128)(2,1)}) custom-call(bf16[8,64,2048]{2,1,0:T(8,128)(2,1)} %slot_grads.1.slot, bf16[256,2048]{1,0:T(8,128)(2,1)} %bitcast.158, bf16[8,256,1024]{2,1,0:T(8,128)(2,1)} %get-tuple-element.102.vision_low, ...), custom_call_target="tpu_custom_call" | custom-call | tf_op jit(solution)/shard_map/pool_back/pallas_call | solution.py:1700
  697.1 4.4 convolution_convert_fusion.3
  701.6 5.4 convolution_convert_fusion
  706.9 70.9 %sampler_scatter.1 = (bf16[8,32,512]{2,1,0:T(8,128)(2,1)}, f32[64,2048]{1,0:T(8,128)}, f32[256,1536]{1,0:T(8,128)}, f32[256,512]{1,0:T(8,128)}, f32[8,64,256]{2,...) custom-call(bf16[2,4,4,32,512]{4,3,2,1,0:T(8,128)(2,1)} %bitcast.174, bf16[4,64,2048]{2,1,0:T(8,128)(2,1)} %bitcast.175, ...), custom_call_target="tpu_custom_call" | custom-call | tf_op jit(solution)/shard_map/sampler_scatter/pallas_call | solution.py:1223
  (225 shorter events, 89.8 us)
Async XLA Ops:
  7.2 9.0 %copy-start = (bf16[64,2048]{1,0:T(8,128)(2,1)S(1)}, bf16[64,2048]{1,0:T(8,128)(2,1)}, u32[]{:S(2)}) copy-start(bf16[64,2048]{1,0:T(8,128)(2,1)} %param.37) | copy-start | bytes 786436
  7.2 9.0 %copy-start.18 = (bf16[64,64]{1,0:T(8,128)(2,1)S(1)}, bf16[64,64]{1,0:T(8,128)(2,1)}, u32[]{:S(2)}) copy-start(bf16[64,64]{1,0:T(8,128)(2,1)} %param.41) | copy-start | bytes 24580
  7.2 8.4 %copy-start.20 = (bf16[32,2048]{1,0:T(8,128)(2,1)S(1)}, bf16[32,2048]{1,0:T(8,128)(2,1)}, u32[]{:S(2)}) copy-start(bf16[32,2048]{1,0:T(8,128)(2,1)} %param.39) | copy-start | bytes 393220
  7.2 163.5 %all-gather.14.cloned.1.call-start = ((), (), s32[]{:S(2)}) async-start(), calls=%async_computation.5 | async-start | bytes 2621440 | tf_op jit(solution)/shard_map/all_gather | solution.py:1829
  8.0 10.3 %copy-start.23 = (s32[2,64]{1,0:T(2,128)S(1)}, s32[2,64]{1,0:T(2,128)}, u32[]{:S(2)}) copy-start(s32[2,64]{1,0:T(2,128)} %param.24) | copy-start | bytes 1540
  8.0 11.0 %copy-start.24 = (bf16[32]{0:T(256)(128)(2,1)S(1)}, bf16[32]{0:T(256)(128)(2,1)}, u32[]{:S(2)}) copy-start(bf16[32]{0:T(256)(128)(2,1)} %param.42) | copy-start | bytes 196
  8.0 11.0 %copy-start.25 = (bf16[64]{0:T(256)(128)(2,1)S(1)}, bf16[64]{0:T(256)(128)(2,1)}, u32[]{:S(2)}) copy-start(bf16[64]{0:T(256)(128)(2,1)} %param.33) | copy-start | bytes 388
  8.0 11.0 %copy-start.26 = (bf16[64]{0:T(256)(128)(2,1)S(1)}, bf16[64]{0:T(256)(128)(2,1)}, u32[]{:S(2)}) copy-start(bf16[64]{0:T(256)(128)(2,1)} %param.35) | copy-start | bytes 388
  8.0 173.7 %all-gather.8.cloned.1.call-start = ((), (), s32[]{:S(2)}) async-start(), calls=%async_computation.1 | async-start | bytes 7077888 | tf_op jit(solution)/shard_map/all_gather | solution.py:1826
  10.1 195.7 %all-gather.10.cloned.1.call-start = ((), (), s32[]{:S(2)}) async-start(), calls=%async_computation.2 | async-start | bytes 2359296 | tf_op jit(solution)/shard_map/all_gather | solution.py:1830
  10.9 316.1 %all-gather.16.cloned.1.call-start = ((), (), s32[]{:S(2)}) async-start(), calls=%async_computation.6 | async-start | bytes 2621440 | tf_op jit(solution)/shard_map/all_gather | solution.py:1870
  190.2 9.3 %copy-start.11 = (bf16[2048,256]{1,0:T(8,128)(2,1)S(1)}, bf16[2048,256]{1,0:T(8,128)(2,1)}, u32[]{:S(2)}) copy-start(bf16[2048,256]{1,0:T(8,128)(2,1)} %param.32) | copy-start | bytes 3145732
  198.2 9.8 %copy-start.12 = (f32[512,512]{1,0:T(8,128)S(1)}, f32[512,512]{1,0:T(8,128)}, u32[]{:S(2)}) copy-start(f32[512,512]{1,0:T(8,128)} %get-tuple-element.84) | copy-start | bytes 3145732
  198.3 130.5 %all-gather.12.cloned.1.call-start = ((), (), s32[]{:S(2)}) async-start(), calls=%async_computation.3 | async-start | bytes 9437184 | tf_op jit(solution)/shard_map/all_gather | solution.py:1831
  198.9 597.9 %reduce-scatter.2.cloned.1.call-start = ((), (), s32[]{:S(2)}) async-start(), calls=%async_computation.4 | async-start | bytes 2621440 | tf_op jit(solution)/shard_map/reduce_scatter | solution.py:1949
  328.8 8.2 %copy-start.27 = (bf16[8,256,2048]{2,1,0:T(8,128)(2,1)S(1)}, bf16[8,256,2048]{2,1,0:T(8,128)(2,1)}, u32[]{:S(2)}) copy-start(bf16[8,256,2048]{2,1,0:T(8,128)(2,1)} %get-tuple-element.89) | copy-start | bytes 25165828
  336.9 15.8 %copy-start.1 = (f32[512,2048]{1,0:T(8,128)}, f32[512,2048]{1,0:T(8,128)S(1)}, u32[]{:S(2)}) copy-start(f32[512,2048]{1,0:T(8,128)S(1)} %fusion.25) | copy-start | bytes 12582916
  362.5 10.7 %copy-start.3 = (f32[512,2048]{1,0:T(8,128)S(1)}, f32[512,2048]{1,0:T(8,128)}, u32[]{:S(2)}) copy-start(f32[512,2048]{1,0:T(8,128)} %get-tuple-element.202) | copy-start | bytes 12582916
  373.1 7.2 copy-start.4
  373.1 7.2 copy-start.5
  513.0 8.8 %copy-start.22 = (f32[1,2048]{1,0:T(1,128)S(1)}, f32[1,2048]{1,0:T(1,128)}, u32[]{:S(2)}) copy-start(f32[1,2048]{1,0:T(1,128)} %get-tuple-element.93) | copy-start | bytes 24580
  706.9 73.0 %copy-start.8 = (f32[256,2048]{1,0:T(8,128)S(1)}, f32[256,2048]{1,0:T(8,128)}, u32[]{:S(2)}) copy-start(f32[256,2048]{1,0:T(8,128)} %get-tuple-element.114) | copy-start | bytes 6291460
  787.7 9.1 %copy-start.6 = (f32[2,64,2048]{2,1,0:T(8,128)S(1)}, f32[2,64,2048]{2,1,0:T(8,128)}, u32[]{:S(2)}) copy-start(f32[2,64,2048]{2,1,0:T(8,128)} %get-tuple-element.86.refs_2_) | copy-start | bytes 3145732
  789.6 9.3 %copy-start.14 = (bf16[2,64,2048]{2,1,0:T(8,128)(2,1)S(1)}, bf16[2,64,2048]{2,1,0:T(8,128)(2,1)}, u32[]{:S(2)}) copy-start(bf16[2,64,2048]{2,1,0:T(8,128)(2,1)} %get-tuple-element.251) | copy-start | bytes 1572868
  (12 other events, 57.1 us)
Sparse Core Ops, SparseCore 0:
  9.6 57.1 all-gather.13
  68.7 46.0 all-gather.7
  116.7 33.2 all-gather.9
  198.4 62.1 all-gather.15
  262.4 63.8 all-gather.11
  496.7 43.9 reduce-scatter.1

commit v2 on v1

--- a/solution.py
+++ b/solution.py
@@ -807,8 +807,8 @@
 
 
 def sampler_gather_kernel(
-    n_mp, feat, key_value, pack, rq_part, slots, wout, latents,
-    feats_o, kv_o, pack_o, slots_o, rq_o, wout_o, latents_o,
+    n_mp, feat, key_value, pack, rq_part, slots, wout, latents, qkv, turned_wo,
+    feats_o, kv_o, pack_o, slots_o, rq_o, wout_o, latents_o, qkv_o, turned_wo_o,
     rq_plane, rq_line, send, recv, here,
 ):
     spot = Spot(n_mp)
@@ -823,6 +823,8 @@
         pltpu.make_async_copy(feat, feats_o.at[p], here.at[3]),
         pltpu.make_async_copy(wout, wout_o.at[z], here.at[4]),
         pltpu.make_async_copy(latents, latents_o.at[z], here.at[5]),
+        pltpu.make_async_copy(qkv, qkv_o.at[p], here.at[6]),
+        pltpu.make_async_copy(turned_wo, turned_wo_o.at[p], here.at[7]),
     ]
     for copy in own:
         copy.start()
@@ -846,7 +848,10 @@
     for k in range(7):
         wire.go(partial(rq_move, k))
     images = PlaneGather(wire, spot, chunked(feats_o, 1))
+    layer = [PlaneGather(wire, spot, chunked(array, 1)) for array in (qkv_o, turned_wo_o)]
     images.begin()
+    for weight in layer:
+        weight.begin()
     for k in range(7):
         kv_move(k).wait_recv()
     kv_line.stage(0)
@@ -879,7 +884,11 @@
     for hop in range(3, n_mp):
         kv_line.stage(hop)
         wout_line.stage(hop)
+    for weight in layer:
+        weight.middle()
     images.core()
+    for weight in layer:
+        weight.end()
     for d in range(1, n_mp):
         line_move(d).wait_recv()
     total = rq_line[0].astype(f32)
@@ -888,10 +897,12 @@
     rq_o[...] = total.astype(bf)
     for k in range(7):
         pack_move(k).wait_recv()
+    for weight in layer:
+        weight.core()
     wire.finish()
 
 
-def call_sampler_gather(n_mp, feat, key_value, pack, rq_part, slots, wout, latents):
+def call_sampler_gather(n_mp, feat, key_value, pack, rq_part, slots, wout, latents, qkv, turned_wo):
     shape = jax.ShapeDtypeStruct
     rows_v, width_v = feat.shape[1:]
     bf = jnp.bfloat16
@@ -903,25 +914,27 @@
         shape(rq_part.shape[1:], bf),
         shape((n_mp,) + wout.shape, bf),
         shape((n_mp,) + latents.shape, bf),
-    )
-    wires = 7 * 3 + 8 + 5 * 2 * (n_mp - 1) + n_mp
+        shape((8,) + qkv.shape, bf),
+        shape((8,) + turned_wo.shape, bf),
+    )
+    wires = 7 * 3 + 3 * 8 + 5 * 2 * (n_mp - 1) + n_mp
     anywhere = pl.BlockSpec(memory_space=pl.ANY)
     near = pl.BlockSpec(memory_space=VMEM)
     return pl.pallas_call(
         partial(sampler_gather_kernel, n_mp),
         name="sampler_gather",
         out_shape=outs,
-        in_specs=[near] * 7,
-        out_specs=(anywhere,) * 4 + (near, anywhere, anywhere),
+        in_specs=[near] * 9,
+        out_specs=(anywhere,) * 4 + (near,) + (anywhere,) * 4,
         scratch_shapes=[
             VMEM(rq_part.shape, bf),
             VMEM((n_mp,) + rq_part.shape[1:], bf),
             pltpu.SemaphoreType.DMA((wires,)),
             pltpu.SemaphoreType.DMA((wires,)),
-            pltpu.SemaphoreType.DMA((6,)),
+            pltpu.SemaphoreType.DMA((8,)),
         ],
         compiler_params=pltpu.CompilerParams(collective_id=1, has_side_effects=True, vmem_limit_bytes=BIG),
-    )(feat[0], key_value, pack, rq_part, slots, wout, latents)
+    )(feat[0], key_value, pack, rq_part, slots, wout, latents, qkv, turned_wo)
 
 
 def table_kernel(n_mp, part, table, near_c, half_x, half_y, full_x, full_y, sums, emb, send, recv, here):
@@ -1304,10 +1317,10 @@
     )
 
 
-CHUNK = 16
-HOP = 2
+CHUNK = 32
+HOP = 3
 SIDE = 4
-SIDE_STEP = 6
+SIDE_STEP = 3
 
 
 def rows_kernel(n_mp, kind, *refs):
@@ -1725,9 +1738,11 @@
 
 
 def call_entry(slot, table, tokens, gain):
-    blocks, rows, width = tokens.shape
+    n_mp, batch, rows, width = tokens.shape
+    blocks = n_mp * batch
     one = pl.BlockSpec((1, rows, width), lambda i, slot: (i, 0, 0))
-    shape = jax.ShapeDtypeStruct(tokens.shape, jnp.bfloat16)
+    shape = jax.ShapeDtypeStruct((blocks, rows, width), jnp.bfloat16)
+    tokens = tokens.reshape(blocks, rows, width)
     return pl.pallas_call(
         entry_kernel,
         name="entry",
@@ -1736,7 +1751,7 @@
             grid=(blocks,),
             in_specs=[
                 pl.BlockSpec((1, rows, width), lambda i, slot: (jnp.maximum(slot[i], 0), 0, 0)),
-                one,
+                pl.BlockSpec((1, rows, width), lambda i, slot: (lax.rem(i, n_mp) * batch + i // n_mp, 0, 0)),
                 pl.BlockSpec((1, width), lambda i, slot: (0, 0)),
             ],
             out_specs=(one, one),
@@ -1812,7 +1827,7 @@
     gain_rows = 16
     pack = jnp.pad(flat_gains, (0, gain_rows * LANE - flat_gains.shape[0])).reshape(gain_rows, LANE)
     first_slots = jnp.zeros((8, LANE), jnp.int32).at[:batch, 0].set(slot_index[:, 0])
-    feats, kv_all, packs, slots, rq, wout_all, latents_line = call_sampler_gather(
+    feats, kv_all, packs, slots, rq, wout_all, latents_line, qkv_full, wo_turned = call_sampler_gather(
         n_mp,
         features,
         key_value,
@@ -1821,15 +1836,15 @@
         first_slots,
         sampler_output,
         latents.reshape(-1, LANE),
-    )
-    over = (DP, IMG)
-    qkv_full = lax.all_gather(
-        jnp.concatenate([query_weight, key_weight, value_weight], 1), over, axis=0, tiled=True
-    )
+        jnp.concatenate([query_weight, key_weight, value_weight], 1),
+        output_weight.T,
+    )
+    qkv_full = qkv_full.reshape(width, -1)
+    wo_turned = wo_turned.reshape(width, -1)
     tokens_all = lax.all_gather(tokens, MP, axis=0)
-    wo_full = lax.all_gather(output_weight, over, axis=1, tiled=True)
-    up_full = lax.all_gather(up_weight, over, axis=0, tiled=True)
-
+    up_sent, out_grad_sent = after_those((tokens_all, slots), (up_weight, out_grad))
+    up_full = lax.all_gather(up_sent, (DP, IMG), axis=0, tiled=True)
+    grads_all = lax.all_gather(out_grad_sent, MP, axis=0)
     own_cols = latents.shape[1]
     column = lambda n, at: jnp.arange(n) == at
     here = (column(2, y)[:, None, None] & column(4, img)[None, None, :])[None, ..., None]
@@ -1857,19 +1872,17 @@
     table = call_table(n_mp, branch).reshape(-1, LAT, width)
 
     block_image = jnp.where(slot_first >= 0, slot_first // LAT, -1)
-    tokens_blocks = tokens_all.transpose(1, 0, 2, 3).reshape(batch * n_mp, block, width)
     entry_all, normed_rows = call_entry(
-        block_image.T.reshape(-1).astype(jnp.int32), table, tokens_blocks, input_gain
+        block_image.T.reshape(-1).astype(jnp.int32), table, tokens_all, input_gain
     )
     entry = lax.dynamic_index_in_dim(entry_all.reshape(batch, n_mp, block, width), z, 1, keepdims=False)
     normed_rows = normed_rows.reshape(-1, width)
     rows = normed_rows.shape[0]
-    local_width = wo_full.shape[0]
+    local_width = wo_turned.shape[1]
     tables = rotary_rows()
     low, attended = call_attention(batch, dot(normed_rows, qkv_full), tables)
-    grads_all = lax.all_gather(after_those(attended, out_grad), MP, axis=0)
     owner_first = lambda field: field.reshape(batch, n_mp, block).transpose(1, 0, 2).reshape(-1)
-    turned = jnp.sum(wo_full.astype(f32) * attention_gain[:, None], 0)
+    turned = dot(jnp.broadcast_to(attention_gain.astype(bf), (8, local_width)), wo_turned.T)[0]
     first = jnp.concatenate([owner_first(jnp.sum(attended, -1)), turned])
     second = jnp.pad(owner_first(jnp.sum(attended * attended, -1)), (0, width))
     stats = as_rows(jnp.stack([first, second]))
@@ -1883,7 +1896,7 @@
         "forward",
         5,
         (shape(own_shape, f32), shape(split_rows, bf), shape(stats.shape, f32), shape(side_shape, bf)),
-        dot((attended * attention_gain).astype(bf), wo_full).astype(bf).reshape(split_rows),
+        dot((attended * attention_gain).astype(bf), wo_turned.T).astype(bf).reshape(split_rows),
         down_weight.T,
         entry,
         middle_gain,
@@ -1951,7 +1964,7 @@
     )
     result = after + result_sum.astype(f32)
     after_rows = after_rows.reshape(rows, width)
-    d_mixed = dot(after_rows, wo_full.T)
+    d_mixed = dot(after_rows, wo_turned)
     scaled = d_mixed * attention_gain
     d_again = jnp.sum(d_mixed * attn_normed, 0)
     d_attended = attn_factor * (

time: 819 us -> 785 us (0.958)
  Pallas kernels: 615 us -> 584 us
    pallas_call x3, Pallas kernels: 278 us -> 228 us  [call_rows(): pl.pallas_call(partial(rows_kernel, n_mp, kind), name=f'rows_{kind}', out...]
    pallas_call x1, Pallas kernels: 49.4 us -> 69.9 us  [call_table(): pl.pallas_call(partial(table_kernel, n_mp), name='table', out_shape=jax.S...]
  transfers between devices with their start and end apart: 6 -> 4, of which waited for: 0 -> 0; matrix products, arithmetic and copies ran while one was open for 13% -> 11% of each run, Pallas kernels for 64% -> 55%
where the time goes in v2:
time: 785 us; the launch traced here: 778 us
  Pallas kernels  584 us (74%)
  matrix products  95.7 us (12%)
  local copies, waits for them, and re-layouts  60.6 us (8%)
  other arithmetic  20.7 us (3%)
  between operations  14.7 us (2%)
    pallas_call x3, Pallas kernels, call_rows(): pl.pallas_call(partial(rows_kernel, n_mp, kind), name=f'rows_{kind}', out...  228 us
    pallas_call x1, Pallas kernels, call_sampler_scatter(): pl.pallas_call(partial(sampler_scatter_kernel, n_mp), name='sampler_scatt...  71 us
    pallas_call x1, Pallas kernels, call_table(): pl.pallas_call(partial(table_kernel, n_mp), name='table', out_shape=jax.S...  69.9 us
    pallas_call x1, Pallas kernels, call_sampler_gather(): pl.pallas_call(partial(sampler_gather_kernel, n_mp), name='sampler_gather...  69.5 us
    pallas_call x1, Pallas kernels, call_slot(): pl.pallas_call(partial(slot_kernel, n_mp), name='slot_grads', out_shape=j...  59.7 us
    pallas_call x1, Pallas kernels, call_pool_back(): pl.pallas_call(pool_back_kernel, name='pool_back', grid=(images,), out_sh...  30.3 us
    pallas_call x1, Pallas kernels, call_pool(): pl.pallas_call(pool_kernel, name='pool', grid=(images,), out_shape=outs,...  19.6 us
    dot_general x1, matrix products, plane_local(): d_hidden = dot(grad_rows, down_turned)  15.7 us
  transfers between devices with their start and end apart: 4, of which 0 were waited for; matrix products, arithmetic and copies ran while one was open for 11% of the time, Pallas kernels for 55%

profile of v2, /device:TPU:8, one launch (start us, length us, event | category | flops | bytes accessed | tf_op | source)
XLA Modules:
  0.0 777.8 jit_solution(2932062078402669273)
XLA Ops:
  23.6 69.5 %sampler_gather.1 = (bf16[8,256,1024]{2,1,0:T(8,128)(2,1)}, bf16[2,4,4,32,512]{4,3,2,1,0:T(8,128)(2,1)}, bf16[8,4,16,128]{3,2,1,0:T(8,128)(2,1)}, s32[4,8,128]{2...) custom-call(bf16[256,1024]{1,0:T(8,128)(2,1)} %bitcast.185, ...), custom_call_target="tpu_custom_call" | custom-call | tf_op jit(solution)/shard_map/sampler_gather/pallas_call | solution.py:923
  104.5 19.6 %pool.1 = (bf16[8,256,1024]{2,1,0:T(8,128)(2,1)}, bf16[8,256,512]{2,1,0:T(8,128)(2,1)}, bf16[8,64,256]{2,1,0:T(8,128)(2,1)}, bf16[8,64,2048]{2,1,0:T(8,128)(2,1)}) custom-call(bf16[8,256,1024]{2,1,0:T(8,128)(2,1)} %get-tuple-element.79.feats, f32[1,1024]{1,0:T(1,128)} %reshape.454.gain, bf16[1024,512]{1,0:T(8,128)(2,1)} %bitcast.156, ...), custom_call_target="tpu_custom_call" | custom-call | tf_op jit(solution)/shard_map/pool/pallas_call | solution.py:1633
  124.2 69.9 %table.1 = bf16[4,4,64,2048]{3,2,1,0:T(8,128)(2,1)} custom-call(bf16[2,2,2,64,2048]{4,3,2,1,0:T(8,128)(2,1)} %bitcast.160), custom_call_target="tpu_custom_call" | custom-call | tf_op jit(solution)/shard_map/table/pallas_call | solution.py:1027
  199.9 8.0 %entry.1 = (bf16[8,64,2048]{2,1,0:T(8,128)(2,1)}, bf16[8,64,2048]{2,1,0:T(8,128)(2,1)}) custom-call(s32[8]{0:T(128)} %reshape.452.slot, bf16[16,64,2048]{2,1,0:T(8,128)(2,1)} %bitcast.149, bf16[8,64,2048]{2,1,0:T(8,128)(2,1)} %all-gather.8.cloned.1.call-done.tokens, f32[1,2048]{1,0:T(1,128)} %reshape.460.gain.refs_4_), custom_call_target="tpu_custom_call" | custom-call | tf_op jit(solution)/shard_map/entry/pallas_call | solution.py:1746
  207.9 8.5 %fusion.24.proj = f32[512,1536]{1,0:T(8,128)} fusion(bf16[512,2048]{1,0:T(8,128)(2,1)} %bitcast.217, bf16[2048,1536]{1,0:T(8,128)(2,1)} %bitcast.215), kind=kOutput, calls=%fused_computation.116 | convolution fusion | flops 3221225472 | bytes 11534336 | tf_op jit(solution)/shard_map/dot_general | solution.py:1883
  216.3 8.0 %attention.1 = (bf16[512,1536]{1,0:T(8,128)(2,1)}, f32[512,512]{1,0:T(8,128)}) custom-call(f32[512,1536]{1,0:T(8,128)} %fusion.24.proj, f32[4,256,128]{2,1,0:T(8,128)} %constant.199.clone.tables), custom_call_target="tpu_custom_call" | custom-call | tf_op jit(solution)/shard_map/attention/pallas_call | solution.py:1524
  233.0 83.5 %rows_forward.1 = (f32[2,64,2048]{2,1,0:T(8,128)}, bf16[2,4,64,2048]{3,2,1,0:T(8,128)(2,1)}, f32[8,2560]{1,0:T(8,128)}, bf16[8,256,2048]{2,1,0:T(8,128)(2,1)}) custom-call(bf16[2,4,64,2048]{3,2,1,0:T(8,128)(2,1)} %bitcast.161, bf16[256,2048]{1,0:T(8,128)(2,1)} %bitcast.153, bf16[2,64,2048]{2,1,0:T(8,128)(2,1)} %dynamic-slice_bitcast_fusion.refs_2_.refs_5_, ...), custom_call_target="tpu_custom_call" | custom-call | tf_op jit(solution)/shard_map/rows_forward/pallas_call | solution.py:1462
  319.1 7.9 %fusion.25 = f32[512,2048]{1,0:T(8,128)S(1)} fusion(bf16[512,2048]{1,0:T(8,128)(2,1)} %bitcast.221, bf16[2048,2048]{1,0:T(8,128)(2,1)} %all-gather.6.cloned.1.call-done), kind=kOutput, calls=%fused_computation.117 | convolution fusion | flops 4294967296 | bytes 14680064 | tf_op jit(solution)/shard_map/dot_general | solution.py:1913
  327.0 15.7 %multiply_reduce_fusion.1 = (f32[512]{0:T(512)S(1)}, f32[512]{0:T(512)S(1)}, f32[512]{0:T(512)S(1)}, f32[512]{0:T(512)S(1)}, f32[512,2048]{1,0:T(8,128)}, /*index=5*/f32[512,2048]{1,0:T(8,128)}, f32[512,2048]{1,0:T(8,128)}) fusion(f32[2048]{0:T(1024)S(1)} %mul.172, f32[512,2048]{1,0:T(8,128)S(1)} %fusion.25, bf16[512,2048]{1,0:T(8,128)(2,1)S(1)} %bitcast.167, ...), kind=kOutput, calls=%fused_computation.10 | convolution fusion | flops 4369414144 | bytes 27279360 | tf_op jit(solution)/shard_map/dot_general | solution.py:1917
  343.4 8.9 %line_sum_8.1 = f32[8,512]{1,0:T(8,128)} custom-call(f32[8,512]{1,0:T(8,128)} %concatenate.31.own), custom_call_target="tpu_custom_call" | custom-call | tf_op jit(solution)/shard_map/line_sum_8/pallas_call | solution.py:1289
  353.2 10.7 %convolution_convert_fusion.5 = bf16[512,2048]{1,0:T(8,128)(2,1)} fusion(bf16[2048,2048]{1,0:T(8,128)(2,1)} %bitcast.213, f32[512,2048]{1,0:T(8,128)} %get-tuple-element.208, f32[512]{0:T(512)S(1)} %bitcast.196, f32[512]{0:T(512)S(1)} %get-tuple-element.229, f32[2048]{0:T(1024)S(1)} %mul.172), kind=kOutput, calls=%fused_computation.29 | convolution fusion | flops 4300210176 | bytes 14692352 | tf_op jit(solution)/shard_map/dot_general | solution.py:1933
  363.9 7.1 convolution_convert_fusion.2
  371.1 5.0 multiply_reduce_fusion
  376.0 6.9 convolution_convert_fusion.1
  382.9 9.3 %convolution_convert_fusion.6 = bf16[512,2048]{1,0:T(8,128)(2,1)} fusion(bf16[512,2048]{1,0:T(8,128)(2,1)S(1)} %get-tuple-element.211, bf16[2048,2048]{1,0:T(8,128)(2,1)} %all-gather.6.cloned.1.call-done), kind=kOutput, calls=%fused_computation.30 | convolution fusion | flops 4296015872 | bytes 12582912 | tf_op jit(solution)/shard_map/dot_general | solution.py:1940
  392.3 79.4 %rows_middle.1 = (f32[2,64,2048]{2,1,0:T(8,128)}, f32[1,2048]{1,0:T(1,128)}, bf16[2,4,64,2048]{3,2,1,0:T(8,128)(2,1)}, f32[4,8,128]{2,1,0:T(8,128)}, f32[256,2048]{1,0:T(8,128)}) custom-call(bf16[2,4,64,2048]{3,2,1,0:T(8,128)(2,1)} %bitcast.173, bf16[8,256,2048]{2,1,0:T(8,128)(2,1)} %bitcast.150, f32[2,64,2048]{2,1,0:T(8,128)} %get-tuple-element.91.refs_2_, ...), custom_call_target="tpu_custom_call" | custom-call | tf_op jit(solution)/shard_map/rows_middle/pallas_call | solution.py:1462
  480.1 11.4 %attention_back.1 = bf16[512,1536]{1,0:T(8,128)(2,1)} custom-call(bf16[512,1536]{1,0:T(8,128)(2,1)} %get-tuple-element.101.low, bf16[512,512]{1,0:T(8,128)(2,1)} %get-tuple-element.213.grad, f32[4,256,128]{2,1,0:T(8,128)} %constant.199.clone.tables), custom_call_target="tpu_custom_call" | custom-call | tf_op jit(solution)/shard_map/attention_back/pallas_call | solution.py:1579
  491.6 8.1 %convolution_convert_fusion.4 = bf16[512,2048]{1,0:T(8,128)(2,1)} fusion(bf16[512,1536]{1,0:T(8,128)(2,1)} %attention_back.1, bf16[2048,1536]{1,0:T(8,128)(2,1)} %bitcast.216), kind=kOutput, calls=%fused_computation.28 | convolution fusion | flops 3222274048 | bytes 9961472 | tf_op jit(solution)/shard_map/dot_general | solution.py:1982
  501.7 64.7 %rows_last.1 = (bf16[2,64,2048]{2,1,0:T(8,128)(2,1)}, bf16[2,64,2048]{2,1,0:T(8,128)(2,1)}, f32[1,2048]{1,0:T(1,128)}, f32[256,2048]{1,0:T(8,128)}) custom-call(bf16[2,4,64,2048]{3,2,1,0:T(8,128)(2,1)} %bitcast.171, bf16[8,256,2048]{2,1,0:T(8,128)(2,1)} %bitcast.151, bf16[2,64,2048]{2,1,0:T(8,128)(2,1)} %dynamic-slice_bitcast_fusion.refs_2_.refs_5_, ...), custom_call_target="tpu_custom_call" | custom-call | tf_op jit(solution)/shard_map/rows_last/pallas_call | solution.py:1462
  572.4 59.7 %slot_grads.1.slot = bf16[8,64,2048]{2,1,0:T(8,128)(2,1)} custom-call(bf16[4,4,64,2048]{3,2,1,0:T(8,128)(2,1)} %select_select_fusion.part), custom_call_target="tpu_custom_call" | custom-call | tf_op jit(solution)/shard_map/slot_grads/pallas_call | solution.py:1098
  632.1 30.3 %pool_back.1 = (bf16[1024,512]{1,0:T(8,128)(2,1)}, f32[1024,128]{1,0:T(8,128)}, f32[64,256]{1,0:T(8,128)}, f32[64,2048]{1,0:T(8,128)}, bf16[256,2048]{1,0:T(8,128)(2,1)}) custom-call(bf16[8,64,2048]{2,1,0:T(8,128)(2,1)} %slot_grads.1.slot, bf16[256,2048]{1,0:T(8,128)(2,1)} %bitcast.159, bf16[8,256,1024]{2,1,0:T(8,128)(2,1)} %get-tuple-element.108.vision_low, ...), custom_call_target="tpu_custom_call" | custom-call | tf_op jit(solution)/shard_map/pool_back/pallas_call | solution.py:1713
  667.2 4.4 convolution_convert_fusion.3
  671.6 5.4 convolution_convert_fusion
  677.0 71.0 %sampler_scatter.1 = (bf16[8,32,512]{2,1,0:T(8,128)(2,1)}, f32[64,2048]{1,0:T(8,128)}, f32[256,1536]{1,0:T(8,128)}, f32[256,512]{1,0:T(8,128)}, f32[8,64,256]{2,...) custom-call(bf16[2,4,4,32,512]{4,3,2,1,0:T(8,128)(2,1)} %bitcast.178, bf16[4,64,2048]{2,1,0:T(8,128)(2,1)} %bitcast.179, ...), custom_call_target="tpu_custom_call" | custom-call | tf_op jit(solution)/shard_map/sampler_scatter/pallas_call | solution.py:1236
  (223 shorter events, 90.2 us)
Async XLA Ops:
  7.2 11.4 %copy-start = (bf16[64,2048]{1,0:T(8,128)(2,1)S(1)}, bf16[64,2048]{1,0:T(8,128)(2,1)}, u32[]{:S(2)}) copy-start(bf16[64,2048]{1,0:T(8,128)(2,1)} %param.37) | copy-start | bytes 786436
  7.2 15.4 %copy-start.20 = (bf16[256,512]{1,0:T(8,128)(2,1)S(1)}, bf16[256,512]{1,0:T(8,128)(2,1)}, u32[]{:S(2)}) copy-start(bf16[256,512]{1,0:T(8,128)(2,1)} %param.29) | copy-start | bytes 786436
  7.2 15.4 %copy-start.21 = (bf16[256,512]{1,0:T(8,128)(2,1)S(1)}, bf16[256,512]{1,0:T(8,128)(2,1)}, u32[]{:S(2)}) copy-start(bf16[256,512]{1,0:T(8,128)(2,1)} %param.28) | copy-start | bytes 786436
  7.2 15.4 %copy-start.22 = (bf16[256,512]{1,0:T(8,128)(2,1)S(1)}, bf16[256,512]{1,0:T(8,128)(2,1)}, u32[]{:S(2)}) copy-start(bf16[256,512]{1,0:T(8,128)(2,1)} %param.27) | copy-start | bytes 786436
  7.2 189.5 %all-gather.10.cloned.1.call-start = ((), (), s32[]{:S(2)}) async-start(), calls=%async_computation.4 | async-start | bytes 2621440 | tf_op jit(solution)/shard_map/all_gather | solution.py:1847
  20.3 77.3 %copy-start.13 = (bf16[2048,256]{1,0:T(8,128)(2,1)S(1)}, bf16[2048,256]{1,0:T(8,128)(2,1)}, u32[]{:S(2)}) copy-start(bf16[2048,256]{1,0:T(8,128)(2,1)} %param.32) | copy-start | bytes 3145732
  93.2 106.7 %all-gather.8.cloned.1.call-start = ((), (), s32[]{:S(2)}) async-start(), calls=%async_computation.3 | async-start | bytes 2621440 | tf_op jit(solution)/shard_map/all_gather | solution.py:1844
  93.9 225.1 %all-gather.6.cloned.1.call-start = ((), (), s32[]{:S(2)}) async-start(), calls=%async_computation.1 | async-start | bytes 9437184 | tf_op jit(solution)/shard_map/all_gather | solution.py:1846
  94.7 671.3 %reduce-scatter.2.cloned.1.call-start = ((), (), s32[]{:S(2)}) async-start(), calls=%async_computation.2 | async-start | bytes 2621440 | tf_op jit(solution)/shard_map/reduce_scatter | solution.py:1962
  124.2 71.9 %copy-start.27 = (s32[2,64]{1,0:T(2,128)S(1)}, s32[2,64]{1,0:T(2,128)}, u32[]{:S(2)}) copy-start(s32[2,64]{1,0:T(2,128)} %param.24) | copy-start | bytes 1540
  124.2 71.9 %copy-start.7 = (bf16[8,256,512]{2,1,0:T(8,128)(2,1)S(1)}, bf16[8,256,512]{2,1,0:T(8,128)(2,1)}, u32[]{:S(2)}) copy-start(bf16[8,256,512]{2,1,0:T(8,128)(2,1)} %get-tuple-element.89) | copy-start | bytes 6291460
  319.1 7.9 %copy-start.10 = (bf16[2,4,64,2048]{3,2,1,0:T(8,128)(2,1)S(1)}, bf16[2,4,64,2048]{3,2,1,0:T(8,128)(2,1)}, u32[]{:S(2)}) copy-start(bf16[2,4,64,2048]{3,2,1,0:T(8,128)(2,1)} %copy.114) | copy-start | bytes 6291460
  319.1 8.0 %copy-start.28 = (bf16[8,256,2048]{2,1,0:T(8,128)(2,1)S(1)}, bf16[8,256,2048]{2,1,0:T(8,128)(2,1)}, u32[]{:S(2)}) copy-start(bf16[8,256,2048]{2,1,0:T(8,128)(2,1)} %get-tuple-element.95) | copy-start | bytes 25165828
  327.0 15.8 %copy-start.1 = (f32[512,2048]{1,0:T(8,128)}, f32[512,2048]{1,0:T(8,128)S(1)}, u32[]{:S(2)}) copy-start(f32[512,2048]{1,0:T(8,128)S(1)} %fusion.25) | copy-start | bytes 12582916
  353.2 10.7 %copy-start.3 = (f32[512,2048]{1,0:T(8,128)S(1)}, f32[512,2048]{1,0:T(8,128)}, u32[]{:S(2)}) copy-start(f32[512,2048]{1,0:T(8,128)} %get-tuple-element.208) | copy-start | bytes 12582916
  353.2 10.7 %copy-start.11 = (bf16[2,4,64,2048]{3,2,1,0:T(8,128)(2,1)S(1)}, bf16[2,4,64,2048]{3,2,1,0:T(8,128)(2,1)}, u32[]{:S(2)}) copy-start(bf16[2,4,64,2048]{3,2,1,0:T(8,128)(2,1)} %copy.114) | copy-start | bytes 6291460
  363.9 7.1 copy-start.2
  363.9 7.1 copy-start.4
  363.9 7.1 copy-start.5
  491.6 8.8 %copy-start.26 = (f32[1,2048]{1,0:T(1,128)S(1)}, f32[1,2048]{1,0:T(1,128)}, u32[]{:S(2)}) copy-start(f32[1,2048]{1,0:T(1,128)} %get-tuple-element.99) | copy-start | bytes 24580
  632.1 35.1 %copy-start.14 = (f32[512,512]{1,0:T(8,128)S(1)}, f32[512,512]{1,0:T(8,128)}, u32[]{:S(2)}) copy-start(f32[512,512]{1,0:T(8,128)} %get-tuple-element.88) | copy-start | bytes 3145732
  677.0 73.0 %copy-start.8 = (f32[256,2048]{1,0:T(8,128)S(1)}, f32[256,2048]{1,0:T(8,128)}, u32[]{:S(2)}) copy-start(f32[256,2048]{1,0:T(8,128)} %get-tuple-element.120) | copy-start | bytes 6291460
  756.9 9.1 %copy-start.6 = (f32[2,64,2048]{2,1,0:T(8,128)S(1)}, f32[2,64,2048]{2,1,0:T(8,128)}, u32[]{:S(2)}) copy-start(f32[2,64,2048]{2,1,0:T(8,128)} %get-tuple-element.91.refs_2_) | copy-start | bytes 3145732
  758.7 9.3 %copy-start.16 = (bf16[2,64,2048]{2,1,0:T(8,128)(2,1)S(1)}, bf16[2,64,2048]{2,1,0:T(8,128)(2,1)}, u32[]{:S(2)}) copy-start(bf16[2,64,2048]{2,1,0:T(8,128)(2,1)} %get-tuple-element.257) | copy-start | bytes 1572868
  (11 other events, 53.1 us)
Sparse Core Ops, SparseCore 0:
  93.3 44.3 all-gather.9
  139.3 52.7 all-gather.7
  194.0 56.5 all-gather.5
  475.0 43.5 reduce-scatter.1

commit v3 on v2

--- a/solution.py
+++ b/solution.py
@@ -794,7 +794,10 @@
         for k in (1, 2):
             self.side(chunk, k).wait_recv()
             total = total + self.land[k, self.span(chunk)].astype(jnp.float32)
-        self.out[self.span(chunk)] = total
+        at = 0
+        for out in self.out:
+            out[self.span(chunk)] = total[:, at : at + out.shape[-1]]
+            at += out.shape[-1]
 
     def timed(self, step, lag, start=0):
         parts = []
@@ -807,7 +810,7 @@
 
 
 def sampler_gather_kernel(
-    n_mp, feat, key_value, pack, rq_part, slots, wout, latents, qkv, turned_wo,
+    n_mp, feat, key_value, pack, rq_part, slots, wout, latents, query, key, value, turned_wo,
     feats_o, kv_o, pack_o, slots_o, rq_o, wout_o, latents_o, qkv_o, turned_wo_o,
     rq_plane, rq_line, send, recv, here,
 ):
@@ -823,9 +826,12 @@
         pltpu.make_async_copy(feat, feats_o.at[p], here.at[3]),
         pltpu.make_async_copy(wout, wout_o.at[z], here.at[4]),
         pltpu.make_async_copy(latents, latents_o.at[z], here.at[5]),
-        pltpu.make_async_copy(qkv, qkv_o.at[p], here.at[6]),
-        pltpu.make_async_copy(turned_wo, turned_wo_o.at[p], here.at[7]),
+        pltpu.make_async_copy(turned_wo, turned_wo_o.at[p], here.at[6]),
     ]
+    third = query.shape[1]
+    for i, weight in enumerate((query, key, value)):
+        place = qkv_o.at[p, :, pl.ds(i * third, third)]
+        own.append(pltpu.make_async_copy(weight, place, here.at[7 + i]))
     for copy in own:
         copy.start()
     others = [(spot.device(flip), spot.place(flip)) for flip in FLIPS]
@@ -902,7 +908,7 @@
     wire.finish()
 
 
-def call_sampler_gather(n_mp, feat, key_value, pack, rq_part, slots, wout, latents, qkv, turned_wo):
+def call_sampler_gather(n_mp, feat, key_value, pack, rq_part, slots, wout, latents, *weights):
     shape = jax.ShapeDtypeStruct
     rows_v, width_v = feat.shape[1:]
     bf = jnp.bfloat16
@@ -914,8 +920,8 @@
         shape(rq_part.shape[1:], bf),
         shape((n_mp,) + wout.shape, bf),
         shape((n_mp,) + latents.shape, bf),
-        shape((8,) + qkv.shape, bf),
-        shape((8,) + turned_wo.shape, bf),
+        shape((8, weights[0].shape[0], 3 * weights[0].shape[1]), bf),
+        shape((8,) + weights[3].shape, bf),
     )
     wires = 7 * 3 + 3 * 8 + 5 * 2 * (n_mp - 1) + n_mp
     anywhere = pl.BlockSpec(memory_space=pl.ANY)
@@ -924,17 +930,17 @@
         partial(sampler_gather_kernel, n_mp),
         name="sampler_gather",
         out_shape=outs,
-        in_specs=[near] * 9,
+        in_specs=[near] * 11,
         out_specs=(anywhere,) * 4 + (near,) + (anywhere,) * 4,
         scratch_shapes=[
             VMEM(rq_part.shape, bf),
             VMEM((n_mp,) + rq_part.shape[1:], bf),
             pltpu.SemaphoreType.DMA((wires,)),
             pltpu.SemaphoreType.DMA((wires,)),
-            pltpu.SemaphoreType.DMA((8,)),
+            pltpu.SemaphoreType.DMA((10,)),
         ],
         compiler_params=pltpu.CompilerParams(collective_id=1, has_side_effects=True, vmem_limit_bytes=BIG),
-    )(feat[0], key_value, pack, rq_part, slots, wout, latents, qkv, turned_wo)
+    )(feat[0], key_value, pack, rq_part, slots, wout, latents, *weights)
 
 
 def table_kernel(n_mp, part, table, near_c, half_x, half_y, full_x, full_y, sums, emb, send, recv, here):
@@ -1118,7 +1124,7 @@
 
 def sampler_scatter_kernel(
     n_mp, dkv, dwout, side_1, side_2, drq, resid, gains, local_gains,
-    dkv_o, dwout_o, sum_1, sum_2, drq_o, resid_o, gains_o,
+    dkv_o, dwout_o, sum_q, sum_k, sum_v, sum_2, drq_o, resid_o, gains_o,
     kv_land, kv_low, w_land, rq_line, resid_line, gain_line, gain_plane, gain_low,
     near_1, land_1, near_2, land_2, send, recv,
 ):
@@ -1130,6 +1136,7 @@
     resid_line[z] = resid[z]
     gain_line[z] = gains[z]
     others = [(spot.device(flip), spot.place(flip)) for flip in FLIPS]
+    sums = (sum_q, sum_k, sum_v)
     per_line = 2 * n_mp
     half_rows = dwout.shape[1] // 2
 
@@ -1209,9 +1216,9 @@
         steps.add(lines[1].settle_time(k), own_kv)
         for h in range(2):
             steps.add(lines[2 + h].settle_time(k), partial(own_w, h))
-        first = PlaneScatter(wire, spot, side_1, near_1, land_1, sum_1, SIDE)
-        second = PlaneScatter(wire, spot, side_2, near_2, land_2, sum_2, 2)
-        for step, c, time in first.timed(2.5, 2.5, 1) + second.timed(1.5, 2, 12):
+        first = PlaneScatter(wire, spot, side_1, near_1, land_1, sums, SIDE)
+        second = PlaneScatter(wire, spot, side_2, near_2, land_2, (sum_2,), 2)
+        for step, c, time in first.timed(3, 4, 0) + second.timed(1.5, 3, 11):
             steps.add(time + 0.25, partial(step, c))
         steps.run()
         for moves in sent:
@@ -1239,14 +1246,14 @@
         out_shape=(
             shape((8, rows, cols), bf),
             shape(dwout.shape[1:], f32),
-            shape(sides[0].shape[1:], f32),
+            *(shape((sides[0].shape[1], sides[0].shape[2] // 3), f32) for _ in range(3)),
             shape(sides[1].shape[1:], f32),
             shape((8,) + drq.shape, f32),
             shape(resid.shape[1:], f32),
             shape(gains.shape[2:], f32),
         ),
         in_specs=[near] * 8,
-        out_specs=(near,) * 7,
+        out_specs=(near,) * 9,
         scratch_shapes=[
             VMEM((2, 2, n_mp, 4, rows, cols), bf),
             VMEM((8, rows, cols), bf),
@@ -1414,7 +1421,7 @@
             parts = [(plane.begin, 0), (plane.middle, 5), (plane.end, 9), (plane.core, 12)]
             parts = [(step, c, late + c * SIDE_STEP) for step, late in parts for c in range(SIDE)]
         else:
-            plane = PlaneScatter(wire, spot, side, *room, side_sum, SIDE)
+            plane = PlaneScatter(wire, spot, side, *room, (side_sum,), SIDE)
             parts = plane.timed(SIDE_STEP, 4)
         for step, c, time in parts:
             steps.add(time + 0.5, partial(step, c))
@@ -1643,7 +1650,7 @@
 
 def pool_back_kernel(
     slot, wout, vision_low, keys_values, query, weights, pooled,
-    d_weights, d_products, d_query, residual, d_wout, total, d_kv, w_total,
+    d_weights, d_products, d_query, residual, d_wout, d_kv,
 ):
     f32, bf = jnp.float32, jnp.bfloat16
     i = pl.program_id(0)
@@ -1654,14 +1661,11 @@
 
     @pl.when(i == 0)
     def _():
-        total[...] = jnp.zeros_like(total)
-        w_total[...] = jnp.zeros_like(w_total)
         d_query[...] = jnp.zeros_like(d_query)
         residual[...] = jnp.zeros_like(residual)
 
-    above = slot[0]
+    above = slot[i]
     residual[...] += above.astype(f32)
-    w_total[...] += lax.dot_general(pooled[0], above, rows_in, preferred_element_type=f32)
     d_pooled = lax.dot_general(above, wout[...], lanes_in, preferred_element_type=f32).astype(bf)
     lane = lax.broadcasted_iota(jnp.int32, (query.shape[0], LANE), 1)
     patch_lane = lax.broadcasted_iota(jnp.int32, (keys_values.shape[1], LANE), 1)
@@ -1685,17 +1689,17 @@
             dk = k if side == 0 else jnp.where(patch_mine, k, dk)
             dv = v if side == 0 else jnp.where(patch_mine, v, dv)
         d_query[:, at : at + LANE] += dq.astype(bf).astype(f32)
-        d_kv[:, at : at + LANE] = dk.astype(bf)
-        d_kv[:, cols + at : cols + at + LANE] = dv.astype(bf)
-    total[...] += lax.dot_general(vision_low[0], d_kv[...], rows_in, preferred_element_type=f32)
+        d_kv[i, :, at : at + LANE] = dk.astype(bf)
+        d_kv[i, :, cols + at : cols + at + LANE] = dv.astype(bf)
 
     @pl.when(i == pl.num_programs(0) - 1)
     def _():
-        value = total[...]
+        flat = lambda array: array[...].reshape(-1, array.shape[-1])
+        value = lax.dot_general(flat(vision_low), flat(d_kv), rows_in, preferred_element_type=f32)
         d_weights[...] = value.astype(bf)
         products = jnp.sum(value * weights[...].astype(f32), -1, keepdims=True)
         d_products[...] = jnp.broadcast_to(products, d_products.shape)
-        d_wout[...] = w_total[...].astype(bf)
+        d_wout[...] = lax.dot_general(flat(pooled), flat(slot), rows_in, preferred_element_type=f32).astype(bf)
 
 
 def call_pool_back(slot, wout, vision_low, keys_values, query, weights, pooled):
@@ -1716,13 +1720,11 @@
         grid=(images,),
         out_shape=outs,
         in_specs=[
-            one(slot), whole(wout), one(vision_low), one(keys_values), whole(query), whole(weights), one(pooled)
+            whole(slot), whole(wout), whole(vision_low), one(keys_values), whole(query), whole(weights), whole(pooled)
         ],
         out_specs=tuple(whole(out) for out in outs),
         scratch_shapes=[
-            VMEM(weights.shape, f32),
-            VMEM((keys_values.shape[1], weights.shape[1]), bf),
-            VMEM(wout.shape, f32),
+            VMEM(keys_values.shape, bf),
         ],
         compiler_params=pltpu.CompilerParams(vmem_limit_bytes=BIG),
     )(slot, wout, vision_low, keys_values, query, weights, pooled)
@@ -1738,11 +1740,9 @@
 
 
 def call_entry(slot, table, tokens, gain):
-    n_mp, batch, rows, width = tokens.shape
-    blocks = n_mp * batch
+    blocks, rows, width = tokens.shape
     one = pl.BlockSpec((1, rows, width), lambda i, slot: (i, 0, 0))
     shape = jax.ShapeDtypeStruct((blocks, rows, width), jnp.bfloat16)
-    tokens = tokens.reshape(blocks, rows, width)
     return pl.pallas_call(
         entry_kernel,
         name="entry",
@@ -1751,7 +1751,7 @@
             grid=(blocks,),
             in_specs=[
                 pl.BlockSpec((1, rows, width), lambda i, slot: (jnp.maximum(slot[i], 0), 0, 0)),
-                pl.BlockSpec((1, rows, width), lambda i, slot: (lax.rem(i, n_mp) * batch + i // n_mp, 0, 0)),
+                pl.BlockSpec((1, rows, width), lambda i, slot: (i, 0, 0)),
                 pl.BlockSpec((1, width), lambda i, slot: (0, 0)),
             ],
             out_specs=(one, one),
@@ -1836,15 +1836,15 @@
         first_slots,
         sampler_output,
         latents.reshape(-1, LANE),
-        jnp.concatenate([query_weight, key_weight, value_weight], 1),
+        query_weight,
+        key_weight,
+        value_weight,
         output_weight.T,
     )
     qkv_full = qkv_full.reshape(width, -1)
     wo_turned = wo_turned.reshape(width, -1)
-    tokens_all = lax.all_gather(tokens, MP, axis=0)
-    up_sent, out_grad_sent = after_those((tokens_all, slots), (up_weight, out_grad))
-    up_full = lax.all_gather(up_sent, (DP, IMG), axis=0, tiled=True)
-    grads_all = lax.all_gather(out_grad_sent, MP, axis=0)
+    tokens_all = lax.all_gather(tokens, MP, axis=0).transpose(1, 0, 2, 3).reshape(batch * n_mp, block, width)
+    up_full = lax.all_gather(up_weight, (DP, IMG), axis=0, tiled=True)
     own_cols = latents.shape[1]
     column = lambda n, at: jnp.arange(n) == at
     here = (column(2, y)[:, None, None] & column(4, img)[None, None, :])[None, ..., None]
@@ -1869,6 +1869,7 @@
     kv_rows = kv_all.reshape(-1, 2 * cols)
     wout_rows = wout_all.reshape(cols, width)
     vision_low, keys_values, pooled, branch = call_pool(feats, vision_gain, kv_rows, rq, wout_rows, placed)
+    grads_all = lax.all_gather(after_those(feats, out_grad), MP, axis=0)
     table = call_table(n_mp, branch).reshape(-1, LAT, width)
 
     block_image = jnp.where(slot_first >= 0, slot_first // LAT, -1)
@@ -1959,10 +1960,6 @@
         entry,
         turned,
     )
-    result_sum = lax.psum_scatter(
-        after_those(d_mgain, result_part), MP, scatter_dimension=1, tiled=False
-    )
-    result = after + result_sum.astype(f32)
     after_rows = after_rows.reshape(rows, width)
     d_mixed = dot(after_rows, wo_turned)
     scaled = d_mixed * attention_gain
@@ -1993,6 +1990,10 @@
     for s in range(batch):
         spread = jnp.where(each == own_image[s], entry_low[s][None], spread)
     slot_low = call_slot(n_mp, spread.reshape(n_mp, 4, block, width))
+    result_sum = lax.psum_scatter(
+        after_those(slot_low, result_part), MP, scatter_dimension=1, tiled=False
+    )
+    result = after + result_sum.astype(f32)
     d_kv_weight, d_products, d_rq, residual, d_wout = call_pool_back(
         slot_low, wout_rows, vision_low, keys_values, rq, kv_rows, pooled
     )
@@ -2011,7 +2012,7 @@
     residual = lax.dynamic_index_in_dim(residual.reshape(LAT, 2, n_mp, 4, own_cols), y, 1, keepdims=False)
     residual = lax.dynamic_index_in_dim(residual, img, 2, keepdims=False)
     residual = residual.transpose(1, 0, 2).reshape(n_mp, LAT * own_cols // LANE, LANE)
-    d_kv_own, d_wout_own, d_qkv_own, d_wo_own, d_rq_all, residual, gains_own = call_sampler_scatter(
+    d_kv_own, d_wout_own, d_wq_own, d_wk_own, d_wv_own, d_wo_own, d_rq_all, residual, gains_own = call_sampler_scatter(
         n_mp,
         d_kv_weight.reshape(2, n_mp, 4, -1, 2 * cols),
         d_wout.reshape(n_mp, own_heads * HD, width),
@@ -2031,13 +2032,12 @@
     d_latents = residual.reshape(LAT, own_cols) + exact(d_rq_all, sampler_query.astype(f32).T)
     gains_own = gains_own.reshape(-1)
     parts = jnp.split(gains_own, (n_vision, n_vision + n_row, n_vision + 2 * n_row, half, half + n_att, half + n_att + n_hid))
-    third = local_width
     return (
         result.astype(bf),
         tokens_grad,
-        d_qkv_own[:, :third],
-        d_qkv_own[:, third : 2 * third],
-        d_qkv_own[:, 2 * third :],
+        d_wq_own,
+        d_wk_own,
+        d_wv_own,
         d_wo_own.T,
         d_up_own,
         d_down_own.T,

time: 785 us -> 770 us (0.981)
  Pallas kernels: 584 us -> 573 us
    pallas_call x3, Pallas kernels: 228 us -> 214 us  [call_rows(): pl.pallas_call(partial(rows_kernel, n_mp, kind), name=f'rows_{kind}', out...]
    pallas_call x1, Pallas kernels: 69.5 us -> 79.3 us  [call_sampler_gather(): pl.pallas_call(partial(sampler_gather_kernel, n_mp), name='sampler_gather...]
  transfers between devices with their start and end apart: 4 -> 4, of which waited for: 0 -> 0; matrix products, arithmetic and copies ran while one was open for 11% -> 11% of each run, Pallas kernels for 55% -> 46%
where the time goes in v3:
time: 770 us; the launch traced here: 766 us
  Pallas kernels  573 us (74%)
  matrix products  96.1 us (12%)
  local copies, waits for them, and re-layouts  60.5 us (8%)
  other arithmetic  18.8 us (2%)
  between operations  14.8 us (2%)
    pallas_call x3, Pallas kernels, call_rows(): pl.pallas_call(partial(rows_kernel, n_mp, kind), name=f'rows_{kind}', out...  214 us
    pallas_call x1, Pallas kernels, call_sampler_gather(): pl.pallas_call(partial(sampler_gather_kernel, n_mp), name='sampler_gather...  79.3 us
    pallas_call x1, Pallas kernels, call_sampler_scatter(): pl.pallas_call(partial(sampler_scatter_kernel, n_mp), name='sampler_scatt...  70.9 us
    pallas_call x1, Pallas kernels, call_table(): pl.pallas_call(partial(table_kernel, n_mp), name='table', out_shape=jax.S...  67.5 us
    pallas_call x1, Pallas kernels, call_slot(): pl.pallas_call(partial(slot_kernel, n_mp), name='slot_grads', out_shape=j...  57.3 us
    pallas_call x1, Pallas kernels, call_pool_back(): pl.pallas_call(pool_back_kernel, name='pool_back', grid=(images,), out_sh...  28.7 us
    pallas_call x1, Pallas kernels, call_pool(): pl.pallas_call(pool_kernel, name='pool', grid=(images,), out_shape=outs,...  19.7 us
    dot_general x1, matrix products, plane_local(): d_hidden = dot(grad_rows, down_turned)  15.9 us
  transfers between devices with their start and end apart: 4, of which 0 were waited for; matrix products, arithmetic and copies ran while one was open for 11% of the time, Pallas kernels for 46%

profile of v3, /device:TPU:8, one launch (start us, length us, event | category | flops | bytes accessed | tf_op | source)
XLA Modules:
  0.0 765.5 jit_solution(2754515583393605382)
XLA Ops:
  20.7 79.3 %sampler_gather.1 = (bf16[8,256,1024]{2,1,0:T(8,128)(2,1)}, bf16[2,4,4,32,512]{4,3,2,1,0:T(8,128)(2,1)}, bf16[8,4,16,128]{3,2,1,0:T(8,128)(2,1)}, s32[4,8,128]{2...) custom-call(bf16[256,1024]{1,0:T(8,128)(2,1)} %bitcast.191, ...), custom_call_target="tpu_custom_call" | custom-call | tf_op jit(solution)/shard_map/sampler_gather/pallas_call | solution.py:929
  110.6 19.7 %pool.1 = (bf16[8,256,1024]{2,1,0:T(8,128)(2,1)}, bf16[8,256,512]{2,1,0:T(8,128)(2,1)}, bf16[8,64,256]{2,1,0:T(8,128)(2,1)}, bf16[8,64,2048]{2,1,0:T(8,128)(2,1)}) custom-call(bf16[8,256,1024]{2,1,0:T(8,128)(2,1)} %get-tuple-element.80.feats, f32[1,1024]{1,0:T(1,128)} %reshape.454.gain, bf16[1024,512]{1,0:T(8,128)(2,1)} %bitcast.161, ...), custom_call_target="tpu_custom_call" | custom-call | tf_op jit(solution)/shard_map/pool/pallas_call | solution.py:1640
  130.2 67.5 %table.1 = bf16[4,4,64,2048]{3,2,1,0:T(8,128)(2,1)} custom-call(bf16[2,2,2,64,2048]{4,3,2,1,0:T(8,128)(2,1)} %bitcast.165), custom_call_target="tpu_custom_call" | custom-call | tf_op jit(solution)/shard_map/table/pallas_call | solution.py:1033
  206.9 7.7 %entry.1 = (bf16[8,64,2048]{2,1,0:T(8,128)(2,1)}, bf16[8,64,2048]{2,1,0:T(8,128)(2,1)}) custom-call(s32[8]{0:T(128)} %reshape.452.slot, bf16[16,64,2048]{2,1,0:T(8,128)(2,1)} %bitcast.153, bf16[8,64,2048]{2,1,0:T(8,128)(2,1)} %bitcast.156, f32[1,2048]{1,0:T(1,128)} %reshape.460.gain.refs_4_), custom_call_target="tpu_custom_call" | custom-call | tf_op jit(solution)/shard_map/entry/pallas_call | solution.py:1746
  214.5 8.7 %fusion.23.proj = f32[512,1536]{1,0:T(8,128)} fusion(bf16[512,2048]{1,0:T(8,128)(2,1)} %bitcast.223, bf16[2048,1536]{1,0:T(8,128)(2,1)} %bitcast.221), kind=kOutput, calls=%fused_computation.114 | convolution fusion | flops 3221225472 | bytes 11534336 | tf_op jit(solution)/shard_map/dot_general | solution.py:1884
  223.2 8.0 %attention.1 = (bf16[512,1536]{1,0:T(8,128)(2,1)}, f32[512,512]{1,0:T(8,128)}) custom-call(f32[512,1536]{1,0:T(8,128)} %fusion.23.proj, f32[4,256,128]{2,1,0:T(8,128)} %constant.199.clone.tables), custom_call_target="tpu_custom_call" | custom-call | tf_op jit(solution)/shard_map/attention/pallas_call | solution.py:1531
  239.6 73.1 %rows_forward.1 = (f32[2,64,2048]{2,1,0:T(8,128)}, bf16[2,4,64,2048]{3,2,1,0:T(8,128)(2,1)}, f32[8,2560]{1,0:T(8,128)}, bf16[8,256,2048]{2,1,0:T(8,128)(2,1)}) custom-call(bf16[2,4,64,2048]{3,2,1,0:T(8,128)(2,1)} %bitcast.166, bf16[256,2048]{1,0:T(8,128)(2,1)} %bitcast.158, bf16[2,64,2048]{2,1,0:T(8,128)(2,1)} %dynamic-slice_bitcast_fusion.refs_2_.refs_5_, ...), custom_call_target="tpu_custom_call" | custom-call | tf_op jit(solution)/shard_map/rows_forward/pallas_call | solution.py:1469
  315.3 7.9 %fusion.24 = f32[512,2048]{1,0:T(8,128)S(1)} fusion(bf16[512,2048]{1,0:T(8,128)(2,1)} %bitcast.227, bf16[2048,2048]{1,0:T(8,128)(2,1)} %all-gather.6.cloned.1.call-done), kind=kOutput, calls=%fused_computation.115 | convolution fusion | flops 4294967296 | bytes 14680064 | tf_op jit(solution)/shard_map/dot_general | solution.py:1914
  323.2 15.9 %multiply_reduce_fusion.1 = (f32[512]{0:T(512)S(1)}, f32[512]{0:T(512)S(1)}, f32[512]{0:T(512)S(1)}, f32[512]{0:T(512)S(1)}, f32[512,2048]{1,0:T(8,128)}, /*index=5*/f32[512,2048]{1,0:T(8,128)}, f32[512,2048]{1,0:T(8,128)}) fusion(f32[2048]{0:T(1024)S(1)} %mul.174, f32[512,2048]{1,0:T(8,128)S(1)} %fusion.24, bf16[512,2048]{1,0:T(8,128)(2,1)S(1)} %bitcast.173, ...), kind=kOutput, calls=%fused_computation.10 | convolution fusion | flops 4369414144 | bytes 27279360 | tf_op jit(solution)/shard_map/dot_general | solution.py:1918
  339.7 9.3 %line_sum_8.1 = f32[8,512]{1,0:T(8,128)} custom-call(f32[8,512]{1,0:T(8,128)} %concatenate.27.own), custom_call_target="tpu_custom_call" | custom-call | tf_op jit(solution)/shard_map/line_sum_8/pallas_call | solution.py:1296
  350.0 10.7 %convolution_convert_fusion.4 = bf16[512,2048]{1,0:T(8,128)(2,1)} fusion(bf16[2048,2048]{1,0:T(8,128)(2,1)} %bitcast.219, f32[512,2048]{1,0:T(8,128)} %get-tuple-element.210, f32[512]{0:T(512)S(1)} %bitcast.202, f32[512]{0:T(512)S(1)} %get-tuple-element.228, f32[2048]{0:T(1024)S(1)} %mul.174), kind=kOutput, calls=%fused_computation.28 | convolution fusion | flops 4300210176 | bytes 14692352 | tf_op jit(solution)/shard_map/dot_general | solution.py:1934
  360.6 7.2 convolution_convert_fusion.2
  367.9 5.0 multiply_reduce_fusion
  372.9 6.8 convolution_convert_fusion.1
  379.7 9.3 %convolution_convert_fusion.6 = bf16[512,2048]{1,0:T(8,128)(2,1)} fusion(bf16[512,2048]{1,0:T(8,128)(2,1)S(1)} %get-tuple-element.213, bf16[2048,2048]{1,0:T(8,128)(2,1)} %all-gather.6.cloned.1.call-done), kind=kOutput, calls=%fused_computation.30 | convolution fusion | flops 4296015872 | bytes 12582912 | tf_op jit(solution)/shard_map/dot_general | solution.py:1941
  389.0 78.6 %rows_middle.1 = (f32[2,64,2048]{2,1,0:T(8,128)}, f32[1,2048]{1,0:T(1,128)}, bf16[2,4,64,2048]{3,2,1,0:T(8,128)(2,1)}, f32[4,8,128]{2,1,0:T(8,128)}, f32[256,2048]{1,0:T(8,128)}) custom-call(bf16[2,4,64,2048]{3,2,1,0:T(8,128)(2,1)} %bitcast.178, bf16[8,256,2048]{2,1,0:T(8,128)(2,1)} %bitcast.154, f32[2,64,2048]{2,1,0:T(8,128)} %get-tuple-element.92.refs_2_, ...), custom_call_target="tpu_custom_call" | custom-call | tf_op jit(solution)/shard_map/rows_middle/pallas_call | solution.py:1469
  472.8 11.1 %attention_back.1 = bf16[512,1536]{1,0:T(8,128)(2,1)} custom-call(bf16[512,1536]{1,0:T(8,128)(2,1)} %get-tuple-element.93.low, bf16[512,512]{1,0:T(8,128)(2,1)} %get-tuple-element.215.grad, f32[4,256,128]{2,1,0:T(8,128)} %constant.199.clone.tables), custom_call_target="tpu_custom_call" | custom-call | tf_op jit(solution)/shard_map/attention_back/pallas_call | solution.py:1586
  483.9 8.1 %convolution_convert_fusion.5 = bf16[512,2048]{1,0:T(8,128)(2,1)} fusion(bf16[512,1536]{1,0:T(8,128)(2,1)} %attention_back.1, bf16[2048,1536]{1,0:T(8,128)(2,1)} %bitcast.222), kind=kOutput, calls=%fused_computation.29 | convolution fusion | flops 3222274048 | bytes 9961472 | tf_op jit(solution)/shard_map/dot_general | solution.py:1979
  492.7 62.3 %rows_last.1 = (bf16[2,64,2048]{2,1,0:T(8,128)(2,1)}, bf16[2,64,2048]{2,1,0:T(8,128)(2,1)}, f32[1,2048]{1,0:T(1,128)}, f32[256,2048]{1,0:T(8,128)}) custom-call(bf16[2,4,64,2048]{3,2,1,0:T(8,128)(2,1)} %bitcast.179, bf16[8,256,2048]{2,1,0:T(8,128)(2,1)} %bitcast.155, bf16[2,64,2048]{2,1,0:T(8,128)(2,1)} %dynamic-slice_bitcast_fusion.refs_2_.refs_5_, ...), custom_call_target="tpu_custom_call" | custom-call | tf_op jit(solution)/shard_map/rows_last/pallas_call | solution.py:1469
  558.6 57.3 %slot_grads.1.slot = bf16[8,64,2048]{2,1,0:T(8,128)(2,1)} custom-call(bf16[4,4,64,2048]{3,2,1,0:T(8,128)(2,1)} %select_select_fusion.part), custom_call_target="tpu_custom_call" | custom-call | tf_op jit(solution)/shard_map/slot_grads/pallas_call | solution.py:1104
  620.6 28.7 %pool_back.1 = (bf16[1024,512]{1,0:T(8,128)(2,1)}, f32[1024,128]{1,0:T(8,128)}, f32[64,256]{1,0:T(8,128)}, f32[64,2048]{1,0:T(8,128)}, bf16[256,2048]{1,0:T(8,128)(2,1)}) custom-call(bf16[8,64,2048]{2,1,0:T(8,128)(2,1)} %slot_grads.1.slot, bf16[256,2048]{1,0:T(8,128)(2,1)} %bitcast.164, bf16[8,256,1024]{2,1,0:T(8,128)(2,1)} %get-tuple-element.107.vision_low, ...), custom_call_target="tpu_custom_call" | custom-call | tf_op jit(solution)/shard_map/pool_back/pallas_call | solution.py:1717
  654.1 4.4 convolution_convert_fusion.3
  658.5 5.4 convolution_convert_fusion
  663.9 70.9 %sampler_scatter.1 = (bf16[8,32,512]{2,1,0:T(8,128)(2,1)}, f32[64,2048]{1,0:T(8,128)}, f32[256,512]{1,0:T(8,128)}, f32[256,512]{1,0:T(8,128)}, f32[256,512]{1,0:...) custom-call(bf16[2,4,4,32,512]{4,3,2,1,0:T(8,128)(2,1)} %bitcast.184, ...), custom_call_target="tpu_custom_call" | custom-call | tf_op jit(solution)/shard_map/sampler_scatter/pallas_call | solution.py:1243
  (233 shorter events, 88.2 us)
Async XLA Ops:
  7.2 8.6 %copy-start = (bf16[64,2048]{1,0:T(8,128)(2,1)S(1)}, bf16[64,2048]{1,0:T(8,128)(2,1)}, u32[]{:S(2)}) copy-start(bf16[64,2048]{1,0:T(8,128)(2,1)} %param.37) | copy-start | bytes 786436
  7.2 11.4 %copy-start.28 = (s32[2,64]{1,0:T(2,128)S(1)}, s32[2,64]{1,0:T(2,128)}, u32[]{:S(2)}) copy-start(s32[2,64]{1,0:T(2,128)} %param.24) | copy-start | bytes 1540
  7.2 12.1 %copy-start.29 = (bf16[32]{0:T(256)(128)(2,1)S(1)}, bf16[32]{0:T(256)(128)(2,1)}, u32[]{:S(2)}) copy-start(bf16[32]{0:T(256)(128)(2,1)} %param.42) | copy-start | bytes 196
  7.2 12.1 %copy-start.31 = (bf16[64]{0:T(256)(128)(2,1)S(1)}, bf16[64]{0:T(256)(128)(2,1)}, u32[]{:S(2)}) copy-start(bf16[64]{0:T(256)(128)(2,1)} %param.35) | copy-start | bytes 388
  7.2 12.1 %copy-start.30 = (bf16[64]{0:T(256)(128)(2,1)S(1)}, bf16[64]{0:T(256)(128)(2,1)}, u32[]{:S(2)}) copy-start(bf16[64]{0:T(256)(128)(2,1)} %param.33) | copy-start | bytes 388
  7.2 193.1 %all-gather.8.cloned.1.call-start = ((), (), s32[]{:S(2)}) async-start(), calls=%async_computation.3 | async-start | bytes 2621440 | tf_op jit(solution)/shard_map/all_gather | solution.py:1846
  8.0 195.6 %all-gather.10.cloned.1.call-start = ((), (), s32[]{:S(2)}) async-start(), calls=%async_computation.4 | async-start | bytes 2621440 | tf_op jit(solution)/shard_map/all_gather | solution.py:1872
  15.8 87.2 %copy-start.14 = (bf16[2048,256]{1,0:T(8,128)(2,1)S(1)}, bf16[2048,256]{1,0:T(8,128)(2,1)}, u32[]{:S(2)}) copy-start(bf16[2048,256]{1,0:T(8,128)(2,1)} %param.32) | copy-start | bytes 3145732
  100.0 215.2 %all-gather.6.cloned.1.call-start = ((), (), s32[]{:S(2)}) async-start(), calls=%async_computation.1 | async-start | bytes 9437184 | tf_op jit(solution)/shard_map/all_gather | solution.py:1847
  100.8 649.5 %reduce-scatter.2.cloned.1.call-start = ((), (), s32[]{:S(2)}) async-start(), calls=%async_computation.2 | async-start | bytes 2621440 | tf_op jit(solution)/shard_map/reduce_scatter | solution.py:1993
  130.2 69.5 %copy-start.7 = (bf16[8,256,512]{2,1,0:T(8,128)(2,1)S(1)}, bf16[8,256,512]{2,1,0:T(8,128)(2,1)}, u32[]{:S(2)}) copy-start(bf16[8,256,512]{2,1,0:T(8,128)(2,1)} %get-tuple-element.90) | copy-start | bytes 6291460
  315.3 7.9 %copy-start.10 = (bf16[2,4,64,2048]{3,2,1,0:T(8,128)(2,1)S(1)}, bf16[2,4,64,2048]{3,2,1,0:T(8,128)(2,1)}, u32[]{:S(2)}) copy-start(bf16[2,4,64,2048]{3,2,1,0:T(8,128)(2,1)} %copy.120) | copy-start | bytes 6291460
  315.3 8.0 %copy-start.32 = (bf16[8,256,2048]{2,1,0:T(8,128)(2,1)S(1)}, bf16[8,256,2048]{2,1,0:T(8,128)(2,1)}, u32[]{:S(2)}) copy-start(bf16[8,256,2048]{2,1,0:T(8,128)(2,1)} %get-tuple-element.97) | copy-start | bytes 25165828
  323.2 15.9 %copy-start.1 = (f32[512,2048]{1,0:T(8,128)}, f32[512,2048]{1,0:T(8,128)S(1)}, u32[]{:S(2)}) copy-start(f32[512,2048]{1,0:T(8,128)S(1)} %fusion.24) | copy-start | bytes 12582916
  349.9 10.7 %copy-start.3 = (f32[512,2048]{1,0:T(8,128)S(1)}, f32[512,2048]{1,0:T(8,128)}, u32[]{:S(2)}) copy-start(f32[512,2048]{1,0:T(8,128)} %get-tuple-element.210) | copy-start | bytes 12582916
  349.9 10.7 %copy-start.11 = (bf16[2,4,64,2048]{3,2,1,0:T(8,128)(2,1)S(1)}, bf16[2,4,64,2048]{3,2,1,0:T(8,128)(2,1)}, u32[]{:S(2)}) copy-start(bf16[2,4,64,2048]{3,2,1,0:T(8,128)(2,1)} %copy.120) | copy-start | bytes 6291460
  360.6 7.3 copy-start.2
  558.6 57.3 %copy-start.12 = (bf16[512,2048]{1,0:T(8,128)(2,1)S(1)}, bf16[512,2048]{1,0:T(8,128)(2,1)}, u32[]{:S(2)}) copy-start(bf16[512,2048]{1,0:T(8,128)(2,1)} %convolution_convert_fusion.4) | copy-start | bytes 6291460
  620.6 33.4 %copy-start.15 = (f32[512,512]{1,0:T(8,128)S(1)}, f32[512,512]{1,0:T(8,128)}, u32[]{:S(2)}) copy-start(f32[512,512]{1,0:T(8,128)} %get-tuple-element.89) | copy-start | bytes 3145732
  663.9 73.0 %copy-start.9 = (f32[256,2048]{1,0:T(8,128)S(1)}, f32[256,2048]{1,0:T(8,128)}, u32[]{:S(2)}) copy-start(f32[256,2048]{1,0:T(8,128)} %get-tuple-element.122) | copy-start | bytes 6291460
  742.9 7.4 copy-start.6
  743.7 8.6 %copy-start.17 = (bf16[2,64,2048]{2,1,0:T(8,128)(2,1)S(1)}, bf16[2,64,2048]{2,1,0:T(8,128)(2,1)}, u32[]{:S(2)}) copy-start(bf16[2,64,2048]{2,1,0:T(8,128)(2,1)} %get-tuple-element.256) | copy-start | bytes 1572868
  745.6 10.2 %copy-start.19 = (f32[256,512]{1,0:T(8,128)S(1)}, f32[256,512]{1,0:T(8,128)}, u32[]{:S(2)}) copy-start(f32[256,512]{1,0:T(8,128)} %get-tuple-element.259) | copy-start | bytes 1572868
  746.7 8.3 %copy-start.20 = (f32[256,512]{1,0:T(8,128)S(1)}, f32[256,512]{1,0:T(8,128)}, u32[]{:S(2)}) copy-start(f32[256,512]{1,0:T(8,128)} %get-tuple-element.258) | copy-start | bytes 1572868
  (15 other events, 75.9 us)
Sparse Core Ops, SparseCore 0:
  9.6 57.1 all-gather.7
  100.2 54.1 all-gather.9
  156.3 65.4 all-gather.5
  617.6 40.9 reduce-scatter.1
